TPU v7x, 32 devices: a whole 2x2x4 slice. The times are simulated.
32 devices in a mesh: depth: 8 (over z, y), freq: 4 (over x, core).
Axes of the slice: x: 2, y: 2, z: 4, core: 2. Of those that a mesh axis runs over, the one named last changes fastest.
Arguments:
- extrap: bfloat16 [8, 4, 2, 1024, 1024], P('depth', 'freq'), may hold values from -0.125 to 0.125
- source_field: bfloat16 [4, 128, 2, 1024], P('freq'), may hold values from -6 to 6
- record_field: bfloat16 [4, 128, 2, 1024], P('freq'), may hold values from -6 to 6
- shot_of_record: int32 [128], replicated, may hold values from 0 to 127, each once
- freq_index: int32 [4], P('freq'), may hold values from 0 to 31, as said below
- angle_lag: int32 [1024, 256], replicated, may hold values from 0 to 7
Outputs:
- gathers: float32 [1024, 8, 256], P(('freq', 'depth'))
Inputs may be any that keep to these rules, and one draw needn't show every extreme that they name: `shot_of_record`: each shot is named once. `freq_index`: the frequency numbers are distinct, and the largest one, 31, is always held by some slot.
All inputs are finite; a program needn't handle non-finite values.
Results may differ from a plain program's by a relative error of at most 0.035.
Values may be sent and summed in bfloat16 or wider, within the bound.
No kernel may reach another device: no remote copies, remote signals or barrier semaphores. Data moves between devices by JAX's collectives and lax.ppermute only.
A program may use at most 64 MiB of HBM per device.

v0:
```python
import math

import jax
import jax.numpy as jnp
from jax import lax
from jax.sharding import PartitionSpec as P

MICRO = 4


def from_behind(value, axis, steps):
    count = lax.axis_size(axis)
    leading, last = (max(0, -steps), min(count, count - steps))
    return lax.ppermute(value, axis, [(source, source + steps) for source in range(leading, last)])


def make_block(real_part, imag_part):
    upper = jnp.concatenate([real_part, imag_part], axis=1)
    lower = jnp.concatenate([-imag_part, real_part], axis=1)
    return jnp.concatenate([upper, lower], axis=0)


def shards(extrap, source_field, record_field, shot_of_record, freq_index, angle_lag):
    segment_index = lax.axis_index("depth")
    depth_count = lax.axis_size("depth")
    freq_count = lax.axis_size("freq")
    points = source_field.shape[3]
    shot_count = source_field.shape[1]
    extrapolator = make_block(extrap[0, 0, 0], extrap[0, 0, 1])
    paired = jnp.take(source_field[0].reshape(shot_count, 2 * points), shot_of_record, axis=0)
    record_rows = jnp.concatenate([record_field[0, :, 1], record_field[0, :, 0]], axis=1)
    batch_count = MICRO
    batch_rows = shot_count // batch_count
    inputs = jnp.concatenate(
        [
            paired.reshape(batch_count, batch_rows, 2 * points),
            record_rows.reshape(batch_count, batch_rows, 2 * points),
        ],
        axis=1,
    )

    def extend(values):
        return jnp.dot(values, extrapolator, preferred_element_type=jnp.float32).astype(
            jnp.bfloat16
        )

    def vacant(values):
        return jnp.zeros_like(values)

    def advance(tick_index, state_pair):
        arrived, finished = state_pair
        batch_slot = tick_index - segment_index
        active = (batch_slot >= 0) & (batch_slot < batch_count)
        slot_clamped = jnp.clip(batch_slot, 0, batch_count - 1)
        incoming = lax.dynamic_index_in_dim(inputs, slot_clamped, 0, keepdims=False)
        entering = jnp.where(segment_index == 0, incoming, arrived)
        advanced = lax.cond(active, extend, vacant, entering)
        previous = lax.dynamic_index_in_dim(finished, slot_clamped, 0, keepdims=False)
        finished = lax.dynamic_update_index_in_dim(
            finished, jnp.where(active, advanced, previous), slot_clamped, 0
        )
        arrived = from_behind(advanced, "depth", 1)
        return (arrived, finished)

    start_state = (jnp.zeros((2 * batch_rows, 2 * points), jnp.bfloat16), jnp.zeros_like(inputs))
    arrived, finished = lax.fori_loop(0, batch_count + depth_count - 1, advance, start_state)
    source_stack = finished[:, :batch_rows].reshape(2 * shot_count, points)
    record_stack = (
        finished[:, batch_rows:]
        .reshape(shot_count, 2, points)[:, ::-1]
        .reshape(2 * shot_count, points)
    )
    factor = (
        (freq_index[0].astype(jnp.float32) + 1.0)
        / (8 * freq_count)
        / math.sqrt(shot_count * freq_count)
    )
    partial_value = lax.dot_general(
        source_stack, record_stack, (((0,), (0,)), ((), ())), preferred_element_type=jnp.float32
    )
    image_panel = lax.psum_scatter(
        (partial_value * factor).astype(jnp.bfloat16), "freq", scatter_dimension=0, tiled=True
    )
    gathered = lax.all_to_all(
        image_panel[:, None, :], "depth", split_axis=0, concat_axis=1, tiled=True
    )
    row_count = gathered.shape[0]
    padded = jnp.concatenate([gathered, jnp.zeros_like(gathered)], axis=1)

    def add_lagged(lag_value, stacked_sum):
        shifted = lax.dynamic_slice_in_dim(padded, lag_value, depth_count, 1).reshape(
            row_count * depth_count, points
        )
        selector = (angle_lag == lag_value).astype(jnp.bfloat16)
        return stacked_sum + jnp.dot(shifted, selector, preferred_element_type=jnp.float32)

    stacked_sum = lax.fori_loop(
        0,
        depth_count,
        add_lagged,
        jnp.zeros((row_count * depth_count, angle_lag.shape[1]), jnp.float32),
    )
    return (stacked_sum / math.sqrt(points)).reshape(row_count, depth_count, angle_lag.shape[1])


def solution(mesh):
    placed = (
        P("depth", "freq", None, None, None),
        P("freq", None, None, None),
        P("freq", None, None, None),
        P(),
        P("freq"),
        P(),
    )
    return jax.shard_map(
        shards,
        mesh=mesh,
        in_specs=placed,
        out_specs=P(("freq", "depth"), None, None),
        check_vma=False,
    )
```

profile of v0, /device:TPU:0, one launch (start us, length us, event | category | flops | bytes accessed | tf_op | source)
XLA Modules:
  0.0 250.7 jit_solution(8519418264634463854)
XLA Ops:
  6.5 4.8 %slice_bitcast_fusion = (bf16[1024,1024]{1,0:T(8,128)(2,1)}, bf16[1024,1024]{1,0:T(8,128)(2,1)}) fusion(bf16[1,1,2,1024,1024]{4,3,2,1,0:T(8,128)(2,1)} %param.12), kind=kLoop, calls=%fused_computation.16 | loop fusion | bytes 8388608 | tf_op jit(solution)/shard_map/squeeze | solution.py:29
  12.4 0.7 fusion.7
  13.2 0.8 copy.22
  14.2 0.9 gather_fusion
  15.3 13.2 %maximum_maximum_fusion = bf16[2048,2048]{1,0:T(8,128)(2,1)} fusion(bf16[1024,1024]{1,0:T(8,128)(2,1)} %get-tuple-element.304, bf16[1024,1024]{1,0:T(8,128)(2,1)S(1)} %fusion.5, bf16[1024,1024]{1,0:T(8,128)(2,1)} %get-tuple-element.303), kind=kLoop, calls=%fused_computation.14 | loop fusion | flops 33554432 | bytes 14680064 | tf_op jit(solution)/shard_map/concatenate | solution.py:20
  28.8 137.4 %while.30 = (s32[]{:T(128)}, bf16[64,2048]{1,0:T(8,128)(2,1)S(1)}, bf16[4,64,2048]{2,1,0:T(8,128)(2,1)S(1)}, s32[]{:T(128)}, pred[]{:T(512)}, /*index=5*/bf16[4,...) while((s32[]{:T(128)}, bf16[64,2048]{1,0:T(8,128)(2,1)S(1)}, ...), condition=%wide.region_3.4_spmd, body=%wide.region_0.3_spmd.sunk | while | flops 537264128 | bytes 11534609 | solution.py:66
  28.8 5.0 %conditional.2 = (bf16[64,2048]{1,0:T(8,128)(2,1)S(1)}) conditional(s32[]{:T(128)} %convert_element_type.27, () %tuple.72, (pred[]{:T(512)}, bf16[4,64,2048]{2,1,0:T(8,128)(2,1)S(1)}, s32[]{:T(128)}, bf16[64,2048]{1,0:T(8,128)(2,1)S(1)}, bf16[2048,2048]{1,0:T(8,128)(2,1)}) %tuple.73), branch_computations={%region_1.1_spmd, %region_2.2_spmd} | conditional | flops 537133056 | bytes 9175053 | solution.py:57
  28.8 5.0 %convolution_convert_fusion = bf16[64,2048]{1,0:T(8,128)(2,1)S(1)} fusion(bf16[2048,2048]{1,0:T(8,128)(2,1)} %get-tuple-element.244, bf16[64,2048]{1,0:T(8,128)(2,1)S(1)} %get-tuple-element.243, bf16[4,64,2048]{2,1,0:T(8,128)(2,1)S(1)} %get-tuple-element.241, s32[]{:T(128)} %get-tuple-element.242, pred[]{:T(512)} %get-tuple-element.240), kind=kOutput, calls=%fused_computation.1 | convolution fusion | flops 537133056 | bytes 9175045 | tf_op jit(solution)/shard_map/while/body/eval_jaxpr/cond/branch_1_fun/dot_general | solution.py:43
  33.8 1.3 collective-permute-start
  35.2 6.3 %collective-permute-done = bf16[64,2048]{1,0:T(8,128)(2,1)S(1)} collective-permute-done((bf16[64,2048]{1,0:T(8,128)(2,1)S(1)}, bf16[64,2048]{1,0:T(8,128)(2,1)S(1)}, u32[]{:S(2)}, u32[]{:S(2)}) %collective-permute-start) | collective-permute-done | bytes 262176 | tf_op jit(solution)/shard_map/while/body/eval_jaxpr/ppermute | solution.py:14
  41.5 5.0 %conditional.2 = (bf16[64,2048]{1,0:T(8,128)(2,1)S(1)}) conditional(s32[]{:T(128)} %convert_element_type.27, () %tuple.72, (pred[]{:T(512)}, bf16[4,64,2048]{2,1,0:T(8,128)(2,1)S(1)}, s32[]{:T(128)}, bf16[64,2048]{1,0:T(8,128)(2,1)S(1)}, bf16[2048,2048]{1,0:T(8,128)(2,1)}) %tuple.73), branch_computations={%region_1.1_spmd, %region_2.2_spmd} | conditional | flops 537133056 | bytes 9175053 | solution.py:57
  41.5 4.9 %convolution_convert_fusion = bf16[64,2048]{1,0:T(8,128)(2,1)S(1)} fusion(bf16[2048,2048]{1,0:T(8,128)(2,1)} %get-tuple-element.244, bf16[64,2048]{1,0:T(8,128)(2,1)S(1)} %get-tuple-element.243, bf16[4,64,2048]{2,1,0:T(8,128)(2,1)S(1)} %get-tuple-element.241, s32[]{:T(128)} %get-tuple-element.242, pred[]{:T(512)} %get-tuple-element.240), kind=kOutput, calls=%fused_computation.1 | convolution fusion | flops 537133056 | bytes 9175045 | tf_op jit(solution)/shard_map/while/body/eval_jaxpr/cond/branch_1_fun/dot_general | solution.py:43
  46.5 4.4 %collective-permute-start = (bf16[64,2048]{1,0:T(8,128)(2,1)S(1)}, bf16[64,2048]{1,0:T(8,128)(2,1)S(1)}, u32[]{:S(2)}, u32[]{:S(2)}) collective-permute-start(bf16[64,2048]{1,0:T(8,128)(2,1)S(1)} %get-tuple-element.428), channel_id=1, source_target_pairs={{0,4},{4,8},{8,12},{12,16},{16,20},{20,24},{24,28},{1,5},{5,9},{9,... | collective-permute-start | bytes 786440 | tf_op jit(solution)/shard_map/while/body/eval_jaxpr/ppermute | solution.py:14
  51.0 5.5 %collective-permute-done = bf16[64,2048]{1,0:T(8,128)(2,1)S(1)} collective-permute-done((bf16[64,2048]{1,0:T(8,128)(2,1)S(1)}, bf16[64,2048]{1,0:T(8,128)(2,1)S(1)}, u32[]{:S(2)}, u32[]{:S(2)}) %collective-permute-start) | collective-permute-done | bytes 262176 | tf_op jit(solution)/shard_map/while/body/eval_jaxpr/ppermute | solution.py:14
  56.4 5.0 %conditional.2 = (bf16[64,2048]{1,0:T(8,128)(2,1)S(1)}) conditional(s32[]{:T(128)} %convert_element_type.27, () %tuple.72, (pred[]{:T(512)}, bf16[4,64,2048]{2,1,0:T(8,128)(2,1)S(1)}, s32[]{:T(128)}, bf16[64,2048]{1,0:T(8,128)(2,1)S(1)}, bf16[2048,2048]{1,0:T(8,128)(2,1)}) %tuple.73), branch_computations={%region_1.1_spmd, %region_2.2_spmd} | conditional | flops 537133056 | bytes 9175053 | solution.py:57
  56.5 4.9 %convolution_convert_fusion = bf16[64,2048]{1,0:T(8,128)(2,1)S(1)} fusion(bf16[2048,2048]{1,0:T(8,128)(2,1)} %get-tuple-element.244, bf16[64,2048]{1,0:T(8,128)(2,1)S(1)} %get-tuple-element.243, bf16[4,64,2048]{2,1,0:T(8,128)(2,1)S(1)} %get-tuple-element.241, s32[]{:T(128)} %get-tuple-element.242, pred[]{:T(512)} %get-tuple-element.240), kind=kOutput, calls=%fused_computation.1 | convolution fusion | flops 537133056 | bytes 9175045 | tf_op jit(solution)/shard_map/while/body/eval_jaxpr/cond/branch_1_fun/dot_general | solution.py:43
  61.4 4.4 %collective-permute-start = (bf16[64,2048]{1,0:T(8,128)(2,1)S(1)}, bf16[64,2048]{1,0:T(8,128)(2,1)S(1)}, u32[]{:S(2)}, u32[]{:S(2)}) collective-permute-start(bf16[64,2048]{1,0:T(8,128)(2,1)S(1)} %get-tuple-element.428), channel_id=1, source_target_pairs={{0,4},{4,8},{8,12},{12,16},{16,20},{20,24},{24,28},{1,5},{5,9},{9,... | collective-permute-start | bytes 786440 | tf_op jit(solution)/shard_map/while/body/eval_jaxpr/ppermute | solution.py:14
  65.9 4.6 %collective-permute-done = bf16[64,2048]{1,0:T(8,128)(2,1)S(1)} collective-permute-done((bf16[64,2048]{1,0:T(8,128)(2,1)S(1)}, bf16[64,2048]{1,0:T(8,128)(2,1)S(1)}, u32[]{:S(2)}, u32[]{:S(2)}) %collective-permute-start) | collective-permute-done | bytes 262176 | tf_op jit(solution)/shard_map/while/body/eval_jaxpr/ppermute | solution.py:14
  70.5 4.9 %conditional.2 = (bf16[64,2048]{1,0:T(8,128)(2,1)S(1)}) conditional(s32[]{:T(128)} %convert_element_type.27, () %tuple.72, (pred[]{:T(512)}, bf16[4,64,2048]{2,1,0:T(8,128)(2,1)S(1)}, s32[]{:T(128)}, bf16[64,2048]{1,0:T(8,128)(2,1)S(1)}, bf16[2048,2048]{1,0:T(8,128)(2,1)}) %tuple.73), branch_computations={%region_1.1_spmd, %region_2.2_spmd} | conditional | flops 537133056 | bytes 9175053 | solution.py:57
  70.5 4.9 %convolution_convert_fusion = bf16[64,2048]{1,0:T(8,128)(2,1)S(1)} fusion(bf16[2048,2048]{1,0:T(8,128)(2,1)} %get-tuple-element.244, bf16[64,2048]{1,0:T(8,128)(2,1)S(1)} %get-tuple-element.243, bf16[4,64,2048]{2,1,0:T(8,128)(2,1)S(1)} %get-tuple-element.241, s32[]{:T(128)} %get-tuple-element.242, pred[]{:T(512)} %get-tuple-element.240), kind=kOutput, calls=%fused_computation.1 | convolution fusion | flops 537133056 | bytes 9175045 | tf_op jit(solution)/shard_map/while/body/eval_jaxpr/cond/branch_1_fun/dot_general | solution.py:43
  75.5 4.4 %collective-permute-start = (bf16[64,2048]{1,0:T(8,128)(2,1)S(1)}, bf16[64,2048]{1,0:T(8,128)(2,1)S(1)}, u32[]{:S(2)}, u32[]{:S(2)}) collective-permute-start(bf16[64,2048]{1,0:T(8,128)(2,1)S(1)} %get-tuple-element.428), channel_id=1, source_target_pairs={{0,4},{4,8},{8,12},{12,16},{16,20},{20,24},{24,28},{1,5},{5,9},{9,... | collective-permute-start | bytes 786440 | tf_op jit(solution)/shard_map/while/body/eval_jaxpr/ppermute | solution.py:14
  80.0 3.7 %collective-permute-done = bf16[64,2048]{1,0:T(8,128)(2,1)S(1)} collective-permute-done((bf16[64,2048]{1,0:T(8,128)(2,1)S(1)}, bf16[64,2048]{1,0:T(8,128)(2,1)S(1)}, u32[]{:S(2)}, u32[]{:S(2)}) %collective-permute-start) | collective-permute-done | bytes 262176 | tf_op jit(solution)/shard_map/while/body/eval_jaxpr/ppermute | solution.py:14
  83.8 9.5 %collective-permute-start = (bf16[64,2048]{1,0:T(8,128)(2,1)S(1)}, bf16[64,2048]{1,0:T(8,128)(2,1)S(1)}, u32[]{:S(2)}, u32[]{:S(2)}) collective-permute-start(bf16[64,2048]{1,0:T(8,128)(2,1)S(1)} %get-tuple-element.428), channel_id=1, source_target_pairs={{0,4},{4,8},{8,12},{12,16},{16,20},{20,24},{24,28},{1,5},{5,9},{9,... | collective-permute-start | bytes 786440 | tf_op jit(solution)/shard_map/while/body/eval_jaxpr/ppermute | solution.py:14
  93.4 3.7 %collective-permute-done = bf16[64,2048]{1,0:T(8,128)(2,1)S(1)} collective-permute-done((bf16[64,2048]{1,0:T(8,128)(2,1)S(1)}, bf16[64,2048]{1,0:T(8,128)(2,1)S(1)}, u32[]{:S(2)}, u32[]{:S(2)}) %collective-permute-start) | collective-permute-done | bytes 262176 | tf_op jit(solution)/shard_map/while/body/eval_jaxpr/ppermute | solution.py:14
  97.2 5.3 %collective-permute-start = (bf16[64,2048]{1,0:T(8,128)(2,1)S(1)}, bf16[64,2048]{1,0:T(8,128)(2,1)S(1)}, u32[]{:S(2)}, u32[]{:S(2)}) collective-permute-start(bf16[64,2048]{1,0:T(8,128)(2,1)S(1)} %get-tuple-element.428), channel_id=1, source_target_pairs={{0,4},{4,8},{8,12},{12,16},{16,20},{20,24},{24,28},{1,5},{5,9},{9,... | collective-permute-start | bytes 786440 | tf_op jit(solution)/shard_map/while/body/eval_jaxpr/ppermute | solution.py:14
  102.6 3.7 %collective-permute-done = bf16[64,2048]{1,0:T(8,128)(2,1)S(1)} collective-permute-done((bf16[64,2048]{1,0:T(8,128)(2,1)S(1)}, bf16[64,2048]{1,0:T(8,128)(2,1)S(1)}, u32[]{:S(2)}, u32[]{:S(2)}) %collective-permute-start) | collective-permute-done | bytes 262176 | tf_op jit(solution)/shard_map/while/body/eval_jaxpr/ppermute | solution.py:14
  106.4 10.2 %collective-permute-start = (bf16[64,2048]{1,0:T(8,128)(2,1)S(1)}, bf16[64,2048]{1,0:T(8,128)(2,1)S(1)}, u32[]{:S(2)}, u32[]{:S(2)}) collective-permute-start(bf16[64,2048]{1,0:T(8,128)(2,1)S(1)} %get-tuple-element.428), channel_id=1, source_target_pairs={{0,4},{4,8},{8,12},{12,16},{16,20},{20,24},{24,28},{1,5},{5,9},{9,... | collective-permute-start | bytes 786440 | tf_op jit(solution)/shard_map/while/body/eval_jaxpr/ppermute | solution.py:14
  116.7 3.9 %collective-permute-done = bf16[64,2048]{1,0:T(8,128)(2,1)S(1)} collective-permute-done((bf16[64,2048]{1,0:T(8,128)(2,1)S(1)}, bf16[64,2048]{1,0:T(8,128)(2,1)S(1)}, u32[]{:S(2)}, u32[]{:S(2)}) %collective-permute-start) | collective-permute-done | bytes 262176 | tf_op jit(solution)/shard_map/while/body/eval_jaxpr/ppermute | solution.py:14
  120.7 5.1 %collective-permute-start = (bf16[64,2048]{1,0:T(8,128)(2,1)S(1)}, bf16[64,2048]{1,0:T(8,128)(2,1)S(1)}, u32[]{:S(2)}, u32[]{:S(2)}) collective-permute-start(bf16[64,2048]{1,0:T(8,128)(2,1)S(1)} %get-tuple-element.428), channel_id=1, source_target_pairs={{0,4},{4,8},{8,12},{12,16},{16,20},{20,24},{24,28},{1,5},{5,9},{9,... | collective-permute-start | bytes 786440 | tf_op jit(solution)/shard_map/while/body/eval_jaxpr/ppermute | solution.py:14
  125.9 3.8 %collective-permute-done = bf16[64,2048]{1,0:T(8,128)(2,1)S(1)} collective-permute-done((bf16[64,2048]{1,0:T(8,128)(2,1)S(1)}, bf16[64,2048]{1,0:T(8,128)(2,1)S(1)}, u32[]{:S(2)}, u32[]{:S(2)}) %collective-permute-start) | collective-permute-done | bytes 262176 | tf_op jit(solution)/shard_map/while/body/eval_jaxpr/ppermute | solution.py:14
  129.8 8.9 %collective-permute-start = (bf16[64,2048]{1,0:T(8,128)(2,1)S(1)}, bf16[64,2048]{1,0:T(8,128)(2,1)S(1)}, u32[]{:S(2)}, u32[]{:S(2)}) collective-permute-start(bf16[64,2048]{1,0:T(8,128)(2,1)S(1)} %get-tuple-element.428), channel_id=1, source_target_pairs={{0,4},{4,8},{8,12},{12,16},{16,20},{20,24},{24,28},{1,5},{5,9},{9,... | collective-permute-start | bytes 786440 | tf_op jit(solution)/shard_map/while/body/eval_jaxpr/ppermute | solution.py:14
  138.8 6.6 %collective-permute-done = bf16[64,2048]{1,0:T(8,128)(2,1)S(1)} collective-permute-done((bf16[64,2048]{1,0:T(8,128)(2,1)S(1)}, bf16[64,2048]{1,0:T(8,128)(2,1)S(1)}, u32[]{:S(2)}, u32[]{:S(2)}) %collective-permute-start) | collective-permute-done | bytes 262176 | tf_op jit(solution)/shard_map/while/body/eval_jaxpr/ppermute | solution.py:14
  145.4 4.9 %collective-permute-start = (bf16[64,2048]{1,0:T(8,128)(2,1)S(1)}, bf16[64,2048]{1,0:T(8,128)(2,1)S(1)}, u32[]{:S(2)}, u32[]{:S(2)}) collective-permute-start(bf16[64,2048]{1,0:T(8,128)(2,1)S(1)} %get-tuple-element.428), channel_id=1, source_target_pairs={{0,4},{4,8},{8,12},{12,16},{16,20},{20,24},{24,28},{1,5},{5,9},{9,... | collective-permute-start | bytes 786440 | tf_op jit(solution)/shard_map/while/body/eval_jaxpr/ppermute | solution.py:14
  150.4 6.1 %collective-permute-done = bf16[64,2048]{1,0:T(8,128)(2,1)S(1)} collective-permute-done((bf16[64,2048]{1,0:T(8,128)(2,1)S(1)}, bf16[64,2048]{1,0:T(8,128)(2,1)S(1)}, u32[]{:S(2)}, u32[]{:S(2)}) %collective-permute-start) | collective-permute-done | bytes 262176 | tf_op jit(solution)/shard_map/while/body/eval_jaxpr/ppermute | solution.py:14
  156.6 5.7 %collective-permute-start = (bf16[64,2048]{1,0:T(8,128)(2,1)S(1)}, bf16[64,2048]{1,0:T(8,128)(2,1)S(1)}, u32[]{:S(2)}, u32[]{:S(2)}) collective-permute-start(bf16[64,2048]{1,0:T(8,128)(2,1)S(1)} %get-tuple-element.428), channel_id=1, source_target_pairs={{0,4},{4,8},{8,12},{12,16},{16,20},{20,24},{24,28},{1,5},{5,9},{9,... | collective-permute-start | bytes 786440 | tf_op jit(solution)/shard_map/while/body/eval_jaxpr/ppermute | solution.py:14
  162.4 3.7 %collective-permute-done = bf16[64,2048]{1,0:T(8,128)(2,1)S(1)} collective-permute-done((bf16[64,2048]{1,0:T(8,128)(2,1)S(1)}, bf16[64,2048]{1,0:T(8,128)(2,1)S(1)}, u32[]{:S(2)}, u32[]{:S(2)}) %collective-permute-start) | collective-permute-done | bytes 262176 | tf_op jit(solution)/shard_map/while/body/eval_jaxpr/ppermute | solution.py:14
  166.7 2.8 %rev.3 = bf16[128,2,1024]{2,1,0:T(2,128)(2,1)S(1)} reverse(bf16[128,2,1024]{2,1,0:T(2,128)(2,1)S(1)} %reshape.42), dimensions={1} | reverse | bytes 1048576 | tf_op jit(solution)/shard_map/rev | solution.py:69
  170.5 2.1 multiply_convert_fusion
  172.6 41.3 %reduce-scatter.2.cloned.1.call-done = bf16[256,1024]{1,0:T(8,128)(2,1)} async-done(((bf16[1024,1024]{1,0:T(8,128)(2,1)}), bf16[256,1024]{1,0:T(8,128)(2,1)}) %reduce-scatter.2.cloned.1.call-update) | async-done | bytes 524304 | tf_op jit(solution)/shard_map/reduce_scatter | solution.py:81
  213.9 0.5 broadcast.25
  214.4 2.0 reduce
  216.4 1.2 reshape.55
  217.6 5.5 %all-to-all-start = ((bf16[8,2,16384]{2,1,0:T(2,128)(2,1)}), bf16[8,2,16384]{2,1,0:T(2,128)(2,1)S(1)}, u32[]{:S(2)}, u32[]{:S(2)}) async-start(bf16[8,2,16384]{2,1,0:T(2,128)(2,1)} %reshape.55), calls=%async_computation.1 | async-start | bytes 1048576 | tf_op jit(solution)/shard_map/all_to_all | solution.py:84
  223.1 14.5 %all-to-all-done = bf16[8,2,16384]{2,1,0:T(2,128)(2,1)S(1)} async-done(((bf16[8,2,16384]{2,1,0:T(2,128)(2,1)}), bf16[8,2,16384]{2,1,0:T(2,128)(2,1)S(1)}, u32[]{:S(2)}, u32[]{:S(2)}) %all-to-all-start) | async-done | bytes 524320 | tf_op jit(solution)/shard_map/all_to_all | solution.py:84
  237.6 0.5 reshape.56
  238.4 4.7 %while.31 = (s32[]{:T(128)}, f32[256,256]{1,0:T(8,128)S(1)}, bf16[32,16,1024]{2,0,1:T(8,128)(2,1)S(1)}, s32[1024,256]{1,0:T(8,128)S(1)}, s32[]{:T(128)}, /*index=5*/s32[]{:T(128)}) while((s32[]{:T(128)}, f32[256,256]{1,0:T(8,128)S(1)}, bf16[32,16,1024]{2,0,1:T(8,128)(2,1)S(1)}, s32[1024,256]{1,0:T(8,128)S(1)}, s32[]{:T(128)}, ...), condition=%wide.region_6.7_spmd.clone, body=%wide.region_5.6_spmd.clone.sunk | while | flops 134610944 | bytes 3145815 | solution.py:97
  238.5 0.5 convolution_add_fusion.2
  243.1 0.7 multiply_bitcast_fusion
  (83 shorter events, 8.0 us)
Async XLA Ops:
  6.5 207.3 %reduce-scatter.2.cloned.1.call-start = ((), (), s32[]{:S(2)}) async-start(), calls=%async_computation.2 | async-start | bytes 2621440 | tf_op jit(solution)/shard_map/reduce_scatter | solution.py:81
  6.5 4.8 %copy-start.1 = (bf16[1,1,2,1024,1024]{4,3,2,1,0:T(8,128)(2,1)S(1)}, bf16[1,1,2,1024,1024]{4,3,2,1,0:T(8,128)(2,1)}, u32[]{:S(2)}) copy-start(bf16[1,1,2,1024,1024]{4,3,2,1,0:T(8,128)(2,1)} %param.12) | copy-start | bytes 12582916
  11.3 0.7 copy-start.5
  11.4 1.1 copy-start.2
  11.4 2.7 %copy-start.4 = (bf16[1,128,2,1024]{3,2,1,0:T(2,128)(2,1)S(1)}, bf16[1,128,2,1024]{3,2,1,0:T(2,128)(2,1)}, u32[]{:S(2)}) copy-start(bf16[1,128,2,1024]{3,2,1,0:T(2,128)(2,1)} %param.13) | copy-start | bytes 1572868
  15.3 13.2 %copy-start.3 = (bf16[1,128,1,1024]{3,1,2,0:T(8,128)(2,1)S(1)}, bf16[1,128,1,1024]{3,1,2,0:T(8,128)(2,1)}, u32[]{:S(2)}) copy-start(bf16[1,128,1,1024]{3,1,2,0:T(8,128)(2,1)} %copy.22) | copy-start | bytes 786436
  33.8 7.7 %collective-permute-start = (bf16[64,2048]{1,0:T(8,128)(2,1)S(1)}, bf16[64,2048]{1,0:T(8,128)(2,1)S(1)}, u32[]{:S(2)}, u32[]{:S(2)}) collective-permute-start(bf16[64,2048]{1,0:T(8,128)(2,1)S(1)} %get-tuple-element.428), channel_id=1, source_target_pairs={{0,4},{4,8},{8,12},{12,16},{16,20},{20,24},{24,28},{1,5},{5,9},{9,... | collective-permute-start | bytes 786440 | tf_op jit(solution)/shard_map/while/body/eval_jaxpr/ppermute | solution.py:14
  46.5 10.0 %collective-permute-start = (bf16[64,2048]{1,0:T(8,128)(2,1)S(1)}, bf16[64,2048]{1,0:T(8,128)(2,1)S(1)}, u32[]{:S(2)}, u32[]{:S(2)}) collective-permute-start(bf16[64,2048]{1,0:T(8,128)(2,1)S(1)} %get-tuple-element.428), channel_id=1, source_target_pairs={{0,4},{4,8},{8,12},{12,16},{16,20},{20,24},{24,28},{1,5},{5,9},{9,... | collective-permute-start | bytes 786440 | tf_op jit(solution)/shard_map/while/body/eval_jaxpr/ppermute | solution.py:14
  61.4 9.1 %collective-permute-start = (bf16[64,2048]{1,0:T(8,128)(2,1)S(1)}, bf16[64,2048]{1,0:T(8,128)(2,1)S(1)}, u32[]{:S(2)}, u32[]{:S(2)}) collective-permute-start(bf16[64,2048]{1,0:T(8,128)(2,1)S(1)} %get-tuple-element.428), channel_id=1, source_target_pairs={{0,4},{4,8},{8,12},{12,16},{16,20},{20,24},{24,28},{1,5},{5,9},{9,... | collective-permute-start | bytes 786440 | tf_op jit(solution)/shard_map/while/body/eval_jaxpr/ppermute | solution.py:14
  75.5 8.3 %collective-permute-start = (bf16[64,2048]{1,0:T(8,128)(2,1)S(1)}, bf16[64,2048]{1,0:T(8,128)(2,1)S(1)}, u32[]{:S(2)}, u32[]{:S(2)}) collective-permute-start(bf16[64,2048]{1,0:T(8,128)(2,1)S(1)} %get-tuple-element.428), channel_id=1, source_target_pairs={{0,4},{4,8},{8,12},{12,16},{16,20},{20,24},{24,28},{1,5},{5,9},{9,... | collective-permute-start | bytes 786440 | tf_op jit(solution)/shard_map/while/body/eval_jaxpr/ppermute | solution.py:14
  83.8 13.4 %collective-permute-start = (bf16[64,2048]{1,0:T(8,128)(2,1)S(1)}, bf16[64,2048]{1,0:T(8,128)(2,1)S(1)}, u32[]{:S(2)}, u32[]{:S(2)}) collective-permute-start(bf16[64,2048]{1,0:T(8,128)(2,1)S(1)} %get-tuple-element.428), channel_id=1, source_target_pairs={{0,4},{4,8},{8,12},{12,16},{16,20},{20,24},{24,28},{1,5},{5,9},{9,... | collective-permute-start | bytes 786440 | tf_op jit(solution)/shard_map/while/body/eval_jaxpr/ppermute | solution.py:14
  97.2 9.2 %collective-permute-start = (bf16[64,2048]{1,0:T(8,128)(2,1)S(1)}, bf16[64,2048]{1,0:T(8,128)(2,1)S(1)}, u32[]{:S(2)}, u32[]{:S(2)}) collective-permute-start(bf16[64,2048]{1,0:T(8,128)(2,1)S(1)} %get-tuple-element.428), channel_id=1, source_target_pairs={{0,4},{4,8},{8,12},{12,16},{16,20},{20,24},{24,28},{1,5},{5,9},{9,... | collective-permute-start | bytes 786440 | tf_op jit(solution)/shard_map/while/body/eval_jaxpr/ppermute | solution.py:14
  106.4 14.3 %collective-permute-start = (bf16[64,2048]{1,0:T(8,128)(2,1)S(1)}, bf16[64,2048]{1,0:T(8,128)(2,1)S(1)}, u32[]{:S(2)}, u32[]{:S(2)}) collective-permute-start(bf16[64,2048]{1,0:T(8,128)(2,1)S(1)} %get-tuple-element.428), channel_id=1, source_target_pairs={{0,4},{4,8},{8,12},{12,16},{16,20},{20,24},{24,28},{1,5},{5,9},{9,... | collective-permute-start | bytes 786440 | tf_op jit(solution)/shard_map/while/body/eval_jaxpr/ppermute | solution.py:14
  120.7 9.1 %collective-permute-start = (bf16[64,2048]{1,0:T(8,128)(2,1)S(1)}, bf16[64,2048]{1,0:T(8,128)(2,1)S(1)}, u32[]{:S(2)}, u32[]{:S(2)}) collective-permute-start(bf16[64,2048]{1,0:T(8,128)(2,1)S(1)} %get-tuple-element.428), channel_id=1, source_target_pairs={{0,4},{4,8},{8,12},{12,16},{16,20},{20,24},{24,28},{1,5},{5,9},{9,... | collective-permute-start | bytes 786440 | tf_op jit(solution)/shard_map/while/body/eval_jaxpr/ppermute | solution.py:14
  129.8 15.6 %collective-permute-start = (bf16[64,2048]{1,0:T(8,128)(2,1)S(1)}, bf16[64,2048]{1,0:T(8,128)(2,1)S(1)}, u32[]{:S(2)}, u32[]{:S(2)}) collective-permute-start(bf16[64,2048]{1,0:T(8,128)(2,1)S(1)} %get-tuple-element.428), channel_id=1, source_target_pairs={{0,4},{4,8},{8,12},{12,16},{16,20},{20,24},{24,28},{1,5},{5,9},{9,... | collective-permute-start | bytes 786440 | tf_op jit(solution)/shard_map/while/body/eval_jaxpr/ppermute | solution.py:14
  145.4 11.1 %collective-permute-start = (bf16[64,2048]{1,0:T(8,128)(2,1)S(1)}, bf16[64,2048]{1,0:T(8,128)(2,1)S(1)}, u32[]{:S(2)}, u32[]{:S(2)}) collective-permute-start(bf16[64,2048]{1,0:T(8,128)(2,1)S(1)} %get-tuple-element.428), channel_id=1, source_target_pairs={{0,4},{4,8},{8,12},{12,16},{16,20},{20,24},{24,28},{1,5},{5,9},{9,... | collective-permute-start | bytes 786440 | tf_op jit(solution)/shard_map/while/body/eval_jaxpr/ppermute | solution.py:14
  156.6 9.6 %collective-permute-start = (bf16[64,2048]{1,0:T(8,128)(2,1)S(1)}, bf16[64,2048]{1,0:T(8,128)(2,1)S(1)}, u32[]{:S(2)}, u32[]{:S(2)}) collective-permute-start(bf16[64,2048]{1,0:T(8,128)(2,1)S(1)} %get-tuple-element.428), channel_id=1, source_target_pairs={{0,4},{4,8},{8,12},{12,16},{16,20},{20,24},{24,28},{1,5},{5,9},{9,... | collective-permute-start | bytes 786440 | tf_op jit(solution)/shard_map/while/body/eval_jaxpr/ppermute | solution.py:14
  172.6 65.8 %copy-start = (s32[1024,256]{1,0:T(8,128)S(1)}, s32[1024,256]{1,0:T(8,128)}, u32[]{:S(2)}) copy-start(s32[1024,256]{1,0:T(8,128)} %param.17) | copy-start | bytes 3145732
  217.6 20.0 %all-to-all-start = ((bf16[8,2,16384]{2,1,0:T(2,128)(2,1)}), bf16[8,2,16384]{2,1,0:T(2,128)(2,1)S(1)}, u32[]{:S(2)}, u32[]{:S(2)}) async-start(bf16[8,2,16384]{2,1,0:T(2,128)(2,1)} %reshape.55), calls=%async_computation.1 | async-start | bytes 1048576 | tf_op jit(solution)/shard_map/all_to_all | solution.py:84
Sparse Core Ops, SparseCore 0:
  172.7 41.1 reduce-scatter.1
where the time goes:
time: 251 us
  waiting for transfers between devices  108 us (43%)
  starting transfers between devices  69.7 us (28%)
  matrix products  25.9 us (10%)
  other arithmetic  17.1 us (7%)
  local copies, waits for them, and re-layouts  15.4 us (6%)
  between operations  14.2 us (6%)
    ppermute x11, starting transfers between devices, from_behind(): lax.ppermute(value, axis, [(source, source + steps) for source in range(l...  64.2 us
    ppermute x11, waiting for transfers between devices, from_behind(): lax.ppermute(value, axis, [(source, source + steps) for source in range(l...  51.8 us
    reduce_scatter x1, waiting for transfers between devices, shards(): lax.psum_scatter((partial_value * factor).astype(jnp.bfloat16), 'freq', s...  41.3 us
    dot_general x4, matrix products, extend(): jnp.dot(values, extrapolator, preferred_element_type=jnp.float32)  19.8 us
    all_to_all x1, waiting for transfers between devices, shards(): lax.all_to_all(image_panel[:, None, :], 'depth', split_axis=0, concat_axi...  14.5 us
    concatenate x1, other arithmetic, make_block(): return jnp.concatenate([upper, lower], axis=0)  13.2 us
    all_to_all x1, starting transfers between devices, shards(): lax.all_to_all(image_panel[:, None, :], 'depth', split_axis=0, concat_axi...  5.51 us
  transfers between devices with their start and end apart: 13, of which 13 were waited for; matrix products, arithmetic and copies ran while one was open for 0% of the time, Pallas kernels for 0%

commit v1 on v0

v1 whole, which is shorter than its diff:
```python
import math

import jax
import jax.numpy as jnp
from jax import lax
from jax.sharding import PartitionSpec as P

CHUNKS = 4


def first_round(level):
    return 3 * (level // 2) + level % 2


def pairs_of(round_index, parity, depth_count, chunk_count):
    return [
        (level, level + 1)
        for level in range(parity, depth_count - 1, 2)
        if 0 <= round_index - first_round(level) < chunk_count
    ]


def busy(round_index, parity, depth_count, chunk_count):
    return any(
        0 <= round_index - first_round(level) < chunk_count
        for level in range(parity, depth_count, 2)
    )


def shards(extrap, source_field, record_field, shot_of_record, freq_index, angle_lag):
    level = lax.axis_index("depth")
    depth_count = lax.axis_size("depth")
    freq_count = lax.axis_size("freq")
    freq_slot = lax.axis_index("freq")
    points = source_field.shape[3]
    shot_count = source_field.shape[1]
    chunk_count = CHUNKS
    part = shot_count // chunk_count
    rows = 4 * part
    half_rows = 2 * part

    weights = jnp.concatenate([extrap[0, 0, 0], extrap[0, 0, 1]], axis=1)
    sources = jnp.take(source_field[0], shot_of_record, axis=0)
    records = record_field[0]

    def local_chunk(index):
        span = slice(index * part, (index + 1) * part)
        return jnp.concatenate(
            [sources[span, 0], records[span, 1], sources[span, 1], records[span, 0]], axis=0
        )

    def extend(values):
        product = jnp.dot(values, weights, preferred_element_type=jnp.float32)
        real = product[:half_rows, :points] - product[half_rows:, points:]
        imag = product[:half_rows, points:] + product[half_rows:, :points]
        return jnp.concatenate([real, imag], axis=0).astype(jnp.bfloat16)

    finished = jnp.zeros((chunk_count + 2, rows, points), jnp.bfloat16)
    sent = {}
    round_count = first_round(depth_count - 1) + chunk_count
    my_first = 3 * (level // 2) + level % 2
    for round_index in range(round_count):
        outcome = {}
        for parity in (0, 1):
            if not busy(round_index, parity, depth_count, chunk_count):
                continue
            arrived = sent.get((1 - parity, round_index - 2 + parity))
            entering = arrived
            if parity == 0 and round_index < chunk_count:
                entering = local_chunk(round_index)
                if arrived is not None:
                    entering = jnp.where(level == 0, entering, arrived)
            outcome[parity] = extend(entering)
            pairs = pairs_of(round_index, parity, depth_count, chunk_count)
            if pairs:
                sent[parity, round_index] = lax.ppermute(outcome[parity], "depth", pairs)
        if len(outcome) == 2:
            kept = jnp.where(level % 2 == 0, outcome[0], outcome[1])
        else:
            kept = next(iter(outcome.values()))
        slot = jnp.clip(round_index - my_first, -1, chunk_count) + 1
        finished = lax.dynamic_update_index_in_dim(finished, kept, slot, 0)

    done = finished[1 : chunk_count + 1].reshape(chunk_count, 2, 2, part, points)
    source_stack = done[:, :, 0].reshape(2 * shot_count, points)
    record_stack = done[:, ::-1, 1].reshape(2 * shot_count, points)
    number = freq_index[0].astype(jnp.float32) + 1.0
    scale = 1.0 / (8 * freq_count) / math.sqrt(shot_count * freq_count)

    def correlate(source_part, record_part):
        return lax.dot_general(
            source_part, record_part, (((0,), (0,)), ((), ())), preferred_element_type=jnp.float32
        )

    span = freq_count // 2
    width = points // 2
    upper = (freq_slot // span) % 2 == 1
    partner = [(slot, slot ^ span) for slot in range(freq_count)]
    own_half = jnp.where(upper, source_stack[:, width:], source_stack[:, :width])
    other_half = jnp.where(upper, source_stack[:, :width], source_stack[:, width:])
    payload = jnp.concatenate([record_stack, other_half], axis=1)
    note = jnp.full((16, payload.shape[1]), number, jnp.float32).astype(jnp.bfloat16)
    payload = jnp.concatenate([payload, note], axis=0)
    received = lax.ppermute(payload, "freq", partner)
    their_number = received[2 * shot_count, 0].astype(jnp.float32)
    image = correlate(own_half, record_stack) * (number * scale) + correlate(
        received[: 2 * shot_count, points:], received[: 2 * shot_count, :points]
    ) * (their_number * scale)
    span //= 2
    while span:
        width //= 2
        upper = (freq_slot // span) % 2 == 1
        partner = [(slot, slot ^ span) for slot in range(freq_count)]
        keep = jnp.where(upper, image[width:], image[:width])
        away = jnp.where(upper, image[:width], image[width:]).astype(jnp.bfloat16)
        image = keep + lax.ppermute(away, "freq", partner).astype(jnp.float32)
        span //= 2
    panel = lax.all_to_all(
        image.astype(jnp.bfloat16), "depth", split_axis=0, concat_axis=0, tiled=True
    )
    row_count = panel.shape[0] // depth_count
    angle_count = angle_lag.shape[1]
    lags = jnp.arange(depth_count, dtype=angle_lag.dtype)
    selector = (
        (angle_lag[:, None, :] == lags[None, :, None])
        .astype(jnp.bfloat16)
        .reshape(points, depth_count * angle_count)
    )
    spread = jnp.dot(panel, selector, preferred_element_type=jnp.float32).reshape(
        depth_count, row_count, depth_count, angle_count
    )
    total = spread[:, :, 0]
    for lag in range(1, depth_count):
        total = total.at[: depth_count - lag].add(spread[lag:, :, lag])
    return jnp.transpose(total, (1, 0, 2)) / math.sqrt(points)


def solution(mesh):
    placed = (
        P("depth", "freq", None, None, None),
        P("freq", None, None, None),
        P("freq", None, None, None),
        P(),
        P("freq"),
        P(),
    )
    return jax.shard_map(
        shards,
        mesh=mesh,
        in_specs=placed,
        out_specs=P(("freq", "depth"), None, None),
        check_vma=False,
    )
```

time: 251 us -> 167 us (0.67)
  waiting for transfers between devices: 108 us -> 36.6 us
  between operations: 14.2 us -> 2.65 us
  starting transfers between devices: 69.7 us -> 80.2 us
  other arithmetic: 17.1 us -> 7.86 us
  local copies, waits for them, and re-layouts: 15.4 us -> 12.4 us
    all_to_all x1, starting transfers between devices: 5.51 us -> 50.1 us  [shards(): lax.all_to_all(image.astype(jnp.bfloat16), 'depth', split_axis=0, concat_...]
    reduce_scatter x1 -> x0, waiting for transfers between devices: 41.3 us -> none  [shards(): lax.psum_scatter((partial_value * factor).astype(jnp.bfloat16), 'freq', s...]
    ppermute x11 -> x25, starting transfers between devices: 64.2 us -> 30.1 us  [the longest x23 28.5 us: shards(): sent[parity, round_index] = lax.ppermute(outcome[parity], 'depth', pairs)]
    ppermute x11 -> x25, waiting for transfers between devices: 51.8 us -> 23.4 us  [the longest x1 16.6 us: shards(): received = lax.ppermute(payload, 'freq', partner)]
    concatenate x2 -> x27, other arithmetic: 13.3 us -> 1.38 us  [the longest x26 1.33 us: extend(): return jnp.concatenate([real, imag], axis=0).astype(jnp.bfloat16)]
    rev x1, local copies, waits for them, and re-layouts: 2.77 us -> 0.04 us  [shards(): record_stack = done[:, ::-1, 1].reshape(2 * shot_count, points)]
    dot_general x13 -> x29, matrix products: 25.9 us -> 26.6 us  [the longest x26 23.4 us: extend(): product = jnp.dot(values, weights, preferred_element_type=jnp.float32)]
    squeeze x1 -> x3, local copies, waits for them, and re-layouts: 4.81 us -> 5.41 us  [the longest x1 4.66 us: shards(): weights = jnp.concatenate([extrap[0, 0, 0], extrap[0, 0, 1]], axis=1)]
  transfers between devices with their start and end apart: 13 -> 26, of which waited for: 13 -> 6; matrix products, arithmetic and copies ran while one was open for 0% -> 15% of each run, Pallas kernels for 0% -> 0%
where the time goes in v1:
time: 167 us; the launch traced here: 166 us
  starting transfers between devices  80.2 us (48%)
  waiting for transfers between devices  36.6 us (22%)
  matrix products  26.6 us (16%)
  local copies, waits for them, and re-layouts  12.4 us (7%)
  other arithmetic  7.86 us (5%)
  between operations  2.65 us (2%)
    all_to_all x1, starting transfers between devices, shards(): lax.all_to_all(image.astype(jnp.bfloat16), 'depth', split_axis=0, concat_...  50.1 us
    ppermute x23, starting transfers between devices, shards(): sent[parity, round_index] = lax.ppermute(outcome[parity], 'depth', pairs)  28.5 us
    dot_general x26, matrix products, extend(): product = jnp.dot(values, weights, preferred_element_type=jnp.float32)  23.4 us
    ppermute x1, waiting for transfers between devices, shards(): received = lax.ppermute(payload, 'freq', partner)  16.6 us
    all_to_all x1, waiting for transfers between devices, shards(): lax.all_to_all(image.astype(jnp.bfloat16), 'depth', split_axis=0, concat_...  13.2 us
    ppermute x23, waiting for transfers between devices, shards(): sent[parity, round_index] = lax.ppermute(outcome[parity], 'depth', pairs)  4.91 us
    squeeze x1, local copies, waits for them, and re-layouts, shards(): weights = jnp.concatenate([extrap[0, 0, 0], extrap[0, 0, 1]], axis=1)  4.66 us
    unnamed x22, local copies, waits for them, and re-layouts  3.62 us
  transfers between devices with their start and end apart: 26, of which 6 were waited for; matrix products, arithmetic and copies ran while one was open for 15% of the time, Pallas kernels for 0%

profile of v1, /device:TPU:0, one launch (start us, length us, event | category | flops | bytes accessed | tf_op | source)
XLA Modules:
  0.0 166.3 jit_solution(17573811211560804621)
XLA Ops:
  1.4 1.1 copy.18
  2.6 4.7 %slice_bitcast_fusion.1 = (bf16[1024,1024]{1,0:T(8,128)(2,1)}, bf16[1024,1024]{1,0:T(8,128)(2,1)}) fusion(bf16[1,1,2,1024,1024]{4,3,2,1,0:T(8,128)(2,1)} %param.20), kind=kLoop, calls=%fused_computation.5 | loop fusion | bytes 8388608 | tf_op jit(solution)/shard_map/squeeze | solution.py:42
  7.2 1.6 gather_fusion
  9.0 0.7 slice_bitcast_fusion.5
  9.7 0.8 copy-done.2
  10.5 2.5 %fusion.59 = f32[128,2048]{1,0:T(8,128)S(1)} fusion(bf16[32,1024]{1,0:T(8,128)(2,1)S(1)} %get-tuple-element.171, bf16[32,1024]{1,0:T(8,128)(2,1)S(1)} %get-tuple-element.174, bf16[32,1024]{1,0:T(8,128)(2,1)S(1)} %get-tuple-element.172, bf16[32,1024]{1,0:T(8,128)(2,1)S(1)} %get-tuple-element.173, bf16[1024,1024]{1,0:T(8,128)(2,1)} %get-tuple-element.102, ...), kind=kOutput, calls=%fused_computation.123 | convolution fusion | flops 546308096 | bytes 5505024 | tf_op jit(solution)/shard_map/dot_general | solution.py:53
  13.0 5.6 %collective-permute-start = (bf16[128,1024]{1,0:T(8,128)(2,1)S(1)}, bf16[128,1024]{1,0:T(8,128)(2,1)}, u32[]{:S(2)}, u32[]{:S(2)}) collective-permute-start(bf16[128,1024]{1,0:T(8,128)(2,1)S(1)} %pad_maximum_fusion.1), channel_id=1, source_target_pairs={{0,4},{1,5},{2,6},{3,7}} | collective-permute-start | bytes 786440 | tf_op jit(solution)/shard_map/ppermute | solution.py:76
  18.6 0.7 fusion.67
  19.5 2.0 %collective-permute-start.1 = (bf16[128,1024]{1,0:T(8,128)(2,1)S(1)}, bf16[128,1024]{1,0:T(8,128)(2,1)}, u32[]{:S(2)}, u32[]{:S(2)}) collective-permute-start(bf16[128,1024]{1,0:T(8,128)(2,1)S(1)} %pad_maximum_fusion.2), channel_id=1, source_target_pairs={{0,4},{1,5},{2,6},{3,7}} | collective-permute-start | bytes 786440 | tf_op jit(solution)/shard_map/ppermute | solution.py:76
  21.5 0.7 fusion.76
  23.0 2.0 %collective-permute-start.3 = (bf16[128,1024]{1,0:T(8,128)(2,1)}, bf16[128,1024]{1,0:T(8,128)(2,1)}, u32[]{:S(2)}, u32[]{:S(2)}) collective-permute-start(bf16[128,1024]{1,0:T(8,128)(2,1)} %pad_maximum_fusion.4), channel_id=1, source_target_pairs={{0,4},{1,5},{2,6},{3,7}} | collective-permute-start | bytes 786440 | tf_op jit(solution)/shard_map/ppermute | solution.py:76
  26.0 1.3 copy-done.5
  27.3 1.7 %fusion.141 = f32[128,2048]{1,0:T(8,128)S(1)} fusion(bf16[128,1024]{1,0:T(8,128)(2,1)} %collective-permute-done, bf16[1024,1024]{1,0:T(8,128)(2,1)S(1)} %copy-done.5, bf16[1024,1024]{1,0:T(8,128)(2,1)S(1)} %copy-done.3), kind=kOutput, calls=%fused_computation.278 | convolution fusion | flops 545259520 | bytes 5505024 | tf_op jit(solution)/shard_map/dot_general | solution.py:53
  30.2 1.7 %fusion.140 = f32[128,2048]{1,0:T(8,128)S(1)} fusion(bf16[128,1024]{1,0:T(8,128)(2,1)} %collective-permute-done.1, bf16[1024,1024]{1,0:T(8,128)(2,1)S(1)} %copy-done.5, bf16[1024,1024]{1,0:T(8,128)(2,1)S(1)} %copy-done.3), kind=kOutput, calls=%fused_computation.277 | convolution fusion | flops 545259520 | bytes 5505024 | tf_op jit(solution)/shard_map/dot_general | solution.py:53
  32.0 2.8 %collective-permute-done.3 = bf16[128,1024]{1,0:T(8,128)(2,1)} collective-permute-done((bf16[128,1024]{1,0:T(8,128)(2,1)}, bf16[128,1024]{1,0:T(8,128)(2,1)}, u32[]{:S(2)}, u32[]{:S(2)}) %collective-permute-start.3) | collective-permute-done | bytes 262176 | tf_op jit(solution)/shard_map/ppermute | solution.py:76
  34.8 1.7 %fusion.139 = f32[128,2048]{1,0:T(8,128)S(1)} fusion(bf16[128,1024]{1,0:T(8,128)(2,1)} %collective-permute-done.3, bf16[1024,1024]{1,0:T(8,128)(2,1)S(1)} %copy-done.5, bf16[1024,1024]{1,0:T(8,128)(2,1)S(1)} %copy-done.3), kind=kOutput, calls=%fused_computation.276 | convolution fusion | flops 545259520 | bytes 5505024 | tf_op jit(solution)/shard_map/dot_general | solution.py:53
  39.0 5.7 %collective-permute-start.5 = (bf16[128,1024]{1,0:T(8,128)(2,1)S(1)}, bf16[128,1024]{1,0:T(8,128)(2,1)S(1)}, u32[]{:S(2)}, u32[]{:S(2)}) collective-permute-start(bf16[128,1024]{1,0:T(8,128)(2,1)S(1)} %pad_maximum_fusion.6), channel_id=1, source_target_pairs={{0,4},{8,12},{1,5},{9,13},{2,6},{10,14},{3,7},{11,15}} | collective-permute-start | bytes 786440 | tf_op jit(solution)/shard_map/ppermute | solution.py:76
  44.7 0.7 fusion.138
  45.5 0.7 fusion.136
  47.8 1.5 collective-permute-done.5
  49.3 0.7 fusion.137
  50.2 0.9 collective-permute-start.8
  51.0 0.7 fusion.135
  51.8 0.7 fusion.133
  54.2 0.7 fusion.134
  55.7 0.7 fusion.132
  56.6 0.7 fusion.130
  58.9 0.7 fusion.131
  60.4 0.7 fusion.129
  61.2 0.7 fusion.127
  63.6 0.7 fusion.128
  65.1 0.7 fusion.126
  65.9 0.7 fusion.124
  68.2 0.7 fusion.125
  69.0 0.9 collective-permute-start.20
  70.0 0.7 fusion.123
  70.7 0.7 fusion.121
  71.6 0.7 fusion.122
  73.3 0.7 fusion.120
  74.5 1.6 collective-permute-start.23
  76.5 16.6 %collective-permute-done.23 = bf16[272,1536]{1,0:T(8,128)(2,1)S(1)} collective-permute-done((bf16[272,1536]{1,0:T(8,128)(2,1)S(1)}, bf16[272,1536]{1,0:T(8,128)(2,1)S(1)}, u32[]{:S(2)}, u32[]{:S(2)}) %collective-permute-start.23) | collective-permute-done | bytes 835616 | tf_op jit(solution)/shard_map/ppermute | solution.py:104
  94.9 1.9 %collective-permute-done.24 = bf16[256,1024]{1,0:T(8,128)(2,1)S(1)} collective-permute-done((bf16[256,1024]{1,0:T(8,128)(2,1)S(1)}, bf16[256,1024]{1,0:T(8,128)(2,1)S(1)}, u32[]{:S(2)}, u32[]{:S(2)}) %collective-permute-start.24) | collective-permute-done | bytes 524320 | tf_op jit(solution)/shard_map/ppermute | solution.py:116
  96.8 1.1 add_convert_fusion
  97.9 50.1 %all-to-all-start = ((bf16[8,32,1024]{2,1,0:T(8,128)(2,1)}), bf16[8,32,1024]{2,1,0:T(8,128)(2,1)}, u32[]{:S(2)}, u32[]{:S(2)}) async-start(bf16[8,32,1024]{2,1,0:T(8,128)(2,1)} %bitcast.78), calls=%async_computation | async-start | bytes 1048576 | tf_op jit(solution)/shard_map/all_to_all | solution.py:118
  148.3 1.3 bitcast_compare_fusion
  149.7 13.2 %all-to-all-done = bf16[8,32,1024]{2,1,0:T(8,128)(2,1)} async-done(((bf16[8,32,1024]{2,1,0:T(8,128)(2,1)}), bf16[8,32,1024]{2,1,0:T(8,128)(2,1)}, u32[]{:S(2)}, u32[]{:S(2)}) %all-to-all-start) | async-done | bytes 524320 | tf_op jit(solution)/shard_map/all_to_all | solution.py:118
  162.8 2.3 %fusion.4 = f32[8,32,8,256]{3,1,2,0:T(8,128)S(1)} fusion(pred[8,256,1024,1]{2,1,0,3:T(32,128)(4,1)S(1)} %bitcast.170, bf16[8,32,1024]{2,1,0:T(8,128)(2,1)} %all-to-all-done), kind=kOutput, calls=%fused_computation.13 | convolution fusion | flops 1073741824 | bytes 4718592 | tf_op jit(solution)/shard_map/dot_general | solution.py:129
  165.5 0.9 copy.13
  (145 shorter events, 20.5 us)
Async XLA Ops:
  0.0 7.2 %copy-start = (bf16[1,128,2,1024]{3,2,1,0:T(2,128)(2,1)S(1)}, bf16[1,128,2,1024]{3,2,1,0:T(2,128)(2,1)}, u32[]{:S(2)}) copy-start(bf16[1,128,2,1024]{3,2,1,0:T(2,128)(2,1)} %param.21) | copy-start | bytes 1572868
  8.8 1.6 copy-start.2
  10.5 8.2 %copy-start.4 = (bf16[1024,1024]{1,0:T(8,128)(2,1)S(1)}, bf16[1024,1024]{1,0:T(8,128)(2,1)}, u32[]{:S(2)}) copy-start(bf16[1024,1024]{1,0:T(8,128)(2,1)} %get-tuple-element.102) | copy-start | bytes 6291460
  13.0 12.9 %collective-permute-start = (bf16[128,1024]{1,0:T(8,128)(2,1)S(1)}, bf16[128,1024]{1,0:T(8,128)(2,1)}, u32[]{:S(2)}, u32[]{:S(2)}) collective-permute-start(bf16[128,1024]{1,0:T(8,128)(2,1)S(1)} %pad_maximum_fusion.1), channel_id=1, source_target_pairs={{0,4},{1,5},{2,6},{3,7}} | collective-permute-start | bytes 786440 | tf_op jit(solution)/shard_map/ppermute | solution.py:76
  19.5 10.8 %collective-permute-start.1 = (bf16[128,1024]{1,0:T(8,128)(2,1)S(1)}, bf16[128,1024]{1,0:T(8,128)(2,1)}, u32[]{:S(2)}, u32[]{:S(2)}) collective-permute-start(bf16[128,1024]{1,0:T(8,128)(2,1)S(1)} %pad_maximum_fusion.2), channel_id=1, source_target_pairs={{0,4},{1,5},{2,6},{3,7}} | collective-permute-start | bytes 786440 | tf_op jit(solution)/shard_map/ppermute | solution.py:76
  22.2 3.8 %copy-start.3 = (bf16[1024,1024]{1,0:T(8,128)(2,1)S(1)}, bf16[1024,1024]{1,0:T(8,128)(2,1)}, u32[]{:S(2)}) copy-start(bf16[1024,1024]{1,0:T(8,128)(2,1)} %get-tuple-element.101) | copy-start | bytes 6291460
  23.0 11.8 %collective-permute-start.3 = (bf16[128,1024]{1,0:T(8,128)(2,1)}, bf16[128,1024]{1,0:T(8,128)(2,1)}, u32[]{:S(2)}, u32[]{:S(2)}) collective-permute-start(bf16[128,1024]{1,0:T(8,128)(2,1)} %pad_maximum_fusion.4), channel_id=1, source_target_pairs={{0,4},{1,5},{2,6},{3,7}} | collective-permute-start | bytes 786440 | tf_op jit(solution)/shard_map/ppermute | solution.py:76
  25.7 1.6 copy-start.5
  29.1 9.1 %collective-permute-start.2 = (bf16[128,1024]{1,0:T(8,128)(2,1)S(1)}, bf16[128,1024]{1,0:T(8,128)(2,1)S(1)}, u32[]{:S(2)}, u32[]{:S(2)}) collective-permute-start(bf16[128,1024]{1,0:T(8,128)(2,1)S(1)} %pad_maximum_fusion.3), channel_id=1, source_target_pairs={{4,8},{5,9},{6,10},{7,11}} | collective-permute-start | bytes 786440 | tf_op jit(solution)/shard_map/ppermute | solution.py:76
  36.5 1.7 %copy-start.7 = (bf16[32,1024]{1,0:T(8,128)(2,1)S(1)}, bf16[32,1024]{1,0:T(8,128)(2,1)}, u32[]{:S(2)}) copy-start(bf16[32,1024]{1,0:T(8,128)(2,1)} %get-tuple-element.179) | copy-start | bytes 196612
  36.5 1.7 %copy-start.8 = (bf16[32,1024]{1,0:T(8,128)(2,1)S(1)}, bf16[32,1024]{1,0:T(8,128)(2,1)}, u32[]{:S(2)}) copy-start(bf16[32,1024]{1,0:T(8,128)(2,1)} %get-tuple-element.180) | copy-start | bytes 196612
  36.6 8.1 %collective-permute-start.4 = (bf16[128,1024]{1,0:T(8,128)(2,1)S(1)}, bf16[128,1024]{1,0:T(8,128)(2,1)S(1)}, u32[]{:S(2)}, u32[]{:S(2)}) collective-permute-start(bf16[128,1024]{1,0:T(8,128)(2,1)S(1)} %pad_maximum_fusion.5), channel_id=1, source_target_pairs={{4,8},{5,9},{6,10},{7,11}} | collective-permute-start | bytes 786440 | tf_op jit(solution)/shard_map/ppermute | solution.py:76
  37.3 8.2 %collective-permute-start.6 = (bf16[128,1024]{1,0:T(8,128)(2,1)S(1)}, bf16[128,1024]{1,0:T(8,128)(2,1)S(1)}, u32[]{:S(2)}, u32[]{:S(2)}) collective-permute-start(bf16[128,1024]{1,0:T(8,128)(2,1)S(1)} %pad_maximum_fusion.7), channel_id=1, source_target_pairs={{4,8},{5,9},{6,10},{7,11}} | collective-permute-start | bytes 786440 | tf_op jit(solution)/shard_map/ppermute | solution.py:76
  39.0 10.3 %collective-permute-start.5 = (bf16[128,1024]{1,0:T(8,128)(2,1)S(1)}, bf16[128,1024]{1,0:T(8,128)(2,1)S(1)}, u32[]{:S(2)}, u32[]{:S(2)}) collective-permute-start(bf16[128,1024]{1,0:T(8,128)(2,1)S(1)} %pad_maximum_fusion.6), channel_id=1, source_target_pairs={{0,4},{8,12},{1,5},{9,13},{2,6},{10,14},{3,7},{11,15}} | collective-permute-start | bytes 786440 | tf_op jit(solution)/shard_map/ppermute | solution.py:76
  46.3 4.7 %collective-permute-start.7 = (bf16[128,1024]{1,0:T(8,128)(2,1)S(1)}, bf16[128,1024]{1,0:T(8,128)(2,1)S(1)}, u32[]{:S(2)}, u32[]{:S(2)}) collective-permute-start(bf16[128,1024]{1,0:T(8,128)(2,1)S(1)} %pad_maximum_fusion.8), channel_id=1, source_target_pairs={{8,12},{9,13},{10,14},{11,15}} | collective-permute-start | bytes 786440 | tf_op jit(solution)/shard_map/ppermute | solution.py:76
  47.0 4.8 %collective-permute-start.9 = (bf16[128,1024]{1,0:T(8,128)(2,1)S(1)}, bf16[128,1024]{1,0:T(8,128)(2,1)S(1)}, u32[]{:S(2)}, u32[]{:S(2)}) collective-permute-start(bf16[128,1024]{1,0:T(8,128)(2,1)S(1)} %pad_maximum_fusion.10), channel_id=1, source_target_pairs={{8,12},{9,13},{10,14},{11,15}} | collective-permute-start | bytes 786440 | tf_op jit(solution)/shard_map/ppermute | solution.py:76
  50.2 4.1 %collective-permute-start.8 = (bf16[128,1024]{1,0:T(8,128)(2,1)S(1)}, bf16[128,1024]{1,0:T(8,128)(2,1)S(1)}, u32[]{:S(2)}, u32[]{:S(2)}) collective-permute-start(bf16[128,1024]{1,0:T(8,128)(2,1)S(1)} %pad_maximum_fusion.9), channel_id=1, source_target_pairs={{4,8},{12,16},{5,9},{13,17},{6,10},{14,18},{7,11},{15,19}} | collective-permute-start | bytes 786440 | tf_op jit(solution)/shard_map/ppermute | solution.py:76
  52.7 3.1 %collective-permute-start.10 = (bf16[128,1024]{1,0:T(8,128)(2,1)S(1)}, bf16[128,1024]{1,0:T(8,128)(2,1)S(1)}, u32[]{:S(2)}, u32[]{:S(2)}) collective-permute-start(bf16[128,1024]{1,0:T(8,128)(2,1)S(1)} %pad_maximum_fusion.11), channel_id=1, source_target_pairs={{12,16},{13,17},{14,18},{15,19}} | collective-permute-start | bytes 786440 | tf_op jit(solution)/shard_map/ppermute | solution.py:76
  53.4 3.2 %collective-permute-start.12 = (bf16[128,1024]{1,0:T(8,128)(2,1)S(1)}, bf16[128,1024]{1,0:T(8,128)(2,1)S(1)}, u32[]{:S(2)}, u32[]{:S(2)}) collective-permute-start(bf16[128,1024]{1,0:T(8,128)(2,1)S(1)} %pad_maximum_fusion.13), channel_id=1, source_target_pairs={{12,16},{13,17},{14,18},{15,19}} | collective-permute-start | bytes 786440 | tf_op jit(solution)/shard_map/ppermute | solution.py:76
  55.0 3.8 %collective-permute-start.11 = (bf16[128,1024]{1,0:T(8,128)(2,1)S(1)}, bf16[128,1024]{1,0:T(8,128)(2,1)S(1)}, u32[]{:S(2)}, u32[]{:S(2)}) collective-permute-start(bf16[128,1024]{1,0:T(8,128)(2,1)S(1)} %pad_maximum_fusion.12), channel_id=1, source_target_pairs={{8,12},{16,20},{9,13},{17,21},{10,14},{18,22},{11,15},{19,23}} | collective-permute-start | bytes 786440 | tf_op jit(solution)/shard_map/ppermute | solution.py:76
  57.4 3.0 %collective-permute-start.13 = (bf16[128,1024]{1,0:T(8,128)(2,1)S(1)}, bf16[128,1024]{1,0:T(8,128)(2,1)S(1)}, u32[]{:S(2)}, u32[]{:S(2)}) collective-permute-start(bf16[128,1024]{1,0:T(8,128)(2,1)S(1)} %pad_maximum_fusion.14), channel_id=1, source_target_pairs={{16,20},{17,21},{18,22},{19,23}} | collective-permute-start | bytes 786440 | tf_op jit(solution)/shard_map/ppermute | solution.py:76
  58.1 3.1 %collective-permute-start.15 = (bf16[128,1024]{1,0:T(8,128)(2,1)S(1)}, bf16[128,1024]{1,0:T(8,128)(2,1)S(1)}, u32[]{:S(2)}, u32[]{:S(2)}) collective-permute-start(bf16[128,1024]{1,0:T(8,128)(2,1)S(1)} %pad_maximum_fusion.16), channel_id=1, source_target_pairs={{16,20},{17,21},{18,22},{19,23}} | collective-permute-start | bytes 786440 | tf_op jit(solution)/shard_map/ppermute | solution.py:76
  59.7 3.9 %collective-permute-start.14 = (bf16[128,1024]{1,0:T(8,128)(2,1)S(1)}, bf16[128,1024]{1,0:T(8,128)(2,1)S(1)}, u32[]{:S(2)}, u32[]{:S(2)}) collective-permute-start(bf16[128,1024]{1,0:T(8,128)(2,1)S(1)} %pad_maximum_fusion.15), channel_id=1, source_target_pairs={{12,16},{20,24},{13,17},{21,25},{14,18},{22,26},{15,19},{23,27}} | collective-permute-start | bytes 786440 | tf_op jit(solution)/shard_map/ppermute | solution.py:76
  62.0 3.1 %collective-permute-start.16 = (bf16[128,1024]{1,0:T(8,128)(2,1)S(1)}, bf16[128,1024]{1,0:T(8,128)(2,1)S(1)}, u32[]{:S(2)}, u32[]{:S(2)}) collective-permute-start(bf16[128,1024]{1,0:T(8,128)(2,1)S(1)} %pad_maximum_fusion.17), channel_id=1, source_target_pairs={{20,24},{21,25},{22,26},{23,27}} | collective-permute-start | bytes 786440 | tf_op jit(solution)/shard_map/ppermute | solution.py:76
  62.7 3.2 %collective-permute-start.18 = (bf16[128,1024]{1,0:T(8,128)(2,1)S(1)}, bf16[128,1024]{1,0:T(8,128)(2,1)S(1)}, u32[]{:S(2)}, u32[]{:S(2)}) collective-permute-start(bf16[128,1024]{1,0:T(8,128)(2,1)S(1)} %pad_maximum_fusion.19), channel_id=1, source_target_pairs={{20,24},{21,25},{22,26},{23,27}} | collective-permute-start | bytes 786440 | tf_op jit(solution)/shard_map/ppermute | solution.py:76
  64.4 3.8 %collective-permute-start.17 = (bf16[128,1024]{1,0:T(8,128)(2,1)S(1)}, bf16[128,1024]{1,0:T(8,128)(2,1)S(1)}, u32[]{:S(2)}, u32[]{:S(2)}) collective-permute-start(bf16[128,1024]{1,0:T(8,128)(2,1)S(1)} %pad_maximum_fusion.18), channel_id=1, source_target_pairs={{16,20},{24,28},{17,21},{25,29},{18,22},{26,30},{19,23},{27,31}} | collective-permute-start | bytes 786440 | tf_op jit(solution)/shard_map/ppermute | solution.py:76
  66.7 3.2 %collective-permute-start.19 = (bf16[128,1024]{1,0:T(8,128)(2,1)S(1)}, bf16[128,1024]{1,0:T(8,128)(2,1)S(1)}, u32[]{:S(2)}, u32[]{:S(2)}) collective-permute-start(bf16[128,1024]{1,0:T(8,128)(2,1)S(1)} %pad_maximum_fusion.20), channel_id=1, source_target_pairs={{24,28},{25,29},{26,30},{27,31}} | collective-permute-start | bytes 786440 | tf_op jit(solution)/shard_map/ppermute | solution.py:76
  67.4 3.2 %collective-permute-start.21 = (bf16[128,1024]{1,0:T(8,128)(2,1)S(1)}, bf16[128,1024]{1,0:T(8,128)(2,1)S(1)}, u32[]{:S(2)}, u32[]{:S(2)}) collective-permute-start(bf16[128,1024]{1,0:T(8,128)(2,1)S(1)} %pad_maximum_fusion.22), channel_id=1, source_target_pairs={{24,28},{25,29},{26,30},{27,31}} | collective-permute-start | bytes 786440 | tf_op jit(solution)/shard_map/ppermute | solution.py:76
  69.0 2.5 %collective-permute-start.20 = (bf16[128,1024]{1,0:T(8,128)(2,1)S(1)}, bf16[128,1024]{1,0:T(8,128)(2,1)S(1)}, u32[]{:S(2)}, u32[]{:S(2)}) collective-permute-start(bf16[128,1024]{1,0:T(8,128)(2,1)S(1)} %pad_maximum_fusion.21), channel_id=1, source_target_pairs={{20,24},{21,25},{22,26},{23,27}} | collective-permute-start | bytes 786440 | tf_op jit(solution)/shard_map/ppermute | solution.py:76
  72.4 0.9 collective-permute-start.22
  74.5 18.6 %collective-permute-start.23 = (bf16[272,1536]{1,0:T(8,128)(2,1)S(1)}, bf16[272,1536]{1,0:T(8,128)(2,1)S(1)}, u32[]{:S(2)}, u32[]{:S(2)}) collective-permute-start(bf16[272,1536]{1,0:T(8,128)(2,1)S(1)} %fusion.2), channel_id=1, source_target_pairs={{0,2},{1,3},{2,0},{3,1},{4,6},{5,7},{6,4},{7,5},{8,10},{9,11},{10,... | collective-permute-start | bytes 2506760 | tf_op jit(solution)/shard_map/ppermute | solution.py:104
  94.8 53.1 %copy-start.6 = (s32[1024,256]{1,0:T(8,128)S(1)}, s32[1024,256]{1,0:T(8,128)}, u32[]{:S(2)}) copy-start(s32[1024,256]{1,0:T(8,128)} %param.25) | copy-start | bytes 3145732
  94.8 2.0 %collective-permute-start.24 = (bf16[256,1024]{1,0:T(8,128)(2,1)S(1)}, bf16[256,1024]{1,0:T(8,128)(2,1)S(1)}, u32[]{:S(2)}, u32[]{:S(2)}) collective-permute-start(bf16[256,1024]{1,0:T(8,128)(2,1)S(1)} %select_convert_fusion), channel_id=1, source_target_pairs={{0,1},{1,0},{2,3},{3,2},{4,5},{5,4},{6,7},{7,6},{8,9},{9,8},{10,11... | collective-permute-start | bytes 1572872 | tf_op jit(solution)/shard_map/ppermute | solution.py:116
  97.9 65.0 %all-to-all-start = ((bf16[8,32,1024]{2,1,0:T(8,128)(2,1)}), bf16[8,32,1024]{2,1,0:T(8,128)(2,1)}, u32[]{:S(2)}, u32[]{:S(2)}) async-start(bf16[8,32,1024]{2,1,0:T(8,128)(2,1)} %bitcast.78), calls=%async_computation | async-start | bytes 1048576 | tf_op jit(solution)/shard_map/all_to_all | solution.py:118
  165.2 1.1 copy-start.1

commit v2 on v1

v2 whole, which is shorter than its diff:
```python
import math

import jax
import jax.numpy as jnp
from jax import lax
from jax.experimental import pallas as pl
from jax.experimental.pallas import tpu as pltpu
from jax.sharding import PartitionSpec as P

CHUNKS = 8
GROUPS = (4, 2, 1, 1)

WHOLE = pl.BlockSpec(memory_space=pltpu.VMEM)
FAR = pl.BlockSpec(memory_space=pltpu.HBM)
LOOSE = pl.BlockSpec(memory_space=pl.ANY)


def first_round(level):
    return 3 * (level // 2) + level % 2


def handled(round_index, level, chunk_count):
    return 0 <= round_index - first_round(level) < chunk_count


def march(values, extrap_ref, out_ref):
    half = out_ref.shape[0] // 2
    real = jnp.dot(values, extrap_ref[0], preferred_element_type=jnp.float32)
    imag = jnp.dot(values, extrap_ref[1], preferred_element_type=jnp.float32)
    out_ref[:half] = (real[:half] - imag[half:]).astype(out_ref.dtype)
    out_ref[half:] = (imag[:half] + real[half:]).astype(out_ref.dtype)


def extend(arrived, extrap, order, above=None):
    rows, points = arrived.shape
    above = above or ()

    def kernel(arrived_ref, extrap_ref, order_ref, *refs):
        values = arrived_ref[...]
        if above:
            values = jnp.where(refs[1][...] > 0, refs[0][0], values)
        march(values, extrap_ref, refs[-1])

    return pl.pallas_call(
        kernel,
        out_shape=jax.ShapeDtypeStruct((rows, points), jnp.bfloat16),
        in_specs=[WHOLE, WHOLE, LOOSE] + [WHOLE] * len(above),
        out_specs=WHOLE,
        compiler_params=pltpu.CompilerParams(vmem_limit_bytes=12 << 20),
        cost_estimate=pl.CostEstimate(
            flops=4 * rows * points * points, bytes_accessed=4 * points * points, transcendentals=0
        ),
    )(arrived, extrap, order, *above)


def picked(shot_ref, source_ref, span, component):
    shot_count = source_ref.shape[0]
    count = span.stop - span.start
    pick = (
        shot_ref[span][None, :] == lax.broadcasted_iota(jnp.int32, (shot_count, count), 0)
    ).astype(jnp.bfloat16)
    return lax.dot_general(
        pick,
        source_ref[:, component, :],
        (((0,), (0,)), ((), ())),
        preferred_element_type=jnp.float32,
    ).astype(jnp.bfloat16)


def fill(out_ref, shot_ref, source_ref, record_ref, span):
    part = out_ref.shape[0] // 4
    out_ref[:part] = picked(shot_ref, source_ref, span, 0)
    out_ref[part : 2 * part] = record_ref[span, 1, :]
    out_ref[2 * part : 3 * part] = picked(shot_ref, source_ref, span, 1)
    out_ref[3 * part :] = record_ref[span, 0, :]


def head(extrap, sources, records, shots, part):
    points = extrap.shape[2]

    def kernel(
        extrap_hbm, source_hbm, record_hbm, shot_hbm, out_ref,
        extrap_ref, source_ref, record_ref, shot_ref, chunk_ref, sems,
    ):
        copies = [
            pltpu.make_async_copy(shot_hbm, shot_ref, sems.at[0]),
            pltpu.make_async_copy(source_hbm, source_ref, sems.at[1]),
            pltpu.make_async_copy(record_hbm.at[pl.ds(0, part)], record_ref, sems.at[2]),
            pltpu.make_async_copy(extrap_hbm, extrap_ref, sems.at[3]),
        ]
        for copy in copies:
            copy.start()
        for copy in copies[:3]:
            copy.wait()
        fill(chunk_ref, shot_ref, source_ref, record_ref, slice(0, part))
        copies[3].wait()
        march(chunk_ref[...], extrap_ref, out_ref)

    return pl.pallas_call(
        kernel,
        out_shape=jax.ShapeDtypeStruct((4 * part, points), jnp.bfloat16),
        in_specs=[FAR] * 4,
        out_specs=WHOLE,
        scratch_shapes=[
            pltpu.VMEM(extrap.shape, extrap.dtype),
            pltpu.VMEM(sources.shape, sources.dtype),
            pltpu.VMEM((part,) + records.shape[1:], records.dtype),
            pltpu.VMEM(shots.shape, shots.dtype),
            pltpu.VMEM((4 * part, points), jnp.bfloat16),
            pltpu.SemaphoreType.DMA((4,)),
        ],
        compiler_params=pltpu.CompilerParams(vmem_limit_bytes=56 << 20),
    )(extrap, sources, records, shots)


def surface(sources, records, shots, chunk_count):
    shot_count, _, points = sources.shape
    part = shot_count // chunk_count

    def kernel(source_ref, record_ref, shot_ref, out_ref):
        everything = slice(0, shot_count)
        for place, values in (
            (0, picked(shot_ref, source_ref, everything, 0)),
            (1, record_ref[:, 1, :]),
            (2, picked(shot_ref, source_ref, everything, 1)),
            (3, record_ref[:, 0, :]),
        ):
            for chunk in range(chunk_count):
                out_ref[chunk, place * part : (place + 1) * part] = values[
                    chunk * part : (chunk + 1) * part
                ]

    return pl.pallas_call(
        kernel,
        out_shape=jax.ShapeDtypeStruct((chunk_count, 4 * part, points), jnp.bfloat16),
        in_specs=[WHOLE] * 3,
        out_specs=WHOLE,
        compiler_params=pltpu.CompilerParams(vmem_limit_bytes=12 << 20),
    )(sources, records, shots)


def correlate(own, theirs, upper, own_scale, unit, part):
    points = own[0].shape[1]
    width = points // 2
    group_count = len(own)

    def stacks(ref, chunks, column):
        sources, records = [], []
        for chunk in range(chunks):
            row = 4 * part * chunk
            for first, second in ((0, 3), (2, 1)):
                sources.append(ref[row + first * part : row + (first + 1) * part, column])
                records.append(ref[row + second * part : row + (second + 1) * part, :])
        return sources, records

    def kernel(*refs):
        own_refs, their_refs = refs[:group_count], refs[group_count : 2 * group_count]
        upper_ref, own_scale_ref, out_ref = refs[2 * group_count :]
        note = own_refs[0].shape[0]
        their_scale = their_refs[0][note : note + 16, :128].astype(jnp.float32)[:1, :1] * unit

        def side(these, column):
            sources, records = [], []
            for ref, mine in zip(these, own_refs):
                first, second = stacks(ref, mine.shape[0] // (4 * part), column)
                sources += first
                records += second
            return lax.dot_general(
                jnp.concatenate(sources, axis=0),
                jnp.concatenate(records, axis=0),
                (((0,), (0,)), ((), ())),
                preferred_element_type=jnp.float32,
            )

        for value, column in ((0, slice(0, width)), (1, slice(width, points))):

            @pl.when(upper_ref[0] == value)
            def _():
                total = side(own_refs, column) * own_scale_ref[...]
                total += side(their_refs, column) * their_scale
                out_ref[...] = total.astype(out_ref.dtype)

    return pl.pallas_call(
        kernel,
        out_shape=jax.ShapeDtypeStruct((width, points), jnp.bfloat16),
        in_specs=[WHOLE] * (2 * group_count) + [pl.BlockSpec(memory_space=pltpu.SMEM)] + [WHOLE],
        out_specs=WHOLE,
        compiler_params=pltpu.CompilerParams(vmem_limit_bytes=24 << 20),
    )(*own, *theirs, upper, own_scale)


def angles(panel, angle_lag, depth_count):
    angle_count = angle_lag.shape[1]
    row_count = panel.shape[0] // depth_count
    points = panel.shape[1]

    def kernel(panel_ref, lag_ref, out_ref):
        total = None
        for lag in range(depth_count):
            column = (lag_ref[...] == lag).astype(jnp.bfloat16)
            skip = lag * row_count
            if row_count % 16 == 0:
                term = jnp.dot(panel_ref[skip:], column, preferred_element_type=jnp.float32)
            else:
                term = jnp.dot(panel_ref[...], column, preferred_element_type=jnp.float32)[skip:]
            if total is None:
                total = term
            elif skip:
                kept = total.shape[0] - skip
                total = jnp.concatenate([total[:kept] + term, total[kept:]], axis=0)
        total = total * (1.0 / math.sqrt(points))
        for depth in range(depth_count):
            out_ref[:, depth, :] = total[depth * row_count : (depth + 1) * row_count]

    return pl.pallas_call(
        kernel,
        out_shape=jax.ShapeDtypeStruct((row_count, depth_count, angle_count), jnp.float32),
        in_specs=[WHOLE] * 2,
        out_specs=WHOLE,
        compiler_params=pltpu.CompilerParams(vmem_limit_bytes=24 << 20),
    )(panel, angle_lag)


def shards(extrap, source_field, record_field, shot_of_record, freq_index, angle_lag):
    level = lax.axis_index("depth")
    depth_count = lax.axis_size("depth")
    freq_count = lax.axis_size("freq")
    freq_slot = lax.axis_index("freq")
    points = source_field.shape[3]
    shot_count = source_field.shape[1]
    chunk_count = CHUNKS
    part = shot_count // chunk_count
    rows = 4 * part

    operator = extrap[0, 0]
    sources, records = source_field[0], record_field[0]
    order = head(operator, sources, records, shot_of_record, part)
    above = surface(sources, records, shot_of_record, chunk_count)

    number = freq_index[0].astype(jnp.float32) + 1.0
    span = freq_count // 2
    upper = (freq_slot // span) % 2 == 1
    partner = [(slot, slot ^ span) for slot in range(freq_count)]

    at_surface = jnp.full((rows, points), level == 0).astype(jnp.bfloat16)
    my_first = 3 * (level // 2) + level % 2
    finished = jnp.zeros((chunk_count + 2, rows, points), jnp.bfloat16)
    sent = {}
    own, theirs = [], []
    start = 0
    round_count = first_round(depth_count - 1) + chunk_count
    for round_index in range(round_count):
        outcome = {}
        chunk = round_index - my_first
        for parity in (0, 1):
            levels = [
                z for z in range(parity, depth_count, 2) if handled(round_index, z, chunk_count)
            ]
            if not levels:
                continue
            if round_index or parity:
                arrived = sent.get((1 - parity, round_index - 2 + parity))
                entering = None
                if parity == 0 and round_index < chunk_count:
                    entering = (above[round_index : round_index + 1], at_surface)
                    if arrived is None:
                        arrived, entering = above[round_index], None
                order = extend(arrived, operator, order, entering)
            outcome[parity] = order
            pairs = [(z, z + 1) for z in levels if z + 1 < depth_count]
            if pairs:
                sent[parity, round_index] = lax.ppermute(order, "depth", pairs)
        if len(outcome) == 2:
            kept = jnp.where(level % 2 == 0, outcome[0], outcome[1])
        else:
            kept = next(iter(outcome.values()))
        slot = jnp.clip(chunk, -1, chunk_count) + 1
        finished = lax.dynamic_update_index_in_dim(finished, kept, slot, 0)
        size = GROUPS[len(own)] if len(own) < len(GROUPS) else 0
        if size and round_index - first_round(depth_count - 1) == start + size - 1:
            done = finished[1 + start : 1 + start + size].reshape(size * rows, points)
            own.append(done)
            payload = done
            if start == 0:
                note = jnp.full((16, points), number, jnp.float32).astype(jnp.bfloat16)
                payload = jnp.concatenate([done, note], axis=0)
            payload, order = lax.optimization_barrier((payload, order))
            received = lax.ppermute(payload, "freq", partner)
            theirs.append(received)
            start += size

    scale = 1.0 / (8 * freq_count) / math.sqrt(shot_count * freq_count)
    image = correlate(
        own,
        theirs,
        upper.astype(jnp.int32).reshape(1),
        (number * scale).reshape(1, 1),
        scale,
        part,
    )
    width = points // 2
    span //= 2
    while span:
        width //= 2
        upper = (freq_slot // span) % 2 == 1
        partner = [(slot, slot ^ span) for slot in range(freq_count)]
        keep = jnp.where(upper, image[width:], image[:width])
        away = jnp.where(upper, image[:width], image[width:])
        received = lax.ppermute(away, "freq", partner)
        image = (keep.astype(jnp.float32) + received.astype(jnp.float32)).astype(jnp.bfloat16)
        span //= 2
    panel = lax.all_to_all(image, "depth", split_axis=0, concat_axis=0, tiled=True)
    return angles(panel, angle_lag, depth_count)


def solution(mesh):
    placed = (
        P("depth", "freq", None, None, None),
        P("freq", None, None, None),
        P("freq", None, None, None),
        P(),
        P("freq"),
        P(),
    )
    return jax.shard_map(
        shards,
        mesh=mesh,
        in_specs=placed,
        out_specs=P(("freq", "depth"), None, None),
        check_vma=False,
    )
```

time: 167 us -> 127 us (0.76)
  starting transfers between devices: 80.2 us -> 43.3 us
  Pallas kernels: 0 us -> 36.8 us
  matrix products: 26.6 us -> 0 us
  blocking collectives: 0 us -> 24.6 us
  waiting for transfers between devices: 36.6 us -> 14.9 us
  local copies, waits for them, and re-layouts: 12.4 us -> 4.22 us
  other arithmetic: 7.86 us -> 0.93 us
    all_to_all x1 -> x0, starting transfers between devices: 50.1 us -> none  [shards(): lax.all_to_all(image.astype(jnp.bfloat16), 'depth', split_axis=0, concat_...]
    pallas_call x0 -> x37, Pallas kernels: none -> 36.8 us  [the longest x33 27.7 us: extend(): pl.pallas_call(kernel, out_shape=jax.ShapeDtypeStruct((rows, points), jnp...]
    dot_general x29 -> x0, matrix products: 26.6 us -> none  [the longest x26 23.4 us: extend(): product = jnp.dot(values, weights, preferred_element_type=jnp.float32)]
    all_to_all x0 -> x1, blocking collectives: none -> 24.6 us  [shards(): lax.all_to_all(image, 'depth', split_axis=0, concat_axis=0, tiled=True)]
    all_to_all x1 -> x0, waiting for transfers between devices: 13.2 us -> none  [shards(): lax.all_to_all(image.astype(jnp.bfloat16), 'depth', split_axis=0, concat_...]
    ppermute x24 -> x32, starting transfers between devices: 28.6 us -> 39 us  [the longest x31 38.9 us: shards(): sent[parity, round_index] = lax.ppermute(order, 'depth', pairs)]
    squeeze x3 -> x0, local copies, waits for them, and re-layouts: 5.41 us -> none  [the longest x1 4.66 us: shards(): weights = jnp.concatenate([extrap[0, 0, 0], extrap[0, 0, 1]], axis=1)]
    ppermute x24 -> x32, waiting for transfers between devices: 6.81 us -> 1.98 us  [the longest x1 1.9 us: shards(): received = lax.ppermute(away, 'freq', partner)]
  transfers between devices with their start and end apart: 26 -> 36, of which waited for: 6 -> 3; matrix products, arithmetic and copies ran while one was open for 15% -> 1% of each run, Pallas kernels for 0% -> 24%
where the time goes in v2:
time: 127 us
  starting transfers between devices  43.3 us (34%)
  Pallas kernels  36.8 us (29%)
  blocking collectives  24.6 us (19%)
  waiting for transfers between devices  14.9 us (12%)
  local copies, waits for them, and re-layouts  4.22 us (3%)
  between operations  1.9 us (1%)
    ppermute x31, starting transfers between devices, shards(): sent[parity, round_index] = lax.ppermute(order, 'depth', pairs)  38.9 us
    pallas_call x33, Pallas kernels, extend(): pl.pallas_call(kernel, out_shape=jax.ShapeDtypeStruct((rows, points), jnp...  27.7 us
    all_to_all x1, blocking collectives, shards(): lax.all_to_all(image, 'depth', split_axis=0, concat_axis=0, tiled=True)  24.6 us
    ppermute x4, waiting for transfers between devices, shards(): received = lax.ppermute(payload, 'freq', partner)  13 us
    ppermute x4, starting transfers between devices, shards(): received = lax.ppermute(payload, 'freq', partner)  4.33 us
    pallas_call x1, Pallas kernels, head(): pl.pallas_call(kernel, out_shape=jax.ShapeDtypeStruct((4 * part, points),...  4.2 us
    unnamed x16, local copies, waits for them, and re-layouts  3 us
  transfers between devices with their start and end apart: 36, of which 3 were waited for; matrix products, arithmetic and copies ran while one was open for 1% of the time, Pallas kernels for 24%

profile of v2, /device:TPU:0, one launch (start us, length us, event | category | flops | bytes accessed | tf_op | source)
XLA Modules:
  0.0 126.7 jit_solution(5883868349875851047)
XLA Ops:
  0.0 4.2 %shard_map.64.order_ref = bf16[64,1024]{1,0:T(8,128)(2,1)} custom-call(bf16[2,1024,1024]{2,1,0:T(8,128)(2,1)} %bitcast.54, bf16[128,2,1024]{2,1,0:T(2,128)(2,1)} %bitcast.91, bf16[128,2,1024]{2,1,0:T(2,128)(2,1)} %bitcast.93, s32[128]{0:T(128)} %shot_ref.1), custom_call_target="tpu_custom_call" | custom-call | tf_op jit(solution)/shard_map/pallas_call | solution.py:99
  4.2 4.9 %collective-permute-start = (bf16[64,1024]{1,0:T(8,128)(2,1)}, bf16[64,1024]{1,0:T(8,128)(2,1)S(1)}, u32[]{:S(2)}, u32[]{:S(2)}) collective-permute-start(bf16[64,1024]{1,0:T(8,128)(2,1)} %shard_map.64.order_ref), channel_id=1, source_target_pairs={{0,4},{1,5},{2,6},{3,7}} | collective-permute-start | bytes 393224 | tf_op jit(solution)/shard_map/ppermute | solution.py:272
  9.1 2.5 %shard_map.65 = bf16[8,64,1024]{2,1,0:T(8,128)(2,1)S(1)} custom-call(bf16[128,2,1024]{2,1,0:T(2,128)(2,1)S(1)} %bitcast.92, bf16[128,2,1024]{2,1,0:T(2,128)(2,1)S(1)} %bitcast.94, s32[128]{0:T(128)S(1)} %copy-done.7), custom_call_target="tpu_custom_call" | custom-call | tf_op jit(solution)/shard_map/pallas_call | solution.py:133
  13.4 1.3 %collective-permute-start.1 = (bf16[64,1024]{1,0:T(8,128)(2,1)S(1)}, bf16[64,1024]{1,0:T(8,128)(2,1)S(1)}, u32[]{:S(2)}, u32[]{:S(2)}) collective-permute-start(bf16[64,1024]{1,0:T(8,128)(2,1)S(1)} %shard_map.66.order_ref), channel_id=1, source_target_pairs={{0,4},{1,5},{2,6},{3,7}} | collective-permute-start | bytes 393224 | tf_op jit(solution)/shard_map/ppermute | solution.py:272
  15.8 2.2 %copy-done.1 = bf16[1,1,2,1024,1024]{4,3,2,1,0:T(8,128)(2,1)S(1)} copy-done((bf16[1,1,2,1024,1024]{4,3,2,1,0:T(8,128)(2,1)S(1)}, bf16[1,1,2,1024,1024]{4,3,2,1,0:T(8,128)(2,1)}, u32[]{:S(2)}) %copy-start.1) | copy-done | bytes 4194328
  19.5 0.8 shard_map.68.order_ref
  20.4 2.8 %collective-permute-start.3 = (bf16[64,1024]{1,0:T(8,128)(2,1)S(1)}, bf16[64,1024]{1,0:T(8,128)(2,1)S(1)}, u32[]{:S(2)}, u32[]{:S(2)}) collective-permute-start(bf16[64,1024]{1,0:T(8,128)(2,1)S(1)} %shard_map.68.order_ref), channel_id=1, source_target_pairs={{0,4},{1,5},{2,6},{3,7}} | collective-permute-start | bytes 393224 | tf_op jit(solution)/shard_map/ppermute | solution.py:272
  23.2 0.8 shard_map.69.order_ref
  24.8 0.8 shard_map.70.order_ref
  25.7 1.9 %collective-permute-start.5 = (bf16[64,1024]{1,0:T(8,128)(2,1)S(1)}, bf16[64,1024]{1,0:T(8,128)(2,1)S(1)}, u32[]{:S(2)}, u32[]{:S(2)}) collective-permute-start(bf16[64,1024]{1,0:T(8,128)(2,1)S(1)} %shard_map.70.order_ref), channel_id=1, source_target_pairs={{0,4},{8,12},{1,5},{9,13},{2,6},{10,14},{3,7},{11,15}} | collective-permute-start | bytes 393224 | tf_op jit(solution)/shard_map/ppermute | solution.py:272
  27.6 0.8 shard_map.71.order_ref
  29.1 0.8 shard_map.72.order_ref
  30.0 4.2 %collective-permute-start.7 = (bf16[64,1024]{1,0:T(8,128)(2,1)S(1)}, bf16[64,1024]{1,0:T(8,128)(2,1)S(1)}, u32[]{:S(2)}, u32[]{:S(2)}) collective-permute-start(bf16[64,1024]{1,0:T(8,128)(2,1)S(1)} %shard_map.72.order_ref), channel_id=1, source_target_pairs={{0,4},{8,12},{1,5},{9,13},{2,6},{10,14},{3,7},{11,15}} | collective-permute-start | bytes 393224 | tf_op jit(solution)/shard_map/ppermute | solution.py:272
  34.3 0.8 shard_map.73.order_ref
  35.8 0.8 shard_map.74.order_ref
  36.7 1.9 %collective-permute-start.9 = (bf16[64,1024]{1,0:T(8,128)(2,1)S(1)}, bf16[64,1024]{1,0:T(8,128)(2,1)S(1)}, u32[]{:S(2)}, u32[]{:S(2)}) collective-permute-start(bf16[64,1024]{1,0:T(8,128)(2,1)S(1)} %shard_map.74.order_ref), channel_id=1, source_target_pairs={{0,4},{8,12},{1,5},{9,13},{2,6},{10,14},{3,7},{11,15}} | collective-permute-start | bytes 393224 | tf_op jit(solution)/shard_map/ppermute | solution.py:272
  38.6 0.8 shard_map.75.order_ref
  40.2 0.8 shard_map.76.order_ref
  41.1 4.2 %collective-permute-start.11 = (bf16[64,1024]{1,0:T(8,128)(2,1)S(1)}, bf16[64,1024]{1,0:T(8,128)(2,1)S(1)}, u32[]{:S(2)}, u32[]{:S(2)}) collective-permute-start(bf16[64,1024]{1,0:T(8,128)(2,1)S(1)} %shard_map.76.order_ref), channel_id=1, source_target_pairs={{0,4},{8,12},{16,20},{1,5},{9,13},{17,21},{2,6},{10,14},{18,22},{3... | collective-permute-start | bytes 393224 | tf_op jit(solution)/shard_map/ppermute | solution.py:272
  45.3 0.8 shard_map.77.order_ref
  46.8 0.8 shard_map.78.order_ref
  47.7 1.9 %collective-permute-start.13 = (bf16[64,1024]{1,0:T(8,128)(2,1)S(1)}, bf16[64,1024]{1,0:T(8,128)(2,1)S(1)}, u32[]{:S(2)}, u32[]{:S(2)}) collective-permute-start(bf16[64,1024]{1,0:T(8,128)(2,1)S(1)} %shard_map.78.order_ref), channel_id=1, source_target_pairs={{0,4},{8,12},{16,20},{1,5},{9,13},{17,21},{2,6},{10,14},{18,22},{3... | collective-permute-start | bytes 393224 | tf_op jit(solution)/shard_map/ppermute | solution.py:272
  49.7 0.8 shard_map.79.order_ref
  51.2 0.8 shard_map.80.order_ref
  52.7 0.8 shard_map.81.order_ref
  54.4 0.8 shard_map.82.order_ref
  55.9 0.8 shard_map.83.order_ref
  57.4 0.8 shard_map.84.order_ref
  59.0 0.8 shard_map.85.order_ref
  60.5 0.8 shard_map.86.order_ref
  62.1 0.8 shard_map.87.order_ref
  63.7 0.8 shard_map.88.order_ref
  65.2 0.8 shard_map.89.order_ref
  66.8 0.8 shard_map.90.order_ref
  68.4 0.8 shard_map.91.order_ref
  70.1 0.9 concatenate.3
  71.0 0.8 shard_map.92.order_ref
  72.5 0.8 shard_map.93.order_ref
  74.1 1.6 %collective-permute-start.31 = (bf16[272,1024]{1,0:T(8,128)(2,1)}, bf16[272,1024]{1,0:T(8,128)(2,1)S(1)}, u32[]{:S(2)}, u32[]{:S(2)}) collective-permute-start(bf16[272,1024]{1,0:T(8,128)(2,1)} %concatenate.3), channel_id=1, source_target_pairs={{0,2},{1,3},{2,0},{3,1},{4,6},{5,7},{6,4},{7,5},{8,10},{9,11},{10,... | collective-permute-start | bytes 1671176 | tf_op jit(solution)/shard_map/ppermute | solution.py:288
  77.2 0.8 shard_map.95.order_ref
  78.1 0.8 shard_map.96.order_ref
  78.9 0.9 collective-permute-start.30
  81.4 1.6 %collective-permute-start.33 = (bf16[64,1024]{1,0:T(8,128)(2,1)S(1)}, bf16[64,1024]{1,0:T(8,128)(2,1)S(1)}, u32[]{:S(2)}, u32[]{:S(2)}) collective-permute-start(bf16[64,1024]{1,0:T(8,128)(2,1)S(1)} %slice_bitcast_fusion.1.refs_2_), channel_id=1, source_target_pairs={{0,2},{1,3},{2,0},{3,1},{4,6},{5,7},{6,4},{7,5},{8,10},{9,11},{10,... | collective-permute-start | bytes 393224 | tf_op jit(solution)/shard_map/ppermute | solution.py:288
  84.4 11.5 %collective-permute-done.33.refs_6_ = bf16[64,1024]{1,0:T(8,128)(2,1)S(1)} collective-permute-done((bf16[64,1024]{1,0:T(8,128)(2,1)S(1)}, bf16[64,1024]{1,0:T(8,128)(2,1)S(1)}, u32[]{:S(2)}, u32[]{:S(2)}) %collective-permute-start.33) | collective-permute-done | bytes 131104 | tf_op jit(solution)/shard_map/ppermute | solution.py:288
  96.0 1.4 %collective-permute-done.34.refs_7_ = bf16[64,1024]{1,0:T(8,128)(2,1)S(1)} collective-permute-done((bf16[64,1024]{1,0:T(8,128)(2,1)S(1)}, bf16[64,1024]{1,0:T(8,128)(2,1)S(1)}, u32[]{:S(2)}, u32[]{:S(2)}) %collective-permute-start.34) | collective-permute-done | bytes 131104 | tf_op jit(solution)/shard_map/ppermute | solution.py:288
  98.3 1.9 %collective-permute-done.35 = bf16[256,1024]{1,0:T(8,128)(2,1)S(1)} collective-permute-done((bf16[256,1024]{1,0:T(8,128)(2,1)S(1)}, bf16[256,1024]{1,0:T(8,128)(2,1)S(1)}, u32[]{:S(2)}, u32[]{:S(2)}) %collective-permute-start.35) | collective-permute-done | bytes 524320 | tf_op jit(solution)/shard_map/ppermute | solution.py:309
  100.5 24.6 %all_to_all.11 = bf16[8,32,1024]{2,1,0:T(8,128)(2,1)S(1)} all-to-all(bf16[8,32,1024]{2,1,0:T(8,128)(2,1)S(1)} %bitcast.97), channel_id=1, replica_groups=mesh['depth'=8,'freq'=4] {'depth'}, dimensions={0} | all-to-all | bytes 1048576 | tf_op jit(solution)/shard_map/all_to_all | solution.py:312
  125.0 1.6 %shard_map.100 = f32[32,8,256]{2,1,0:T(8,128)} custom-call(bf16[256,1024]{1,0:T(8,128)(2,1)S(1)} %bitcast.90, s32[1024,256]{1,0:T(8,128)S(1)} %copy-done.6), custom_call_target="tpu_custom_call" | custom-call | tf_op jit(solution)/shard_map/pallas_call | solution.py:215
  (106 shorter events, 23.3 us)
Async XLA Ops:
  0.0 9.1 %copy-start.3 = (bf16[1,128,2,1024]{3,2,1,0:T(2,128)(2,1)S(1)}, bf16[1,128,2,1024]{3,2,1,0:T(2,128)(2,1)}, u32[]{:S(2)}) copy-start(bf16[1,128,2,1024]{3,2,1,0:T(2,128)(2,1)} %param.7) | copy-start | bytes 1572868
  0.0 9.1 %copy-start.4 = (bf16[1,128,2,1024]{3,2,1,0:T(2,128)(2,1)S(1)}, bf16[1,128,2,1024]{3,2,1,0:T(2,128)(2,1)}, u32[]{:S(2)}) copy-start(bf16[1,128,2,1024]{3,2,1,0:T(2,128)(2,1)} %param.8) | copy-start | bytes 1572868
  0.0 9.1 %copy-start.7 = (s32[128]{0:T(128)S(1)}, s32[128]{0:T(128)}, u32[]{:S(2)}) copy-start(s32[128]{0:T(128)} %shot_ref.1) | copy-start | bytes 1540
  0.0 11.8 %copy-start = (bf16[1,1,2,1024,1024]{4,3,2,1,0:T(8,128)(2,1)S(1)}, bf16[1,1,2,1024,1024]{4,3,2,1,0:T(8,128)(2,1)}, u32[]{:S(2)}) copy-start(bf16[1,1,2,1024,1024]{4,3,2,1,0:T(8,128)(2,1)} %param.6) | copy-start | bytes 12582916
  4.2 11.6 %collective-permute-start = (bf16[64,1024]{1,0:T(8,128)(2,1)}, bf16[64,1024]{1,0:T(8,128)(2,1)S(1)}, u32[]{:S(2)}, u32[]{:S(2)}) collective-permute-start(bf16[64,1024]{1,0:T(8,128)(2,1)} %shard_map.64.order_ref), channel_id=1, source_target_pairs={{0,4},{1,5},{2,6},{3,7}} | collective-permute-start | bytes 393224 | tf_op jit(solution)/shard_map/ppermute | solution.py:272
  11.7 0.9 copy-start.5
  13.4 9.8 %collective-permute-start.1 = (bf16[64,1024]{1,0:T(8,128)(2,1)S(1)}, bf16[64,1024]{1,0:T(8,128)(2,1)S(1)}, u32[]{:S(2)}, u32[]{:S(2)}) collective-permute-start(bf16[64,1024]{1,0:T(8,128)(2,1)S(1)} %shard_map.66.order_ref), channel_id=1, source_target_pairs={{0,4},{1,5},{2,6},{3,7}} | collective-permute-start | bytes 393224 | tf_op jit(solution)/shard_map/ppermute | solution.py:272
  15.8 2.2 %copy-start.1 = (bf16[1,1,2,1024,1024]{4,3,2,1,0:T(8,128)(2,1)S(1)}, bf16[1,1,2,1024,1024]{4,3,2,1,0:T(8,128)(2,1)}, u32[]{:S(2)}) copy-start(bf16[1,1,2,1024,1024]{4,3,2,1,0:T(8,128)(2,1)} %param.6) | copy-start | bytes 12582916
  18.8 6.0 %collective-permute-start.2 = (bf16[64,1024]{1,0:T(8,128)(2,1)S(1)}, bf16[64,1024]{1,0:T(8,128)(2,1)S(1)}, u32[]{:S(2)}, u32[]{:S(2)}) collective-permute-start(bf16[64,1024]{1,0:T(8,128)(2,1)S(1)} %shard_map.67.order_ref), channel_id=1, source_target_pairs={{4,8},{5,9},{6,10},{7,11}} | collective-permute-start | bytes 393224 | tf_op jit(solution)/shard_map/ppermute | solution.py:272
  20.4 7.2 %collective-permute-start.3 = (bf16[64,1024]{1,0:T(8,128)(2,1)S(1)}, bf16[64,1024]{1,0:T(8,128)(2,1)S(1)}, u32[]{:S(2)}, u32[]{:S(2)}) collective-permute-start(bf16[64,1024]{1,0:T(8,128)(2,1)S(1)} %shard_map.68.order_ref), channel_id=1, source_target_pairs={{0,4},{1,5},{2,6},{3,7}} | collective-permute-start | bytes 393224 | tf_op jit(solution)/shard_map/ppermute | solution.py:272
  24.0 5.1 %collective-permute-start.4 = (bf16[64,1024]{1,0:T(8,128)(2,1)S(1)}, bf16[64,1024]{1,0:T(8,128)(2,1)S(1)}, u32[]{:S(2)}, u32[]{:S(2)}) collective-permute-start(bf16[64,1024]{1,0:T(8,128)(2,1)S(1)} %shard_map.69.order_ref), channel_id=1, source_target_pairs={{4,8},{5,9},{6,10},{7,11}} | collective-permute-start | bytes 393224 | tf_op jit(solution)/shard_map/ppermute | solution.py:272
  25.7 8.6 %collective-permute-start.5 = (bf16[64,1024]{1,0:T(8,128)(2,1)S(1)}, bf16[64,1024]{1,0:T(8,128)(2,1)S(1)}, u32[]{:S(2)}, u32[]{:S(2)}) collective-permute-start(bf16[64,1024]{1,0:T(8,128)(2,1)S(1)} %shard_map.70.order_ref), channel_id=1, source_target_pairs={{0,4},{8,12},{1,5},{9,13},{2,6},{10,14},{3,7},{11,15}} | collective-permute-start | bytes 393224 | tf_op jit(solution)/shard_map/ppermute | solution.py:272
  28.5 7.4 %collective-permute-start.6 = (bf16[64,1024]{1,0:T(8,128)(2,1)S(1)}, bf16[64,1024]{1,0:T(8,128)(2,1)S(1)}, u32[]{:S(2)}, u32[]{:S(2)}) collective-permute-start(bf16[64,1024]{1,0:T(8,128)(2,1)S(1)} %shard_map.71.order_ref), channel_id=1, source_target_pairs={{4,8},{5,9},{6,10},{7,11}} | collective-permute-start | bytes 393224 | tf_op jit(solution)/shard_map/ppermute | solution.py:272
  30.0 8.6 %collective-permute-start.7 = (bf16[64,1024]{1,0:T(8,128)(2,1)S(1)}, bf16[64,1024]{1,0:T(8,128)(2,1)S(1)}, u32[]{:S(2)}, u32[]{:S(2)}) collective-permute-start(bf16[64,1024]{1,0:T(8,128)(2,1)S(1)} %shard_map.72.order_ref), channel_id=1, source_target_pairs={{0,4},{8,12},{1,5},{9,13},{2,6},{10,14},{3,7},{11,15}} | collective-permute-start | bytes 393224 | tf_op jit(solution)/shard_map/ppermute | solution.py:272
  35.1 5.1 %collective-permute-start.8 = (bf16[64,1024]{1,0:T(8,128)(2,1)S(1)}, bf16[64,1024]{1,0:T(8,128)(2,1)S(1)}, u32[]{:S(2)}, u32[]{:S(2)}) collective-permute-start(bf16[64,1024]{1,0:T(8,128)(2,1)S(1)} %shard_map.73.order_ref), channel_id=1, source_target_pairs={{4,8},{12,16},{5,9},{13,17},{6,10},{14,18},{7,11},{15,19}} | collective-permute-start | bytes 393224 | tf_op jit(solution)/shard_map/ppermute | solution.py:272
  36.7 8.6 %collective-permute-start.9 = (bf16[64,1024]{1,0:T(8,128)(2,1)S(1)}, bf16[64,1024]{1,0:T(8,128)(2,1)S(1)}, u32[]{:S(2)}, u32[]{:S(2)}) collective-permute-start(bf16[64,1024]{1,0:T(8,128)(2,1)S(1)} %shard_map.74.order_ref), channel_id=1, source_target_pairs={{0,4},{8,12},{1,5},{9,13},{2,6},{10,14},{3,7},{11,15}} | collective-permute-start | bytes 393224 | tf_op jit(solution)/shard_map/ppermute | solution.py:272
  39.5 7.4 %collective-permute-start.10 = (bf16[64,1024]{1,0:T(8,128)(2,1)S(1)}, bf16[64,1024]{1,0:T(8,128)(2,1)S(1)}, u32[]{:S(2)}, u32[]{:S(2)}) collective-permute-start(bf16[64,1024]{1,0:T(8,128)(2,1)S(1)} %shard_map.75.order_ref), channel_id=1, source_target_pairs={{4,8},{12,16},{5,9},{13,17},{6,10},{14,18},{7,11},{15,19}} | collective-permute-start | bytes 393224 | tf_op jit(solution)/shard_map/ppermute | solution.py:272
  41.1 8.6 %collective-permute-start.11 = (bf16[64,1024]{1,0:T(8,128)(2,1)S(1)}, bf16[64,1024]{1,0:T(8,128)(2,1)S(1)}, u32[]{:S(2)}, u32[]{:S(2)}) collective-permute-start(bf16[64,1024]{1,0:T(8,128)(2,1)S(1)} %shard_map.76.order_ref), channel_id=1, source_target_pairs={{0,4},{8,12},{16,20},{1,5},{9,13},{17,21},{2,6},{10,14},{18,22},{3... | collective-permute-start | bytes 393224 | tf_op jit(solution)/shard_map/ppermute | solution.py:272
  46.1 5.0 %collective-permute-start.12 = (bf16[64,1024]{1,0:T(8,128)(2,1)S(1)}, bf16[64,1024]{1,0:T(8,128)(2,1)S(1)}, u32[]{:S(2)}, u32[]{:S(2)}) collective-permute-start(bf16[64,1024]{1,0:T(8,128)(2,1)S(1)} %shard_map.77.order_ref), channel_id=1, source_target_pairs={{4,8},{12,16},{5,9},{13,17},{6,10},{14,18},{7,11},{15,19}} | collective-permute-start | bytes 393224 | tf_op jit(solution)/shard_map/ppermute | solution.py:272
  47.7 5.0 %collective-permute-start.13 = (bf16[64,1024]{1,0:T(8,128)(2,1)S(1)}, bf16[64,1024]{1,0:T(8,128)(2,1)S(1)}, u32[]{:S(2)}, u32[]{:S(2)}) collective-permute-start(bf16[64,1024]{1,0:T(8,128)(2,1)S(1)} %shard_map.78.order_ref), channel_id=1, source_target_pairs={{0,4},{8,12},{16,20},{1,5},{9,13},{17,21},{2,6},{10,14},{18,22},{3... | collective-permute-start | bytes 393224 | tf_op jit(solution)/shard_map/ppermute | solution.py:272
  50.5 3.8 %collective-permute-start.14 = (bf16[64,1024]{1,0:T(8,128)(2,1)S(1)}, bf16[64,1024]{1,0:T(8,128)(2,1)S(1)}, u32[]{:S(2)}, u32[]{:S(2)}) collective-permute-start(bf16[64,1024]{1,0:T(8,128)(2,1)S(1)} %shard_map.79.order_ref), channel_id=1, source_target_pairs={{4,8},{12,16},{20,24},{5,9},{13,17},{21,25},{6,10},{14,18},{22,26}... | collective-permute-start | bytes 393224 | tf_op jit(solution)/shard_map/ppermute | solution.py:272
  52.0 3.8 %collective-permute-start.15 = (bf16[64,1024]{1,0:T(8,128)(2,1)S(1)}, bf16[64,1024]{1,0:T(8,128)(2,1)S(1)}, u32[]{:S(2)}, u32[]{:S(2)}) collective-permute-start(bf16[64,1024]{1,0:T(8,128)(2,1)S(1)} %shard_map.80.order_ref), channel_id=1, source_target_pairs={{8,12},{16,20},{9,13},{17,21},{10,14},{18,22},{11,15},{19,23}} | collective-permute-start | bytes 393224 | tf_op jit(solution)/shard_map/ppermute | solution.py:272
  53.6 3.8 %collective-permute-start.16 = (bf16[64,1024]{1,0:T(8,128)(2,1)S(1)}, bf16[64,1024]{1,0:T(8,128)(2,1)S(1)}, u32[]{:S(2)}, u32[]{:S(2)}) collective-permute-start(bf16[64,1024]{1,0:T(8,128)(2,1)S(1)} %shard_map.81.order_ref), channel_id=1, source_target_pairs={{4,8},{12,16},{20,24},{5,9},{13,17},{21,25},{6,10},{14,18},{22,26}... | collective-permute-start | bytes 393224 | tf_op jit(solution)/shard_map/ppermute | solution.py:272
  55.2 3.8 %collective-permute-start.17 = (bf16[64,1024]{1,0:T(8,128)(2,1)S(1)}, bf16[64,1024]{1,0:T(8,128)(2,1)S(1)}, u32[]{:S(2)}, u32[]{:S(2)}) collective-permute-start(bf16[64,1024]{1,0:T(8,128)(2,1)S(1)} %shard_map.82.order_ref), channel_id=1, source_target_pairs={{8,12},{16,20},{24,28},{9,13},{17,21},{25,29},{10,14},{18,22},{26,... | collective-permute-start | bytes 393224 | tf_op jit(solution)/shard_map/ppermute | solution.py:272
  56.7 3.8 %collective-permute-start.18 = (bf16[64,1024]{1,0:T(8,128)(2,1)S(1)}, bf16[64,1024]{1,0:T(8,128)(2,1)S(1)}, u32[]{:S(2)}, u32[]{:S(2)}) collective-permute-start(bf16[64,1024]{1,0:T(8,128)(2,1)S(1)} %shard_map.83.order_ref), channel_id=1, source_target_pairs={{12,16},{20,24},{13,17},{21,25},{14,18},{22,26},{15,19},{23,27}} | collective-permute-start | bytes 393224 | tf_op jit(solution)/shard_map/ppermute | solution.py:272
  58.3 3.8 %collective-permute-start.19 = (bf16[64,1024]{1,0:T(8,128)(2,1)S(1)}, bf16[64,1024]{1,0:T(8,128)(2,1)S(1)}, u32[]{:S(2)}, u32[]{:S(2)}) collective-permute-start(bf16[64,1024]{1,0:T(8,128)(2,1)S(1)} %shard_map.84.order_ref), channel_id=1, source_target_pairs={{8,12},{16,20},{24,28},{9,13},{17,21},{25,29},{10,14},{18,22},{26,... | collective-permute-start | bytes 393224 | tf_op jit(solution)/shard_map/ppermute | solution.py:272
  59.8 3.8 %collective-permute-start.20 = (bf16[64,1024]{1,0:T(8,128)(2,1)S(1)}, bf16[64,1024]{1,0:T(8,128)(2,1)S(1)}, u32[]{:S(2)}, u32[]{:S(2)}) collective-permute-start(bf16[64,1024]{1,0:T(8,128)(2,1)S(1)} %shard_map.85.order_ref), channel_id=1, source_target_pairs={{12,16},{20,24},{13,17},{21,25},{14,18},{22,26},{15,19},{23,27}} | collective-permute-start | bytes 393224 | tf_op jit(solution)/shard_map/ppermute | solution.py:272
  61.4 3.8 %collective-permute-start.21 = (bf16[64,1024]{1,0:T(8,128)(2,1)S(1)}, bf16[64,1024]{1,0:T(8,128)(2,1)S(1)}, u32[]{:S(2)}, u32[]{:S(2)}) collective-permute-start(bf16[64,1024]{1,0:T(8,128)(2,1)S(1)} %shard_map.86.order_ref), channel_id=1, source_target_pairs={{16,20},{24,28},{17,21},{25,29},{18,22},{26,30},{19,23},{27,31}} | collective-permute-start | bytes 393224 | tf_op jit(solution)/shard_map/ppermute | solution.py:272
  62.9 3.8 %collective-permute-start.22 = (bf16[64,1024]{1,0:T(8,128)(2,1)S(1)}, bf16[64,1024]{1,0:T(8,128)(2,1)S(1)}, u32[]{:S(2)}, u32[]{:S(2)}) collective-permute-start(bf16[64,1024]{1,0:T(8,128)(2,1)S(1)} %shard_map.87.order_ref), channel_id=1, source_target_pairs={{12,16},{20,24},{13,17},{21,25},{14,18},{22,26},{15,19},{23,27}} | collective-permute-start | bytes 393224 | tf_op jit(solution)/shard_map/ppermute | solution.py:272
  64.5 3.8 %collective-permute-start.23 = (bf16[64,1024]{1,0:T(8,128)(2,1)S(1)}, bf16[64,1024]{1,0:T(8,128)(2,1)S(1)}, u32[]{:S(2)}, u32[]{:S(2)}) collective-permute-start(bf16[64,1024]{1,0:T(8,128)(2,1)S(1)} %shard_map.88.order_ref), channel_id=1, source_target_pairs={{16,20},{24,28},{17,21},{25,29},{18,22},{26,30},{19,23},{27,31}} | collective-permute-start | bytes 393224 | tf_op jit(solution)/shard_map/ppermute | solution.py:272
  66.1 4.9 %collective-permute-start.24 = (bf16[64,1024]{1,0:T(8,128)(2,1)S(1)}, bf16[64,1024]{1,0:T(8,128)(2,1)S(1)}, u32[]{:S(2)}, u32[]{:S(2)}) collective-permute-start(bf16[64,1024]{1,0:T(8,128)(2,1)S(1)} %shard_map.89.order_ref), channel_id=1, source_target_pairs={{20,24},{21,25},{22,26},{23,27}} | collective-permute-start | bytes 393224 | tf_op jit(solution)/shard_map/ppermute | solution.py:272
  67.6 4.9 %collective-permute-start.25 = (bf16[64,1024]{1,0:T(8,128)(2,1)S(1)}, bf16[64,1024]{1,0:T(8,128)(2,1)S(1)}, u32[]{:S(2)}, u32[]{:S(2)}) collective-permute-start(bf16[64,1024]{1,0:T(8,128)(2,1)S(1)} %shard_map.90.order_ref), channel_id=1, source_target_pairs={{16,20},{24,28},{17,21},{25,29},{18,22},{26,30},{19,23},{27,31}} | collective-permute-start | bytes 393224 | tf_op jit(solution)/shard_map/ppermute | solution.py:272
  68.3 2.6 %copy-start.2 = (bf16[1,1,2,1024,1024]{4,3,2,1,0:T(8,128)(2,1)S(1)}, bf16[1,1,2,1024,1024]{4,3,2,1,0:T(8,128)(2,1)}, u32[]{:S(2)}) copy-start(bf16[1,1,2,1024,1024]{4,3,2,1,0:T(8,128)(2,1)} %param.6) | copy-start | bytes 12582916
  69.2 6.4 %collective-permute-start.26 = (bf16[64,1024]{1,0:T(8,128)(2,1)S(1)}, bf16[64,1024]{1,0:T(8,128)(2,1)S(1)}, u32[]{:S(2)}, u32[]{:S(2)}) collective-permute-start(bf16[64,1024]{1,0:T(8,128)(2,1)S(1)} %shard_map.91.order_ref), channel_id=1, source_target_pairs={{20,24},{21,25},{22,26},{23,27}} | collective-permute-start | bytes 393224 | tf_op jit(solution)/shard_map/ppermute | solution.py:272
  71.8 5.3 %collective-permute-start.27 = (bf16[64,1024]{1,0:T(8,128)(2,1)S(1)}, bf16[64,1024]{1,0:T(8,128)(2,1)S(1)}, u32[]{:S(2)}, u32[]{:S(2)}) collective-permute-start(bf16[64,1024]{1,0:T(8,128)(2,1)S(1)} %shard_map.92.order_ref), channel_id=1, source_target_pairs={{24,28},{25,29},{26,30},{27,31}} | collective-permute-start | bytes 393224 | tf_op jit(solution)/shard_map/ppermute | solution.py:272
  73.3 4.7 %collective-permute-start.28 = (bf16[64,1024]{1,0:T(8,128)(2,1)S(1)}, bf16[64,1024]{1,0:T(8,128)(2,1)S(1)}, u32[]{:S(2)}, u32[]{:S(2)}) collective-permute-start(bf16[64,1024]{1,0:T(8,128)(2,1)S(1)} %shard_map.93.order_ref), channel_id=1, source_target_pairs={{20,24},{21,25},{22,26},{23,27}} | collective-permute-start | bytes 393224 | tf_op jit(solution)/shard_map/ppermute | solution.py:272
  74.1 23.3 %collective-permute-start.31 = (bf16[272,1024]{1,0:T(8,128)(2,1)}, bf16[272,1024]{1,0:T(8,128)(2,1)S(1)}, u32[]{:S(2)}, u32[]{:S(2)}) collective-permute-start(bf16[272,1024]{1,0:T(8,128)(2,1)} %concatenate.3), channel_id=1, source_target_pairs={{0,2},{1,3},{2,0},{3,1},{4,6},{5,7},{6,4},{7,5},{8,10},{9,11},{10,... | collective-permute-start | bytes 1671176 | tf_op jit(solution)/shard_map/ppermute | solution.py:288
  76.5 4.0 %collective-permute-start.29 = (bf16[64,1024]{1,0:T(8,128)(2,1)S(1)}, bf16[64,1024]{1,0:T(8,128)(2,1)S(1)}, u32[]{:S(2)}, u32[]{:S(2)}) collective-permute-start(bf16[64,1024]{1,0:T(8,128)(2,1)S(1)} %shard_map.94.order_ref), channel_id=1, source_target_pairs={{24,28},{25,29},{26,30},{27,31}} | collective-permute-start | bytes 393224 | tf_op jit(solution)/shard_map/ppermute | solution.py:272
  78.9 4.0 %collective-permute-start.30 = (bf16[64,1024]{1,0:T(8,128)(2,1)S(1)}, bf16[64,1024]{1,0:T(8,128)(2,1)S(1)}, u32[]{:S(2)}, u32[]{:S(2)}) collective-permute-start(bf16[64,1024]{1,0:T(8,128)(2,1)S(1)} %shard_map.96.order_ref), channel_id=1, source_target_pairs={{24,28},{25,29},{26,30},{27,31}} | collective-permute-start | bytes 393224 | tf_op jit(solution)/shard_map/ppermute | solution.py:272
  79.8 17.5 %collective-permute-start.32 = (bf16[128,1024]{1,0:T(8,128)(2,1)S(1)}, bf16[128,1024]{1,0:T(8,128)(2,1)S(1)}, u32[]{:S(2)}, u32[]{:S(2)}) collective-permute-start(bf16[128,1024]{1,0:T(8,128)(2,1)S(1)} %bitcast.95), channel_id=1, source_target_pairs={{0,2},{1,3},{2,0},{3,1},{4,6},{5,7},{6,4},{7,5},{8,10},{9,11},{10,... | collective-permute-start | bytes 786440 | tf_op jit(solution)/shard_map/ppermute | solution.py:288
  81.4 14.6 %collective-permute-start.33 = (bf16[64,1024]{1,0:T(8,128)(2,1)S(1)}, bf16[64,1024]{1,0:T(8,128)(2,1)S(1)}, u32[]{:S(2)}, u32[]{:S(2)}) collective-permute-start(bf16[64,1024]{1,0:T(8,128)(2,1)S(1)} %slice_bitcast_fusion.1.refs_2_), channel_id=1, source_target_pairs={{0,2},{1,3},{2,0},{3,1},{4,6},{5,7},{6,4},{7,5},{8,10},{9,11},{10,... | collective-permute-start | bytes 393224 | tf_op jit(solution)/shard_map/ppermute | solution.py:288
  83.8 13.6 %collective-permute-start.34 = (bf16[64,1024]{1,0:T(8,128)(2,1)S(1)}, bf16[64,1024]{1,0:T(8,128)(2,1)S(1)}, u32[]{:S(2)}, u32[]{:S(2)}) collective-permute-start(bf16[64,1024]{1,0:T(8,128)(2,1)S(1)} %slice_bitcast_fusion.refs_3_), channel_id=1, source_target_pairs={{0,2},{1,3},{2,0},{3,1},{4,6},{5,7},{6,4},{7,5},{8,10},{9,11},{10,... | collective-permute-start | bytes 393224 | tf_op jit(solution)/shard_map/ppermute | solution.py:288
  98.2 26.8 %copy-start.6 = (s32[1024,256]{1,0:T(8,128)S(1)}, s32[1024,256]{1,0:T(8,128)}, u32[]{:S(2)}) copy-start(s32[1024,256]{1,0:T(8,128)} %lag_ref.1) | copy-start | bytes 3145732
  98.2 2.0 %collective-permute-start.35 = (bf16[256,1024]{1,0:T(8,128)(2,1)S(1)}, bf16[256,1024]{1,0:T(8,128)(2,1)S(1)}, u32[]{:S(2)}, u32[]{:S(2)}) collective-permute-start(bf16[256,1024]{1,0:T(8,128)(2,1)S(1)} %broadcast_select_fusion), channel_id=1, source_target_pairs={{0,1},{1,0},{2,3},{3,2},{4,5},{5,4},{6,7},{7,6},{8,9},{9,8},{10,11... | collective-permute-start | bytes 1572872 | tf_op jit(solution)/shard_map/ppermute | solution.py:309

commit v3 on v2

v3 whole, which is shorter than its diff:
```python
import math

import jax
import jax.numpy as jnp
from jax import lax
from jax.experimental import pallas as pl
from jax.experimental.pallas import tpu as pltpu
from jax.sharding import PartitionSpec as P

CHUNKS = 8
GROUPS = (1,) * CHUNKS
LAGS = (3, 2)
TILES = 2

WHOLE = pl.BlockSpec(memory_space=pltpu.VMEM)
FAR = pl.BlockSpec(memory_space=pltpu.HBM)
BRIEF = pl.CostEstimate(flops=0, bytes_accessed=0, transcendentals=0)


def first_round(level):
    return sum(LAGS) * (level // 2) + LAGS[1] * (level % 2)


def handled(round_index, level, chunk_count):
    return 0 <= round_index - first_round(level) < chunk_count


def senders(round_index, parity, depth_count, chunk_count):
    everyone = list(range(parity, depth_count - 1, 2))
    levels = [level for level in everyone if handled(round_index, level, chunk_count)]
    if not levels or levels[0] == parity:
        return levels
    wanted = min(len(everyone), -(-chunk_count // sum(LAGS)))
    first, last = everyone.index(levels[0]), everyone.index(levels[-1])
    return everyone[first : max(first + wanted, last + 1)]


def march(values, extrap_ref, out_ref):
    half = out_ref.shape[0] // 2
    points = out_ref.shape[1]
    width = points // TILES

    @pl.loop(0, TILES)
    def _(tile):
        column = pl.ds(pl.multiple_of(tile * width, width), width)
        real = jnp.dot(values, extrap_ref[0, :, column], preferred_element_type=jnp.float32)
        imag = jnp.dot(values, extrap_ref[1, :, column], preferred_element_type=jnp.float32)
        out_ref[:half, column] = (real[:half] - imag[half:]).astype(out_ref.dtype)
        out_ref[half:, column] = (imag[:half] + real[half:]).astype(out_ref.dtype)


def extend(arrived, extrap, finished, round_index, parity, above, sends):
    rows, points = arrived.shape
    chunk_count = finished.shape[0]

    def kernel(arrived_ref, extrap_ref, finished_in, *refs):
        finished_ref = refs[-1]
        level = lax.axis_index("depth")
        chunk = round_index - first_round(level)
        mine = (level % 2 == parity) & (chunk >= 0) & (chunk < chunk_count)
        place_ref = finished_ref.at[jnp.clip(chunk, 0, chunk_count - 1)]
        out_ref = refs[-2] if sends else place_ref
        if above:

            @pl.when(level == 0)
            def _():
                march(refs[0][0], extrap_ref, out_ref)

        @pl.when(mine & ((level > 0) | (not above)))
        def _():
            march(arrived_ref[...], extrap_ref, out_ref)

        if sends:

            @pl.when(mine)
            def _():
                place_ref[...] = out_ref[...]

    kept = jax.ShapeDtypeStruct(finished.shape, finished.dtype)
    sent = jax.ShapeDtypeStruct((rows, points), jnp.bfloat16)
    return pl.pallas_call(
        kernel,
        out_shape=[sent, kept] if sends else [kept],
        in_specs=[WHOLE, WHOLE, WHOLE] + [WHOLE] * len(above),
        out_specs=[WHOLE, WHOLE] if sends else [WHOLE],
        input_output_aliases={2: 1 if sends else 0},
        compiler_params=pltpu.CompilerParams(vmem_limit_bytes=8 << 20),
        cost_estimate=BRIEF,
    )(arrived, extrap, finished, *above)


def pack(finished, number, start, stop, noted):
    rows, points = finished.shape[1:]
    part = rows // 4
    half = points // 2
    count = 2 * part * (stop - start)

    def kernel(finished_ref, number_ref, out_ref):
        span = lax.axis_size("freq") // 2
        upper = (lax.axis_index("freq") // span) % 2
        column = pl.ds(pl.multiple_of((1 - upper) * half, half), half)
        for chunk in range(start, stop):
            for index, (first, second) in enumerate(((0, 3), (2, 1))):
                row = pl.ds((2 * (chunk - start) + index) * part, part)
                out_ref[row, :points] = finished_ref[chunk, pl.ds(second * part, part), :]
                out_ref[row, points:] = finished_ref[chunk, pl.ds(first * part, part), column]
        if noted:
            out_ref[count:] = jnp.broadcast_to(
                number_ref[...].astype(out_ref.dtype), (16, out_ref.shape[1])
            )

    return pl.pallas_call(
        kernel,
        out_shape=jax.ShapeDtypeStruct((count + 16 * noted, points + half), jnp.bfloat16),
        in_specs=[WHOLE] * 2,
        out_specs=WHOLE,
        compiler_params=pltpu.CompilerParams(vmem_limit_bytes=8 << 20),
        cost_estimate=BRIEF,
    )(finished, number)


def picked(shot_ref, source_ref, span, component):
    shot_count = source_ref.shape[0]
    count = span.stop - span.start
    pick = (
        shot_ref[span][None, :] == lax.broadcasted_iota(jnp.int32, (shot_count, count), 0)
    ).astype(jnp.bfloat16)
    return lax.dot_general(
        pick,
        source_ref[:, component, :],
        (((0,), (0,)), ((), ())),
        preferred_element_type=jnp.float32,
    ).astype(jnp.bfloat16)


def fill(out_ref, shot_ref, source_ref, record_ref, span):
    part = out_ref.shape[0] // 4
    out_ref[:part] = picked(shot_ref, source_ref, span, 0)
    out_ref[part : 2 * part] = record_ref[span, 1, :]
    out_ref[2 * part : 3 * part] = picked(shot_ref, source_ref, span, 1)
    out_ref[3 * part :] = record_ref[span, 0, :]


def head(extrap, sources, records, shots, part):
    points = extrap.shape[2]

    def kernel(
        extrap_hbm, source_hbm, record_hbm, shot_hbm, out_ref,
        extrap_ref, source_ref, record_ref, shot_ref, chunk_ref, sems,
    ):
        copies = [
            pltpu.make_async_copy(shot_hbm, shot_ref, sems.at[0]),
            pltpu.make_async_copy(source_hbm, source_ref, sems.at[1]),
            pltpu.make_async_copy(record_hbm.at[pl.ds(0, part)], record_ref, sems.at[2]),
            pltpu.make_async_copy(extrap_hbm, extrap_ref, sems.at[3]),
        ]
        for copy in copies:
            copy.start()
        for copy in copies[:3]:
            copy.wait()
        fill(chunk_ref, shot_ref, source_ref, record_ref, slice(0, part))
        copies[3].wait()
        march(chunk_ref[...], extrap_ref, out_ref)

    return pl.pallas_call(
        kernel,
        out_shape=jax.ShapeDtypeStruct((4 * part, points), jnp.bfloat16),
        in_specs=[FAR] * 4,
        out_specs=WHOLE,
        scratch_shapes=[
            pltpu.VMEM(extrap.shape, extrap.dtype),
            pltpu.VMEM(sources.shape, sources.dtype),
            pltpu.VMEM((part,) + records.shape[1:], records.dtype),
            pltpu.VMEM(shots.shape, shots.dtype),
            pltpu.VMEM((4 * part, points), jnp.bfloat16),
            pltpu.SemaphoreType.DMA((4,)),
        ],
        compiler_params=pltpu.CompilerParams(vmem_limit_bytes=56 << 20),
    )(extrap, sources, records, shots)


def surface(sources, records, shots, chunk_count, first):
    shot_count, _, points = sources.shape
    part = shot_count // chunk_count

    def kernel(source_ref, record_ref, shot_ref, first_ref, out_ref, finished_ref):
        finished_ref[0] = first_ref[...]
        everything = slice(0, shot_count)
        for place, values in (
            (0, picked(shot_ref, source_ref, everything, 0)),
            (1, record_ref[:, 1, :]),
            (2, picked(shot_ref, source_ref, everything, 1)),
            (3, record_ref[:, 0, :]),
        ):
            for chunk in range(chunk_count):
                out_ref[chunk, place * part : (place + 1) * part] = values[
                    chunk * part : (chunk + 1) * part
                ]

    return pl.pallas_call(
        kernel,
        out_shape=[jax.ShapeDtypeStruct((chunk_count, 4 * part, points), jnp.bfloat16)] * 2,
        in_specs=[WHOLE] * 4,
        out_specs=[WHOLE] * 2,
        compiler_params=pltpu.CompilerParams(vmem_limit_bytes=12 << 20),
    )(sources, records, shots, first)


def correlate(finished, theirs, own_scale, unit, part):
    points = finished.shape[2]
    chunk_count = finished.shape[0]
    width = points // 2
    depth = 2 * chunk_count * part

    def kernel(finished_ref, *refs):
        their_refs = refs[: len(theirs)]
        scale_ref, out_ref, source_ref, record_ref = refs[len(theirs) :]
        span = lax.axis_size("freq") // 2
        upper = (lax.axis_index("freq") // span) % 2
        column = pl.ds(pl.multiple_of(upper * width, width), width)

        def product():
            return lax.dot_general(
                source_ref[...],
                record_ref[...],
                (((0,), (0,)), ((), ())),
                preferred_element_type=jnp.float32,
            )

        for chunk in range(chunk_count):
            for index, (first, second) in enumerate(((0, 3), (2, 1))):
                row = pl.ds((2 * chunk + index) * part, part)
                source_ref[row] = finished_ref[chunk, pl.ds(first * part, part), column]
                record_ref[row] = finished_ref[chunk, pl.ds(second * part, part), :]
        total = product() * scale_ref[...]
        start = 0
        for group, ref in zip(GROUPS, their_refs):
            count = 2 * group * part
            source_ref[start : start + count] = ref[:count, points:]
            record_ref[start : start + count] = ref[:count, :points]
            start += count
        count = 2 * GROUPS[0] * part
        number = their_refs[0][count : count + 16, :128].astype(jnp.float32)[:1, :1]
        total += product() * (number * unit)
        out_ref[...] = total.astype(out_ref.dtype)

    return pl.pallas_call(
        kernel,
        out_shape=jax.ShapeDtypeStruct((width, points), jnp.bfloat16),
        in_specs=[WHOLE] * (2 + len(theirs)),
        out_specs=WHOLE,
        scratch_shapes=[
            pltpu.VMEM((depth, width), jnp.bfloat16),
            pltpu.VMEM((depth, points), jnp.bfloat16),
        ],
        compiler_params=pltpu.CompilerParams(vmem_limit_bytes=24 << 20),
    )(finished, *theirs, own_scale)


def angles(panel, angle_lag, depth_count):
    angle_count = angle_lag.shape[1]
    row_count = panel.shape[0] // depth_count
    points = panel.shape[1]

    def kernel(panel_ref, lag_ref, out_ref):
        total = None
        for lag in range(depth_count):
            column = (lag_ref[...] == lag).astype(jnp.bfloat16)
            skip = lag * row_count
            if row_count % 16 == 0:
                term = jnp.dot(panel_ref[skip:], column, preferred_element_type=jnp.float32)
            else:
                term = jnp.dot(panel_ref[...], column, preferred_element_type=jnp.float32)[skip:]
            if total is None:
                total = term
            elif skip:
                kept = total.shape[0] - skip
                total = jnp.concatenate([total[:kept] + term, total[kept:]], axis=0)
        total = total * (1.0 / math.sqrt(points))
        for depth in range(depth_count):
            out_ref[:, depth, :] = total[depth * row_count : (depth + 1) * row_count]

    return pl.pallas_call(
        kernel,
        out_shape=jax.ShapeDtypeStruct((row_count, depth_count, angle_count), jnp.float32),
        in_specs=[WHOLE] * 2,
        out_specs=WHOLE,
        compiler_params=pltpu.CompilerParams(vmem_limit_bytes=24 << 20),
    )(panel, angle_lag)


def shards(extrap, source_field, record_field, shot_of_record, freq_index, angle_lag):
    depth_count = lax.axis_size("depth")
    freq_count = lax.axis_size("freq")
    freq_slot = lax.axis_index("freq")
    points = source_field.shape[3]
    shot_count = source_field.shape[1]
    chunk_count = CHUNKS
    part = shot_count // chunk_count

    operator = extrap[0, 0]
    sources, records = source_field[0], record_field[0]
    order = [head(operator, sources, records, shot_of_record, part)]
    above, finished = surface(sources, records, shot_of_record, chunk_count, order[0])

    number = freq_index[0].astype(jnp.float32).reshape(1, 1) + 1.0
    span = freq_count // 2
    partner = [(slot, slot ^ span) for slot in range(freq_count)]

    sent = {}
    theirs = []
    round_count = first_round(depth_count - 1) + chunk_count
    for round_index in range(round_count):
        for parity in (0, 1):
            levels = [
                z for z in range(parity, depth_count, 2) if handled(round_index, z, chunk_count)
            ]
            if not levels:
                continue
            pairs = [(z, z + 1) for z in senders(round_index, parity, depth_count, chunk_count)]
            if round_index or parity:
                arrived = sent.get((1 - parity, round_index - LAGS[parity]))
                entering = ()
                if parity == 0 and round_index < chunk_count:
                    entering = (above[round_index : round_index + 1],)
                    if arrived is None:
                        arrived, entering = above[round_index], ()
                *order, finished = extend(
                    arrived, operator, finished, round_index, parity, entering, bool(pairs)
                )
            if pairs:
                sent[parity, round_index] = lax.ppermute(order[0], "depth", pairs)
        stop = sum(GROUPS[: len(theirs) + 1])
        if len(theirs) < len(GROUPS) and round_index - first_round(depth_count - 1) == stop - 1:
            start = stop - GROUPS[len(theirs)]
            payload = pack(finished, number, start, stop, start == 0)
            payload, finished = lax.optimization_barrier((payload, finished))
            theirs.append(lax.ppermute(payload, "freq", partner))

    scale = 1.0 / (8 * freq_count) / math.sqrt(shot_count * freq_count)
    image = correlate(finished, theirs, number * scale, scale, part)
    width = points // 2
    span //= 2
    while span:
        width //= 2
        upper = (freq_slot // span) % 2 == 1
        partner = [(slot, slot ^ span) for slot in range(freq_count)]
        keep = jnp.where(upper, image[width:], image[:width])
        away = jnp.where(upper, image[:width], image[width:])
        received = lax.ppermute(away, "freq", partner)
        image = (keep.astype(jnp.float32) + received.astype(jnp.float32)).astype(jnp.bfloat16)
        span //= 2
    panel = lax.all_to_all(image, "depth", split_axis=0, concat_axis=0, tiled=True)
    return angles(panel, angle_lag, depth_count)


def solution(mesh):
    placed = (
        P("depth", "freq", None, None, None),
        P("freq", None, None, None),
        P("freq", None, None, None),
        P(),
        P("freq"),
        P(),
    )
    return jax.shard_map(
        shards,
        mesh=mesh,
        in_specs=placed,
        out_specs=P(("freq", "depth"), None, None),
        check_vma=False,
    )
```

time: 127 us -> 117 us (0.921)
  Pallas kernels: 36.8 us -> 17.6 us
  blocking collectives: 24.6 us -> 35.4 us
  starting transfers between devices: 43.3 us -> 48.8 us
  waiting for transfers between devices: 14.9 us -> 11 us
  local copies, waits for them, and re-layouts: 4.22 us -> 1.01 us
    pallas_call x34 -> x54, Pallas kernels: 30.2 us -> 10.9 us  [the longest x45 8.23 us: extend(): pl.pallas_call(kernel, out_shape=[sent, kept] if sends else [kept], in_sp...]
    all_to_all x1, blocking collectives: 24.6 us -> 35.4 us  [shards(): lax.all_to_all(image, 'depth', split_axis=0, concat_axis=0, tiled=True)]
    ppermute x35 -> x49, starting transfers between devices: 43.2 us -> 48.8 us  [the longest x41 39.4 us: shards(): sent[parity, round_index] = lax.ppermute(order[0], 'depth', pairs)]
    ppermute x35 -> x49, waiting for transfers between devices: 13 us -> 9.11 us  [the longest x8 9 us: shards(): theirs.append(lax.ppermute(payload, 'freq', partner))]
    unnamed x16 -> x12, local copies, waits for them, and re-layouts: 3 us -> 0.93 us
  transfers between devices with their start and end apart: 36 -> 50, of which waited for: 3 -> 8; matrix products, arithmetic and copies ran while one was open for 1% -> 0% of each run, Pallas kernels for 24% -> 9%
where the time goes in v3:
time: 117 us; the launch traced here: 116 us
  starting transfers between devices  48.8 us (42%)
  blocking collectives  35.4 us (30%)
  Pallas kernels  17.6 us (15%)
  waiting for transfers between devices  11 us (9%)
  between operations  1.77 us (2%)
    ppermute x41, starting transfers between devices, shards(): sent[parity, round_index] = lax.ppermute(order[0], 'depth', pairs)  39.4 us
    all_to_all x1, blocking collectives, shards(): lax.all_to_all(image, 'depth', split_axis=0, concat_axis=0, tiled=True)  35.4 us
    ppermute x8, starting transfers between devices, shards(): theirs.append(lax.ppermute(payload, 'freq', partner))  9.33 us
    ppermute x8, waiting for transfers between devices, shards(): theirs.append(lax.ppermute(payload, 'freq', partner))  9 us
    pallas_call x45, Pallas kernels, extend(): pl.pallas_call(kernel, out_shape=[sent, kept] if sends else [kept], in_sp...  8.23 us
    pallas_call x1, Pallas kernels, head(): pl.pallas_call(kernel, out_shape=jax.ShapeDtypeStruct((4 * part, points),...  4.33 us
    pallas_call x1, Pallas kernels, surface(): pl.pallas_call(kernel, out_shape=[jax.ShapeDtypeStruct((chunk_count, 4 *...  2.51 us
  transfers between devices with their start and end apart: 50, of which 8 were waited for; matrix products, arithmetic and copies ran while one was open for 0% of the time, Pallas kernels for 9%

profile of v3, /device:TPU:0, one launch (start us, length us, event | category | flops | bytes accessed | tf_op | source)
XLA Modules:
  0.0 116.0 jit_solution(12450819015679351321)
XLA Ops:
  0.0 4.3 %shard_map.64.first_ref = bf16[64,1024]{1,0:T(8,128)(2,1)} custom-call(bf16[2,1024,1024]{2,1,0:T(8,128)(2,1)} %bitcast.14, bf16[128,2,1024]{2,1,0:T(2,128)(2,1)} %bitcast.61, bf16[128,2,1024]{2,1,0:T(2,128)(2,1)} %bitcast.63, s32[128]{0:T(128)} %shot_ref.1), custom_call_target="tpu_custom_call" | custom-call | tf_op jit(solution)/shard_map/pallas_call | solution.py:165
  4.3 4.9 %collective-permute-start.2 = (bf16[64,1024]{1,0:T(8,128)(2,1)}, bf16[64,1024]{1,0:T(8,128)(2,1)S(1)}, u32[]{:S(2)}, u32[]{:S(2)}) collective-permute-start(bf16[64,1024]{1,0:T(8,128)(2,1)} %shard_map.64.first_ref), channel_id=1, source_target_pairs={{0,4},{1,5},{2,6},{3,7}} | collective-permute-start | bytes 393224 | tf_op jit(solution)/shard_map/ppermute | solution.py:332
  9.3 0.9 copy-done.4
  10.2 2.5 %shard_map.65 = (bf16[8,64,1024]{2,1,0:T(8,128)(2,1)S(1)}, bf16[8,64,1024]{2,1,0:T(8,128)(2,1)S(1)}) custom-call(bf16[128,2,1024]{2,1,0:T(2,128)(2,1)S(1)} %bitcast.62, bf16[128,2,1024]{2,1,0:T(2,128)(2,1)S(1)} %bitcast.64, s32[128]{0:T(128)S(1)} %copy-done.5, bf16[64,1024]{1,0:T(8,128)(2,1)S(1)} %copy-done.4), custom_call_target="tpu_custom_call" | custom-call | tf_op jit(solution)/shard_map/pallas_call | solution.py:200
  12.8 1.0 shard_map.66
  13.8 1.3 %collective-permute-start.1 = (bf16[64,1024]{1,0:T(8,128)(2,1)S(1)}, bf16[64,1024]{1,0:T(8,128)(2,1)S(1)}, u32[]{:S(2)}, u32[]{:S(2)}) collective-permute-start(bf16[64,1024]{1,0:T(8,128)(2,1)S(1)} %get-tuple-element.107), channel_id=1, source_target_pairs={{0,4},{1,5},{2,6},{3,7}} | collective-permute-start | bytes 393224 | tf_op jit(solution)/shard_map/ppermute | solution.py:332
  15.1 1.0 shard_map.67
  16.2 1.3 %collective-permute-start = (bf16[64,1024]{1,0:T(8,128)(2,1)S(1)}, bf16[64,1024]{1,0:T(8,128)(2,1)S(1)}, u32[]{:S(2)}, u32[]{:S(2)}) collective-permute-start(bf16[64,1024]{1,0:T(8,128)(2,1)S(1)} %get-tuple-element.106), channel_id=1, source_target_pairs={{0,4},{1,5},{2,6},{3,7}} | collective-permute-start | bytes 393224 | tf_op jit(solution)/shard_map/ppermute | solution.py:332
  17.5 0.7 collective-permute-start.7
  18.2 1.0 shard_map.69
  19.2 1.3 %collective-permute-start.6 = (bf16[64,1024]{1,0:T(8,128)(2,1)S(1)}, bf16[64,1024]{1,0:T(8,128)(2,1)S(1)}, u32[]{:S(2)}, u32[]{:S(2)}) collective-permute-start(bf16[64,1024]{1,0:T(8,128)(2,1)S(1)} %get-tuple-element.116), channel_id=1, source_target_pairs={{0,4},{1,5},{2,6},{3,7}} | collective-permute-start | bytes 393224 | tf_op jit(solution)/shard_map/ppermute | solution.py:332
  20.6 0.7 collective-permute-start.5
  21.2 1.0 shard_map.71
  22.3 2.8 %collective-permute-start.4 = (bf16[64,1024]{1,0:T(8,128)(2,1)S(1)}, bf16[64,1024]{1,0:T(8,128)(2,1)S(1)}, u32[]{:S(2)}, u32[]{:S(2)}) collective-permute-start(bf16[64,1024]{1,0:T(8,128)(2,1)S(1)} %get-tuple-element.114), channel_id=1, source_target_pairs={{0,4},{1,5},{2,6},{3,7}} | collective-permute-start | bytes 393224 | tf_op jit(solution)/shard_map/ppermute | solution.py:332
  25.1 0.7 collective-permute-start.3
  25.8 1.0 shard_map.73
  26.8 1.9 %collective-permute-start.12 = (bf16[64,1024]{1,0:T(8,128)(2,1)S(1)}, bf16[64,1024]{1,0:T(8,128)(2,1)S(1)}, u32[]{:S(2)}, u32[]{:S(2)}) collective-permute-start(bf16[64,1024]{1,0:T(8,128)(2,1)S(1)} %get-tuple-element.127), channel_id=1, source_target_pairs={{0,4},{8,12},{1,5},{9,13},{2,6},{10,14},{3,7},{11,15}} | collective-permute-start | bytes 393224 | tf_op jit(solution)/shard_map/ppermute | solution.py:332
  28.8 0.7 collective-permute-start.11
  29.5 1.0 shard_map.75
  30.5 1.9 %collective-permute-start.10 = (bf16[64,1024]{1,0:T(8,128)(2,1)S(1)}, bf16[64,1024]{1,0:T(8,128)(2,1)S(1)}, u32[]{:S(2)}, u32[]{:S(2)}) collective-permute-start(bf16[64,1024]{1,0:T(8,128)(2,1)S(1)} %get-tuple-element.125), channel_id=1, source_target_pairs={{0,4},{8,12},{1,5},{9,13},{2,6},{10,14},{3,7},{11,15}} | collective-permute-start | bytes 393224 | tf_op jit(solution)/shard_map/ppermute | solution.py:332
  32.5 0.7 collective-permute-start.9
  33.2 1.0 shard_map.77
  34.2 1.9 %collective-permute-start.8 = (bf16[64,1024]{1,0:T(8,128)(2,1)S(1)}, bf16[64,1024]{1,0:T(8,128)(2,1)S(1)}, u32[]{:S(2)}, u32[]{:S(2)}) collective-permute-start(bf16[64,1024]{1,0:T(8,128)(2,1)S(1)} %get-tuple-element.123), channel_id=1, source_target_pairs={{0,4},{8,12},{1,5},{9,13},{2,6},{10,14},{3,7},{11,15}} | collective-permute-start | bytes 393224 | tf_op jit(solution)/shard_map/ppermute | solution.py:332
  36.2 0.7 collective-permute-start.17
  36.9 0.7 collective-permute-start.16
  37.6 0.7 collective-permute-start.15
  38.3 0.7 collective-permute-start.14
  40.7 0.7 collective-permute-start.21
  41.4 0.7 collective-permute-start.20
  42.1 0.7 collective-permute-start.19
  47.2 0.7 collective-permute-start.32
  47.9 0.7 collective-permute-start.31
  48.7 0.7 collective-permute-start.30
  49.4 0.7 collective-permute-start.29
  55.9 1.6 %collective-permute-start.41 = (bf16[48,1536]{1,0:T(8,128)(2,1)S(1)}, bf16[48,1536]{1,0:T(8,128)(2,1)S(1)}, u32[]{:S(2)}, u32[]{:S(2)}) collective-permute-start(bf16[48,1536]{1,0:T(8,128)(2,1)S(1)} %shard_map.99), channel_id=1, source_target_pairs={{0,2},{1,3},{2,0},{3,1},{4,6},{5,7},{6,4},{7,5},{8,10},{9,11},{10,... | collective-permute-start | bytes 442376 | tf_op jit(solution)/shard_map/ppermute | solution.py:338
  59.6 1.5 %collective-permute-start.42 = (bf16[32,1536]{1,0:T(8,128)(2,1)S(1)}, bf16[32,1536]{1,0:T(8,128)(2,1)S(1)}, u32[]{:S(2)}, u32[]{:S(2)}) collective-permute-start(bf16[32,1536]{1,0:T(8,128)(2,1)S(1)} %shard_map.102), channel_id=1, source_target_pairs={{0,2},{1,3},{2,0},{3,1},{4,6},{5,7},{6,4},{7,5},{8,10},{9,11},{10,... | collective-permute-start | bytes 294920 | tf_op jit(solution)/shard_map/ppermute | solution.py:338
  61.7 1.6 %collective-permute-start.44 = (bf16[32,1536]{1,0:T(8,128)(2,1)S(1)}, bf16[32,1536]{1,0:T(8,128)(2,1)S(1)}, u32[]{:S(2)}, u32[]{:S(2)}) collective-permute-start(bf16[32,1536]{1,0:T(8,128)(2,1)S(1)} %shard_map.108), channel_id=1, source_target_pairs={{0,2},{1,3},{2,0},{3,1},{4,6},{5,7},{6,4},{7,5},{8,10},{9,11},{10,... | collective-permute-start | bytes 294920 | tf_op jit(solution)/shard_map/ppermute | solution.py:338
  63.3 1.4 %collective-permute-done.43.refs_2_ = bf16[32,1536]{1,0:T(8,128)(2,1)S(1)} collective-permute-done((bf16[32,1536]{1,0:T(8,128)(2,1)S(1)}, bf16[32,1536]{1,0:T(8,128)(2,1)S(1)}, u32[]{:S(2)}, u32[]{:S(2)}) %collective-permute-start.43) | collective-permute-done | bytes 98336 | tf_op jit(solution)/shard_map/ppermute | solution.py:338
  64.8 1.5 %collective-permute-start.48 = (bf16[32,1536]{1,0:T(8,128)(2,1)S(1)}, bf16[32,1536]{1,0:T(8,128)(2,1)S(1)}, u32[]{:S(2)}, u32[]{:S(2)}) collective-permute-start(bf16[32,1536]{1,0:T(8,128)(2,1)S(1)} %shard_map.118), channel_id=1, source_target_pairs={{0,2},{1,3},{2,0},{3,1},{4,6},{5,7},{6,4},{7,5},{8,10},{9,11},{10,... | collective-permute-start | bytes 294920 | tf_op jit(solution)/shard_map/ppermute | solution.py:338
  66.9 1.5 %collective-permute-start.47 = (bf16[32,1536]{1,0:T(8,128)(2,1)S(1)}, bf16[32,1536]{1,0:T(8,128)(2,1)S(1)}, u32[]{:S(2)}, u32[]{:S(2)}) collective-permute-start(bf16[32,1536]{1,0:T(8,128)(2,1)S(1)} %shard_map.116), channel_id=1, source_target_pairs={{0,2},{1,3},{2,0},{3,1},{4,6},{5,7},{6,4},{7,5},{8,10},{9,11},{10,... | collective-permute-start | bytes 294920 | tf_op jit(solution)/shard_map/ppermute | solution.py:338
  69.0 2.1 %collective-permute-done.44.refs_3_ = bf16[32,1536]{1,0:T(8,128)(2,1)S(1)} collective-permute-done((bf16[32,1536]{1,0:T(8,128)(2,1)S(1)}, bf16[32,1536]{1,0:T(8,128)(2,1)S(1)}, u32[]{:S(2)}, u32[]{:S(2)}) %collective-permute-start.44) | collective-permute-done | bytes 98336 | tf_op jit(solution)/shard_map/ppermute | solution.py:338
  71.1 2.1 %collective-permute-done.48.refs_7_ = bf16[32,1536]{1,0:T(8,128)(2,1)S(1)} collective-permute-done((bf16[32,1536]{1,0:T(8,128)(2,1)S(1)}, bf16[32,1536]{1,0:T(8,128)(2,1)S(1)}, u32[]{:S(2)}, u32[]{:S(2)}) %collective-permute-start.48) | collective-permute-done | bytes 98336 | tf_op jit(solution)/shard_map/ppermute | solution.py:338
  73.2 1.6 %collective-permute-done.47.refs_6_ = bf16[32,1536]{1,0:T(8,128)(2,1)S(1)} collective-permute-done((bf16[32,1536]{1,0:T(8,128)(2,1)S(1)}, bf16[32,1536]{1,0:T(8,128)(2,1)S(1)}, u32[]{:S(2)}, u32[]{:S(2)}) %collective-permute-start.47) | collective-permute-done | bytes 98336 | tf_op jit(solution)/shard_map/ppermute | solution.py:338
  74.8 1.1 collective-permute-done.46.refs_5_
  75.8 0.8 shard_map.119
  76.8 1.9 %collective-permute-done.49 = bf16[256,1024]{1,0:T(8,128)(2,1)S(1)} collective-permute-done((bf16[256,1024]{1,0:T(8,128)(2,1)S(1)}, bf16[256,1024]{1,0:T(8,128)(2,1)S(1)}, u32[]{:S(2)}, u32[]{:S(2)}) %collective-permute-start.49) | collective-permute-done | bytes 524320 | tf_op jit(solution)/shard_map/ppermute | solution.py:350
  78.9 35.4 %all_to_all.11 = bf16[8,32,1024]{2,1,0:T(8,128)(2,1)S(1)} all-to-all(bf16[8,32,1024]{2,1,0:T(8,128)(2,1)S(1)} %bitcast.65), channel_id=1, replica_groups=mesh['depth'=8,'freq'=4] {'depth'}, dimensions={0} | all-to-all | bytes 1048576 | tf_op jit(solution)/shard_map/all_to_all | solution.py:353
  114.4 1.6 %shard_map.120 = f32[32,8,256]{2,1,0:T(8,128)} custom-call(bf16[256,1024]{1,0:T(8,128)(2,1)S(1)} %bitcast.60, s32[1024,256]{1,0:T(8,128)S(1)} %copy-done.3), custom_call_target="tpu_custom_call" | custom-call | tf_op jit(solution)/shard_map/pallas_call | solution.py:283
  (125 shorter events, 15.7 us)
Async XLA Ops:
  4.3 13.1 %collective-permute-start.2 = (bf16[64,1024]{1,0:T(8,128)(2,1)}, bf16[64,1024]{1,0:T(8,128)(2,1)S(1)}, u32[]{:S(2)}, u32[]{:S(2)}) collective-permute-start(bf16[64,1024]{1,0:T(8,128)(2,1)} %shard_map.64.first_ref), channel_id=1, source_target_pairs={{0,4},{1,5},{2,6},{3,7}} | collective-permute-start | bytes 393224 | tf_op jit(solution)/shard_map/ppermute | solution.py:332
  13.8 6.7 %collective-permute-start.1 = (bf16[64,1024]{1,0:T(8,128)(2,1)S(1)}, bf16[64,1024]{1,0:T(8,128)(2,1)S(1)}, u32[]{:S(2)}, u32[]{:S(2)}) collective-permute-start(bf16[64,1024]{1,0:T(8,128)(2,1)S(1)} %get-tuple-element.107), channel_id=1, source_target_pairs={{0,4},{1,5},{2,6},{3,7}} | collective-permute-start | bytes 393224 | tf_op jit(solution)/shard_map/ppermute | solution.py:332
  16.2 8.9 %collective-permute-start = (bf16[64,1024]{1,0:T(8,128)(2,1)S(1)}, bf16[64,1024]{1,0:T(8,128)(2,1)S(1)}, u32[]{:S(2)}, u32[]{:S(2)}) collective-permute-start(bf16[64,1024]{1,0:T(8,128)(2,1)S(1)} %get-tuple-element.106), channel_id=1, source_target_pairs={{0,4},{1,5},{2,6},{3,7}} | collective-permute-start | bytes 393224 | tf_op jit(solution)/shard_map/ppermute | solution.py:332
  17.5 8.3 %collective-permute-start.7 = (bf16[64,1024]{1,0:T(8,128)(2,1)S(1)}, bf16[64,1024]{1,0:T(8,128)(2,1)S(1)}, u32[]{:S(2)}, u32[]{:S(2)}) collective-permute-start(bf16[64,1024]{1,0:T(8,128)(2,1)S(1)} %get-tuple-element.117), channel_id=1, source_target_pairs={{4,8},{5,9},{6,10},{7,11}} | collective-permute-start | bytes 393224 | tf_op jit(solution)/shard_map/ppermute | solution.py:332
  19.2 9.5 %collective-permute-start.6 = (bf16[64,1024]{1,0:T(8,128)(2,1)S(1)}, bf16[64,1024]{1,0:T(8,128)(2,1)S(1)}, u32[]{:S(2)}, u32[]{:S(2)}) collective-permute-start(bf16[64,1024]{1,0:T(8,128)(2,1)S(1)} %get-tuple-element.116), channel_id=1, source_target_pairs={{0,4},{1,5},{2,6},{3,7}} | collective-permute-start | bytes 393224 | tf_op jit(solution)/shard_map/ppermute | solution.py:332
  20.6 8.9 %collective-permute-start.5 = (bf16[64,1024]{1,0:T(8,128)(2,1)S(1)}, bf16[64,1024]{1,0:T(8,128)(2,1)S(1)}, u32[]{:S(2)}, u32[]{:S(2)}) collective-permute-start(bf16[64,1024]{1,0:T(8,128)(2,1)S(1)} %get-tuple-element.115), channel_id=1, source_target_pairs={{4,8},{5,9},{6,10},{7,11}} | collective-permute-start | bytes 393224 | tf_op jit(solution)/shard_map/ppermute | solution.py:332
  22.3 10.2 %collective-permute-start.4 = (bf16[64,1024]{1,0:T(8,128)(2,1)S(1)}, bf16[64,1024]{1,0:T(8,128)(2,1)S(1)}, u32[]{:S(2)}, u32[]{:S(2)}) collective-permute-start(bf16[64,1024]{1,0:T(8,128)(2,1)S(1)} %get-tuple-element.114), channel_id=1, source_target_pairs={{0,4},{1,5},{2,6},{3,7}} | collective-permute-start | bytes 393224 | tf_op jit(solution)/shard_map/ppermute | solution.py:332
  25.1 8.1 %collective-permute-start.3 = (bf16[64,1024]{1,0:T(8,128)(2,1)S(1)}, bf16[64,1024]{1,0:T(8,128)(2,1)S(1)}, u32[]{:S(2)}, u32[]{:S(2)}) collective-permute-start(bf16[64,1024]{1,0:T(8,128)(2,1)S(1)} %get-tuple-element.113), channel_id=1, source_target_pairs={{4,8},{5,9},{6,10},{7,11}} | collective-permute-start | bytes 393224 | tf_op jit(solution)/shard_map/ppermute | solution.py:332
  26.8 9.3 %collective-permute-start.12 = (bf16[64,1024]{1,0:T(8,128)(2,1)S(1)}, bf16[64,1024]{1,0:T(8,128)(2,1)S(1)}, u32[]{:S(2)}, u32[]{:S(2)}) collective-permute-start(bf16[64,1024]{1,0:T(8,128)(2,1)S(1)} %get-tuple-element.127), channel_id=1, source_target_pairs={{0,4},{8,12},{1,5},{9,13},{2,6},{10,14},{3,7},{11,15}} | collective-permute-start | bytes 393224 | tf_op jit(solution)/shard_map/ppermute | solution.py:332
  28.8 8.1 %collective-permute-start.11 = (bf16[64,1024]{1,0:T(8,128)(2,1)S(1)}, bf16[64,1024]{1,0:T(8,128)(2,1)S(1)}, u32[]{:S(2)}, u32[]{:S(2)}) collective-permute-start(bf16[64,1024]{1,0:T(8,128)(2,1)S(1)} %get-tuple-element.126), channel_id=1, source_target_pairs={{4,8},{5,9},{6,10},{7,11}} | collective-permute-start | bytes 393224 | tf_op jit(solution)/shard_map/ppermute | solution.py:332
  30.5 7.1 %collective-permute-start.10 = (bf16[64,1024]{1,0:T(8,128)(2,1)S(1)}, bf16[64,1024]{1,0:T(8,128)(2,1)S(1)}, u32[]{:S(2)}, u32[]{:S(2)}) collective-permute-start(bf16[64,1024]{1,0:T(8,128)(2,1)S(1)} %get-tuple-element.125), channel_id=1, source_target_pairs={{0,4},{8,12},{1,5},{9,13},{2,6},{10,14},{3,7},{11,15}} | collective-permute-start | bytes 393224 | tf_op jit(solution)/shard_map/ppermute | solution.py:332
  32.5 5.8 %collective-permute-start.9 = (bf16[64,1024]{1,0:T(8,128)(2,1)S(1)}, bf16[64,1024]{1,0:T(8,128)(2,1)S(1)}, u32[]{:S(2)}, u32[]{:S(2)}) collective-permute-start(bf16[64,1024]{1,0:T(8,128)(2,1)S(1)} %get-tuple-element.124), channel_id=1, source_target_pairs={{4,8},{5,9},{6,10},{7,11}} | collective-permute-start | bytes 393224 | tf_op jit(solution)/shard_map/ppermute | solution.py:332
  34.2 4.8 %collective-permute-start.8 = (bf16[64,1024]{1,0:T(8,128)(2,1)S(1)}, bf16[64,1024]{1,0:T(8,128)(2,1)S(1)}, u32[]{:S(2)}, u32[]{:S(2)}) collective-permute-start(bf16[64,1024]{1,0:T(8,128)(2,1)S(1)} %get-tuple-element.123), channel_id=1, source_target_pairs={{0,4},{8,12},{1,5},{9,13},{2,6},{10,14},{3,7},{11,15}} | collective-permute-start | bytes 393224 | tf_op jit(solution)/shard_map/ppermute | solution.py:332
  36.2 3.6 %collective-permute-start.17 = (bf16[64,1024]{1,0:T(8,128)(2,1)S(1)}, bf16[64,1024]{1,0:T(8,128)(2,1)S(1)}, u32[]{:S(2)}, u32[]{:S(2)}) collective-permute-start(bf16[64,1024]{1,0:T(8,128)(2,1)S(1)} %get-tuple-element.137), channel_id=1, source_target_pairs={{4,8},{12,16},{5,9},{13,17},{6,10},{14,18},{7,11},{15,19}} | collective-permute-start | bytes 393224 | tf_op jit(solution)/shard_map/ppermute | solution.py:332
  36.9 3.8 %collective-permute-start.16 = (bf16[64,1024]{1,0:T(8,128)(2,1)S(1)}, bf16[64,1024]{1,0:T(8,128)(2,1)S(1)}, u32[]{:S(2)}, u32[]{:S(2)}) collective-permute-start(bf16[64,1024]{1,0:T(8,128)(2,1)S(1)} %get-tuple-element.136), channel_id=1, source_target_pairs={{8,12},{16,20},{9,13},{17,21},{10,14},{18,22},{11,15},{19,23}} | collective-permute-start | bytes 393224 | tf_op jit(solution)/shard_map/ppermute | solution.py:332
  37.6 3.8 %collective-permute-start.15 = (bf16[64,1024]{1,0:T(8,128)(2,1)S(1)}, bf16[64,1024]{1,0:T(8,128)(2,1)S(1)}, u32[]{:S(2)}, u32[]{:S(2)}) collective-permute-start(bf16[64,1024]{1,0:T(8,128)(2,1)S(1)} %get-tuple-element.135), channel_id=1, source_target_pairs={{4,8},{12,16},{5,9},{13,17},{6,10},{14,18},{7,11},{15,19}} | collective-permute-start | bytes 393224 | tf_op jit(solution)/shard_map/ppermute | solution.py:332
  38.3 3.8 %collective-permute-start.14 = (bf16[64,1024]{1,0:T(8,128)(2,1)S(1)}, bf16[64,1024]{1,0:T(8,128)(2,1)S(1)}, u32[]{:S(2)}, u32[]{:S(2)}) collective-permute-start(bf16[64,1024]{1,0:T(8,128)(2,1)S(1)} %get-tuple-element.134), channel_id=1, source_target_pairs={{8,12},{16,20},{9,13},{17,21},{10,14},{18,22},{11,15},{19,23}} | collective-permute-start | bytes 393224 | tf_op jit(solution)/shard_map/ppermute | solution.py:332
  39.1 3.8 %collective-permute-start.13 = (bf16[64,1024]{1,0:T(8,128)(2,1)S(1)}, bf16[64,1024]{1,0:T(8,128)(2,1)S(1)}, u32[]{:S(2)}, u32[]{:S(2)}) collective-permute-start(bf16[64,1024]{1,0:T(8,128)(2,1)S(1)} %get-tuple-element.133), channel_id=1, source_target_pairs={{4,8},{12,16},{5,9},{13,17},{6,10},{14,18},{7,11},{15,19}} | collective-permute-start | bytes 393224 | tf_op jit(solution)/shard_map/ppermute | solution.py:332
  40.0 3.6 %collective-permute-start.22 = (bf16[64,1024]{1,0:T(8,128)(2,1)S(1)}, bf16[64,1024]{1,0:T(8,128)(2,1)S(1)}, u32[]{:S(2)}, u32[]{:S(2)}) collective-permute-start(bf16[64,1024]{1,0:T(8,128)(2,1)S(1)} %get-tuple-element.147), channel_id=1, source_target_pairs={{8,12},{16,20},{9,13},{17,21},{10,14},{18,22},{11,15},{19,23}} | collective-permute-start | bytes 393224 | tf_op jit(solution)/shard_map/ppermute | solution.py:332
  40.7 3.6 %collective-permute-start.21 = (bf16[64,1024]{1,0:T(8,128)(2,1)S(1)}, bf16[64,1024]{1,0:T(8,128)(2,1)S(1)}, u32[]{:S(2)}, u32[]{:S(2)}) collective-permute-start(bf16[64,1024]{1,0:T(8,128)(2,1)S(1)} %get-tuple-element.146), channel_id=1, source_target_pairs={{12,16},{20,24},{13,17},{21,25},{14,18},{22,26},{15,19},{23,27}} | collective-permute-start | bytes 393224 | tf_op jit(solution)/shard_map/ppermute | solution.py:332
  41.4 3.6 %collective-permute-start.20 = (bf16[64,1024]{1,0:T(8,128)(2,1)S(1)}, bf16[64,1024]{1,0:T(8,128)(2,1)S(1)}, u32[]{:S(2)}, u32[]{:S(2)}) collective-permute-start(bf16[64,1024]{1,0:T(8,128)(2,1)S(1)} %get-tuple-element.145), channel_id=1, source_target_pairs={{8,12},{16,20},{9,13},{17,21},{10,14},{18,22},{11,15},{19,23}} | collective-permute-start | bytes 393224 | tf_op jit(solution)/shard_map/ppermute | solution.py:332
  42.1 3.6 %collective-permute-start.19 = (bf16[64,1024]{1,0:T(8,128)(2,1)S(1)}, bf16[64,1024]{1,0:T(8,128)(2,1)S(1)}, u32[]{:S(2)}, u32[]{:S(2)}) collective-permute-start(bf16[64,1024]{1,0:T(8,128)(2,1)S(1)} %get-tuple-element.144), channel_id=1, source_target_pairs={{12,16},{20,24},{13,17},{21,25},{14,18},{22,26},{15,19},{23,27}} | collective-permute-start | bytes 393224 | tf_op jit(solution)/shard_map/ppermute | solution.py:332
  42.9 3.6 %collective-permute-start.18 = (bf16[64,1024]{1,0:T(8,128)(2,1)S(1)}, bf16[64,1024]{1,0:T(8,128)(2,1)S(1)}, u32[]{:S(2)}, u32[]{:S(2)}) collective-permute-start(bf16[64,1024]{1,0:T(8,128)(2,1)S(1)} %get-tuple-element.143), channel_id=1, source_target_pairs={{8,12},{16,20},{9,13},{17,21},{10,14},{18,22},{11,15},{19,23}} | collective-permute-start | bytes 393224 | tf_op jit(solution)/shard_map/ppermute | solution.py:332
  43.6 3.6 %collective-permute-start.27 = (bf16[64,1024]{1,0:T(8,128)(2,1)S(1)}, bf16[64,1024]{1,0:T(8,128)(2,1)S(1)}, u32[]{:S(2)}, u32[]{:S(2)}) collective-permute-start(bf16[64,1024]{1,0:T(8,128)(2,1)S(1)} %get-tuple-element.157), channel_id=1, source_target_pairs={{12,16},{20,24},{13,17},{21,25},{14,18},{22,26},{15,19},{23,27}} | collective-permute-start | bytes 393224 | tf_op jit(solution)/shard_map/ppermute | solution.py:332
  44.3 3.6 %collective-permute-start.26 = (bf16[64,1024]{1,0:T(8,128)(2,1)S(1)}, bf16[64,1024]{1,0:T(8,128)(2,1)S(1)}, u32[]{:S(2)}, u32[]{:S(2)}) collective-permute-start(bf16[64,1024]{1,0:T(8,128)(2,1)S(1)} %get-tuple-element.156), channel_id=1, source_target_pairs={{16,20},{24,28},{17,21},{25,29},{18,22},{26,30},{19,23},{27,31}} | collective-permute-start | bytes 393224 | tf_op jit(solution)/shard_map/ppermute | solution.py:332
  45.0 3.6 %collective-permute-start.25 = (bf16[64,1024]{1,0:T(8,128)(2,1)S(1)}, bf16[64,1024]{1,0:T(8,128)(2,1)S(1)}, u32[]{:S(2)}, u32[]{:S(2)}) collective-permute-start(bf16[64,1024]{1,0:T(8,128)(2,1)S(1)} %get-tuple-element.155), channel_id=1, source_target_pairs={{12,16},{20,24},{13,17},{21,25},{14,18},{22,26},{15,19},{23,27}} | collective-permute-start | bytes 393224 | tf_op jit(solution)/shard_map/ppermute | solution.py:332
  45.8 3.6 %collective-permute-start.24 = (bf16[64,1024]{1,0:T(8,128)(2,1)S(1)}, bf16[64,1024]{1,0:T(8,128)(2,1)S(1)}, u32[]{:S(2)}, u32[]{:S(2)}) collective-permute-start(bf16[64,1024]{1,0:T(8,128)(2,1)S(1)} %get-tuple-element.154), channel_id=1, source_target_pairs={{16,20},{24,28},{17,21},{25,29},{18,22},{26,30},{19,23},{27,31}} | collective-permute-start | bytes 393224 | tf_op jit(solution)/shard_map/ppermute | solution.py:332
  46.5 3.6 %collective-permute-start.23 = (bf16[64,1024]{1,0:T(8,128)(2,1)S(1)}, bf16[64,1024]{1,0:T(8,128)(2,1)S(1)}, u32[]{:S(2)}, u32[]{:S(2)}) collective-permute-start(bf16[64,1024]{1,0:T(8,128)(2,1)S(1)} %get-tuple-element.153), channel_id=1, source_target_pairs={{12,16},{20,24},{13,17},{21,25},{14,18},{22,26},{15,19},{23,27}} | collective-permute-start | bytes 393224 | tf_op jit(solution)/shard_map/ppermute | solution.py:332
  47.2 3.6 %collective-permute-start.32 = (bf16[64,1024]{1,0:T(8,128)(2,1)S(1)}, bf16[64,1024]{1,0:T(8,128)(2,1)S(1)}, u32[]{:S(2)}, u32[]{:S(2)}) collective-permute-start(bf16[64,1024]{1,0:T(8,128)(2,1)S(1)} %get-tuple-element.167), channel_id=1, source_target_pairs={{16,20},{24,28},{17,21},{25,29},{18,22},{26,30},{19,23},{27,31}} | collective-permute-start | bytes 393224 | tf_op jit(solution)/shard_map/ppermute | solution.py:332
  47.9 4.3 %collective-permute-start.31 = (bf16[64,1024]{1,0:T(8,128)(2,1)S(1)}, bf16[64,1024]{1,0:T(8,128)(2,1)S(1)}, u32[]{:S(2)}, u32[]{:S(2)}) collective-permute-start(bf16[64,1024]{1,0:T(8,128)(2,1)S(1)} %get-tuple-element.166), channel_id=1, source_target_pairs={{20,24},{21,25},{22,26},{23,27}} | collective-permute-start | bytes 393224 | tf_op jit(solution)/shard_map/ppermute | solution.py:332
  48.7 4.3 %collective-permute-start.30 = (bf16[64,1024]{1,0:T(8,128)(2,1)S(1)}, bf16[64,1024]{1,0:T(8,128)(2,1)S(1)}, u32[]{:S(2)}, u32[]{:S(2)}) collective-permute-start(bf16[64,1024]{1,0:T(8,128)(2,1)S(1)} %get-tuple-element.165), channel_id=1, source_target_pairs={{16,20},{24,28},{17,21},{25,29},{18,22},{26,30},{19,23},{27,31}} | collective-permute-start | bytes 393224 | tf_op jit(solution)/shard_map/ppermute | solution.py:332
  49.4 4.3 %collective-permute-start.29 = (bf16[64,1024]{1,0:T(8,128)(2,1)S(1)}, bf16[64,1024]{1,0:T(8,128)(2,1)S(1)}, u32[]{:S(2)}, u32[]{:S(2)}) collective-permute-start(bf16[64,1024]{1,0:T(8,128)(2,1)S(1)} %get-tuple-element.164), channel_id=1, source_target_pairs={{20,24},{21,25},{22,26},{23,27}} | collective-permute-start | bytes 393224 | tf_op jit(solution)/shard_map/ppermute | solution.py:332
  50.1 4.3 %collective-permute-start.28 = (bf16[64,1024]{1,0:T(8,128)(2,1)S(1)}, bf16[64,1024]{1,0:T(8,128)(2,1)S(1)}, u32[]{:S(2)}, u32[]{:S(2)}) collective-permute-start(bf16[64,1024]{1,0:T(8,128)(2,1)S(1)} %get-tuple-element.163), channel_id=1, source_target_pairs={{16,20},{24,28},{17,21},{25,29},{18,22},{26,30},{19,23},{27,31}} | collective-permute-start | bytes 393224 | tf_op jit(solution)/shard_map/ppermute | solution.py:332
  50.8 4.3 %collective-permute-start.37 = (bf16[64,1024]{1,0:T(8,128)(2,1)S(1)}, bf16[64,1024]{1,0:T(8,128)(2,1)S(1)}, u32[]{:S(2)}, u32[]{:S(2)}) collective-permute-start(bf16[64,1024]{1,0:T(8,128)(2,1)S(1)} %get-tuple-element.179), channel_id=1, source_target_pairs={{20,24},{21,25},{22,26},{23,27}} | collective-permute-start | bytes 393224 | tf_op jit(solution)/shard_map/ppermute | solution.py:332
  52.2 3.6 %collective-permute-start.36 = (bf16[64,1024]{1,0:T(8,128)(2,1)S(1)}, bf16[64,1024]{1,0:T(8,128)(2,1)S(1)}, u32[]{:S(2)}, u32[]{:S(2)}) collective-permute-start(bf16[64,1024]{1,0:T(8,128)(2,1)S(1)} %get-tuple-element.178), channel_id=1, source_target_pairs={{24,28},{25,29},{26,30},{27,31}} | collective-permute-start | bytes 393224 | tf_op jit(solution)/shard_map/ppermute | solution.py:332
  53.0 4.5 %collective-permute-start.35 = (bf16[64,1024]{1,0:T(8,128)(2,1)S(1)}, bf16[64,1024]{1,0:T(8,128)(2,1)S(1)}, u32[]{:S(2)}, u32[]{:S(2)}) collective-permute-start(bf16[64,1024]{1,0:T(8,128)(2,1)S(1)} %get-tuple-element.177), channel_id=1, source_target_pairs={{20,24},{21,25},{22,26},{23,27}} | collective-permute-start | bytes 393224 | tf_op jit(solution)/shard_map/ppermute | solution.py:332
  53.7 4.5 %collective-permute-start.34 = (bf16[64,1024]{1,0:T(8,128)(2,1)S(1)}, bf16[64,1024]{1,0:T(8,128)(2,1)S(1)}, u32[]{:S(2)}, u32[]{:S(2)}) collective-permute-start(bf16[64,1024]{1,0:T(8,128)(2,1)S(1)} %get-tuple-element.176), channel_id=1, source_target_pairs={{24,28},{25,29},{26,30},{27,31}} | collective-permute-start | bytes 393224 | tf_op jit(solution)/shard_map/ppermute | solution.py:332
  54.5 3.8 %collective-permute-start.33 = (bf16[64,1024]{1,0:T(8,128)(2,1)S(1)}, bf16[64,1024]{1,0:T(8,128)(2,1)S(1)}, u32[]{:S(2)}, u32[]{:S(2)}) collective-permute-start(bf16[64,1024]{1,0:T(8,128)(2,1)S(1)} %get-tuple-element.175), channel_id=1, source_target_pairs={{20,24},{21,25},{22,26},{23,27}} | collective-permute-start | bytes 393224 | tf_op jit(solution)/shard_map/ppermute | solution.py:332
  55.2 4.4 %collective-permute-start.40 = (bf16[64,1024]{1,0:T(8,128)(2,1)S(1)}, bf16[64,1024]{1,0:T(8,128)(2,1)S(1)}, u32[]{:S(2)}, u32[]{:S(2)}) collective-permute-start(bf16[64,1024]{1,0:T(8,128)(2,1)S(1)} %get-tuple-element.188), channel_id=1, source_target_pairs={{24,28},{25,29},{26,30},{27,31}} | collective-permute-start | bytes 393224 | tf_op jit(solution)/shard_map/ppermute | solution.py:332
  55.9 12.5 %collective-permute-start.41 = (bf16[48,1536]{1,0:T(8,128)(2,1)S(1)}, bf16[48,1536]{1,0:T(8,128)(2,1)S(1)}, u32[]{:S(2)}, u32[]{:S(2)}) collective-permute-start(bf16[48,1536]{1,0:T(8,128)(2,1)S(1)} %shard_map.99), channel_id=1, source_target_pairs={{0,2},{1,3},{2,0},{3,1},{4,6},{5,7},{6,4},{7,5},{8,10},{9,11},{10,... | collective-permute-start | bytes 442376 | tf_op jit(solution)/shard_map/ppermute | solution.py:338
  57.5 3.6 %collective-permute-start.39 = (bf16[64,1024]{1,0:T(8,128)(2,1)S(1)}, bf16[64,1024]{1,0:T(8,128)(2,1)S(1)}, u32[]{:S(2)}, u32[]{:S(2)}) collective-permute-start(bf16[64,1024]{1,0:T(8,128)(2,1)S(1)} %get-tuple-element.187), channel_id=1, source_target_pairs={{24,28},{25,29},{26,30},{27,31}} | collective-permute-start | bytes 393224 | tf_op jit(solution)/shard_map/ppermute | solution.py:332
  59.0 5.8 %collective-permute-start.43 = (bf16[32,1536]{1,0:T(8,128)(2,1)S(1)}, bf16[32,1536]{1,0:T(8,128)(2,1)S(1)}, u32[]{:S(2)}, u32[]{:S(2)}) collective-permute-start(bf16[32,1536]{1,0:T(8,128)(2,1)S(1)} %shard_map.105), channel_id=1, source_target_pairs={{0,2},{1,3},{2,0},{3,1},{4,6},{5,7},{6,4},{7,5},{8,10},{9,11},{10,... | collective-permute-start | bytes 294920 | tf_op jit(solution)/shard_map/ppermute | solution.py:338
  59.6 7.3 %collective-permute-start.42 = (bf16[32,1536]{1,0:T(8,128)(2,1)S(1)}, bf16[32,1536]{1,0:T(8,128)(2,1)S(1)}, u32[]{:S(2)}, u32[]{:S(2)}) collective-permute-start(bf16[32,1536]{1,0:T(8,128)(2,1)S(1)} %shard_map.102), channel_id=1, source_target_pairs={{0,2},{1,3},{2,0},{3,1},{4,6},{5,7},{6,4},{7,5},{8,10},{9,11},{10,... | collective-permute-start | bytes 294920 | tf_op jit(solution)/shard_map/ppermute | solution.py:338
  61.1 7.9 %collective-permute-start.45 = (bf16[32,1536]{1,0:T(8,128)(2,1)S(1)}, bf16[32,1536]{1,0:T(8,128)(2,1)S(1)}, u32[]{:S(2)}, u32[]{:S(2)}) collective-permute-start(bf16[32,1536]{1,0:T(8,128)(2,1)S(1)} %shard_map.111), channel_id=1, source_target_pairs={{0,2},{1,3},{2,0},{3,1},{4,6},{5,7},{6,4},{7,5},{8,10},{9,11},{10,... | collective-permute-start | bytes 294920 | tf_op jit(solution)/shard_map/ppermute | solution.py:338
  61.7 9.4 %collective-permute-start.44 = (bf16[32,1536]{1,0:T(8,128)(2,1)S(1)}, bf16[32,1536]{1,0:T(8,128)(2,1)S(1)}, u32[]{:S(2)}, u32[]{:S(2)}) collective-permute-start(bf16[32,1536]{1,0:T(8,128)(2,1)S(1)} %shard_map.108), channel_id=1, source_target_pairs={{0,2},{1,3},{2,0},{3,1},{4,6},{5,7},{6,4},{7,5},{8,10},{9,11},{10,... | collective-permute-start | bytes 294920 | tf_op jit(solution)/shard_map/ppermute | solution.py:338
  64.8 8.4 %collective-permute-start.48 = (bf16[32,1536]{1,0:T(8,128)(2,1)S(1)}, bf16[32,1536]{1,0:T(8,128)(2,1)S(1)}, u32[]{:S(2)}, u32[]{:S(2)}) collective-permute-start(bf16[32,1536]{1,0:T(8,128)(2,1)S(1)} %shard_map.118), channel_id=1, source_target_pairs={{0,2},{1,3},{2,0},{3,1},{4,6},{5,7},{6,4},{7,5},{8,10},{9,11},{10,... | collective-permute-start | bytes 294920 | tf_op jit(solution)/shard_map/ppermute | solution.py:338
  66.9 7.9 %collective-permute-start.47 = (bf16[32,1536]{1,0:T(8,128)(2,1)S(1)}, bf16[32,1536]{1,0:T(8,128)(2,1)S(1)}, u32[]{:S(2)}, u32[]{:S(2)}) collective-permute-start(bf16[32,1536]{1,0:T(8,128)(2,1)S(1)} %shard_map.116), channel_id=1, source_target_pairs={{0,2},{1,3},{2,0},{3,1},{4,6},{5,7},{6,4},{7,5},{8,10},{9,11},{10,... | collective-permute-start | bytes 294920 | tf_op jit(solution)/shard_map/ppermute | solution.py:338
  68.4 7.5 %collective-permute-start.46 = (bf16[32,1536]{1,0:T(8,128)(2,1)S(1)}, bf16[32,1536]{1,0:T(8,128)(2,1)S(1)}, u32[]{:S(2)}, u32[]{:S(2)}) collective-permute-start(bf16[32,1536]{1,0:T(8,128)(2,1)S(1)} %shard_map.114), channel_id=1, source_target_pairs={{0,2},{1,3},{2,0},{3,1},{4,6},{5,7},{6,4},{7,5},{8,10},{9,11},{10,... | collective-permute-start | bytes 294920 | tf_op jit(solution)/shard_map/ppermute | solution.py:338
  (8 other events, 97.9 us)

commit v4 on v3

--- a/solution.py
+++ b/solution.py
@@ -8,9 +8,9 @@
 from jax.sharding import PartitionSpec as P
 
 CHUNKS = 8
-GROUPS = (1,) * CHUNKS
+GROUPS = (3, 2, 2, 1)
 LAGS = (3, 2)
-TILES = 2
+EARLY = LAGS[1]
 
 WHOLE = pl.BlockSpec(memory_space=pltpu.VMEM)
 FAR = pl.BlockSpec(memory_space=pltpu.HBM)
@@ -35,21 +35,19 @@
     return everyone[first : max(first + wanted, last + 1)]
 
 
-def march(values, extrap_ref, out_ref):
-    half = out_ref.shape[0] // 2
-    points = out_ref.shape[1]
-    width = points // TILES
-
-    @pl.loop(0, TILES)
-    def _(tile):
-        column = pl.ds(pl.multiple_of(tile * width, width), width)
-        real = jnp.dot(values, extrap_ref[0, :, column], preferred_element_type=jnp.float32)
-        imag = jnp.dot(values, extrap_ref[1, :, column], preferred_element_type=jnp.float32)
-        out_ref[:half, column] = (real[:half] - imag[half:]).astype(out_ref.dtype)
-        out_ref[half:, column] = (imag[:half] + real[half:]).astype(out_ref.dtype)
-
-
-def extend(arrived, extrap, finished, round_index, parity, above, sends):
+def march(values, extrap_ref, out_refs):
+    rows = out_refs[0].shape[0]
+    half = rows // 2
+    real = jnp.dot(values, extrap_ref[0], preferred_element_type=jnp.float32)
+    imag = jnp.dot(values, extrap_ref[1], preferred_element_type=jnp.float32)
+    for chunk, out_ref in enumerate(out_refs):
+        upper = slice(chunk * rows, chunk * rows + half)
+        lower = slice(chunk * rows + half, (chunk + 1) * rows)
+        out_ref[:half] = (real[upper] - imag[lower]).astype(out_ref.dtype)
+        out_ref[half:] = (imag[upper] + real[lower]).astype(out_ref.dtype)
+
+
+def extend(arrived, extrap, finished, round_index, parity, sends):
     rows, points = arrived.shape
     chunk_count = finished.shape[0]
 
@@ -57,18 +55,13 @@
         finished_ref = refs[-1]
         level = lax.axis_index("depth")
         chunk = round_index - first_round(level)
-        mine = (level % 2 == parity) & (chunk >= 0) & (chunk < chunk_count)
+        mine = (level > 0) & (level % 2 == parity) & (chunk >= 0) & (chunk < chunk_count)
         place_ref = finished_ref.at[jnp.clip(chunk, 0, chunk_count - 1)]
         out_ref = refs[-2] if sends else place_ref
-        if above:
-
-            @pl.when(level == 0)
-            def _():
-                march(refs[0][0], extrap_ref, out_ref)
-
-        @pl.when(mine & ((level > 0) | (not above)))
+
+        @pl.when(mine)
         def _():
-            march(arrived_ref[...], extrap_ref, out_ref)
+            march(arrived_ref[...], extrap_ref, [out_ref])
 
         if sends:
 
@@ -76,17 +69,23 @@
             def _():
                 place_ref[...] = out_ref[...]
 
+            if parity == 0 and round_index < chunk_count:
+
+                @pl.when(level == 0)
+                def _():
+                    out_ref[...] = finished_ref[round_index]
+
     kept = jax.ShapeDtypeStruct(finished.shape, finished.dtype)
     sent = jax.ShapeDtypeStruct((rows, points), jnp.bfloat16)
     return pl.pallas_call(
         kernel,
         out_shape=[sent, kept] if sends else [kept],
-        in_specs=[WHOLE, WHOLE, WHOLE] + [WHOLE] * len(above),
+        in_specs=[WHOLE, WHOLE, WHOLE],
         out_specs=[WHOLE, WHOLE] if sends else [WHOLE],
         input_output_aliases={2: 1 if sends else 0},
         compiler_params=pltpu.CompilerParams(vmem_limit_bytes=8 << 20),
         cost_estimate=BRIEF,
-    )(arrived, extrap, finished, *above)
+    )(arrived, extrap, finished)
 
 
 def pack(finished, number, start, stop, noted):
@@ -119,91 +118,100 @@
     )(finished, number)
 
 
-def picked(shot_ref, source_ref, span, component):
+def fill(out_ref, shot_ref, source_ref, record_ref, first, part):
     shot_count = source_ref.shape[0]
-    count = span.stop - span.start
+    chunk_count = out_ref.shape[0] // (4 * part)
     pick = (
-        shot_ref[span][None, :] == lax.broadcasted_iota(jnp.int32, (shot_count, count), 0)
+        shot_ref[...][None, :] == lax.broadcasted_iota(jnp.int32, (shot_count, shot_count), 0)
     ).astype(jnp.bfloat16)
-    return lax.dot_general(
-        pick,
-        source_ref[:, component, :],
-        (((0,), (0,)), ((), ())),
-        preferred_element_type=jnp.float32,
-    ).astype(jnp.bfloat16)
-
-
-def fill(out_ref, shot_ref, source_ref, record_ref, span):
-    part = out_ref.shape[0] // 4
-    out_ref[:part] = picked(shot_ref, source_ref, span, 0)
-    out_ref[part : 2 * part] = record_ref[span, 1, :]
-    out_ref[2 * part : 3 * part] = picked(shot_ref, source_ref, span, 1)
-    out_ref[3 * part :] = record_ref[span, 0, :]
+
+    def picked(component):
+        return lax.dot_general(
+            pick,
+            source_ref[:, component, :],
+            (((0,), (0,)), ((), ())),
+            preferred_element_type=jnp.float32,
+        ).astype(jnp.bfloat16)
+
+    for place, values in (
+        (0, picked(0)),
+        (1, record_ref[:, 1, :]),
+        (2, picked(1)),
+        (3, record_ref[:, 0, :]),
+    ):
+        for chunk in range(chunk_count):
+            row = (4 * chunk + place) * part
+            shot = (first + chunk) * part
+            out_ref[row : row + part] = values[shot : shot + part]
 
 
 def head(extrap, sources, records, shots, part):
     points = extrap.shape[2]
-
-    def kernel(
-        extrap_hbm, source_hbm, record_hbm, shot_hbm, out_ref,
-        extrap_ref, source_ref, record_ref, shot_ref, chunk_ref, sems,
-    ):
-        copies = [
-            pltpu.make_async_copy(shot_hbm, shot_ref, sems.at[0]),
-            pltpu.make_async_copy(source_hbm, source_ref, sems.at[1]),
-            pltpu.make_async_copy(record_hbm.at[pl.ds(0, part)], record_ref, sems.at[2]),
-            pltpu.make_async_copy(extrap_hbm, extrap_ref, sems.at[3]),
-        ]
-        for copy in copies:
-            copy.start()
-        for copy in copies[:3]:
-            copy.wait()
-        fill(chunk_ref, shot_ref, source_ref, record_ref, slice(0, part))
-        copies[3].wait()
-        march(chunk_ref[...], extrap_ref, out_ref)
-
-    return pl.pallas_call(
-        kernel,
-        out_shape=jax.ShapeDtypeStruct((4 * part, points), jnp.bfloat16),
+    rows = 4 * part
+
+    def kernel(extrap_hbm, source_hbm, record_hbm, shot_hbm, *refs):
+        out_refs = refs[:EARLY]
+        extrap_ref, source_ref, record_ref, shot_ref, chunk_ref, sems = refs[EARLY:]
+
+        @pl.when(lax.axis_index("depth") == 0)
+        def _():
+            copies = [
+                pltpu.make_async_copy(shot_hbm, shot_ref, sems.at[0]),
+                pltpu.make_async_copy(source_hbm, source_ref, sems.at[1]),
+                pltpu.make_async_copy(record_hbm.at[pl.ds(0, EARLY * part)], record_ref, sems.at[2]),
+                pltpu.make_async_copy(extrap_hbm, extrap_ref, sems.at[3]),
+            ]
+            for copy in copies:
+                copy.start()
+            for copy in copies[:3]:
+                copy.wait()
+            fill(chunk_ref, shot_ref, source_ref, record_ref, 0, part)
+            copies[3].wait()
+            march(chunk_ref[...], extrap_ref, out_refs)
+
+    return pl.pallas_call(
+        kernel,
+        out_shape=[jax.ShapeDtypeStruct((rows, points), jnp.bfloat16)] * EARLY,
         in_specs=[FAR] * 4,
-        out_specs=WHOLE,
+        out_specs=[WHOLE] * EARLY,
         scratch_shapes=[
             pltpu.VMEM(extrap.shape, extrap.dtype),
             pltpu.VMEM(sources.shape, sources.dtype),
-            pltpu.VMEM((part,) + records.shape[1:], records.dtype),
+            pltpu.VMEM((EARLY * part,) + records.shape[1:], records.dtype),
             pltpu.VMEM(shots.shape, shots.dtype),
-            pltpu.VMEM((4 * part, points), jnp.bfloat16),
+            pltpu.VMEM((EARLY * rows, points), jnp.bfloat16),
             pltpu.SemaphoreType.DMA((4,)),
         ],
         compiler_params=pltpu.CompilerParams(vmem_limit_bytes=56 << 20),
     )(extrap, sources, records, shots)
 
 
-def surface(sources, records, shots, chunk_count, first):
+def rest(extrap, sources, records, shots, firsts, chunk_count):
     shot_count, _, points = sources.shape
     part = shot_count // chunk_count
-
-    def kernel(source_ref, record_ref, shot_ref, first_ref, out_ref, finished_ref):
-        finished_ref[0] = first_ref[...]
-        everything = slice(0, shot_count)
-        for place, values in (
-            (0, picked(shot_ref, source_ref, everything, 0)),
-            (1, record_ref[:, 1, :]),
-            (2, picked(shot_ref, source_ref, everything, 1)),
-            (3, record_ref[:, 0, :]),
-        ):
-            for chunk in range(chunk_count):
-                out_ref[chunk, place * part : (place + 1) * part] = values[
-                    chunk * part : (chunk + 1) * part
-                ]
-
-    return pl.pallas_call(
-        kernel,
-        out_shape=[jax.ShapeDtypeStruct((chunk_count, 4 * part, points), jnp.bfloat16)] * 2,
-        in_specs=[WHOLE] * 4,
-        out_specs=[WHOLE] * 2,
-        compiler_params=pltpu.CompilerParams(vmem_limit_bytes=12 << 20),
-    )(sources, records, shots, first)
+    rows = 4 * part
+
+    def kernel(extrap_ref, source_ref, record_ref, shot_ref, *refs):
+        first_refs = refs[: len(firsts)]
+        finished_ref, chunk_ref = refs[len(firsts) :]
+
+        @pl.when(lax.axis_index("depth") == 0)
+        def _():
+            fill(chunk_ref, shot_ref, source_ref, record_ref, len(firsts), part)
+            others = [finished_ref.at[chunk] for chunk in range(len(firsts), chunk_count)]
+            march(chunk_ref[...], extrap_ref, others)
+            for chunk, first_ref in enumerate(first_refs):
+                finished_ref[chunk] = first_ref[...]
+
+    return pl.pallas_call(
+        kernel,
+        out_shape=jax.ShapeDtypeStruct((chunk_count, rows, points), jnp.bfloat16),
+        in_specs=[WHOLE] * (4 + len(firsts)),
+        out_specs=WHOLE,
+        scratch_shapes=[pltpu.VMEM(((chunk_count - len(firsts)) * rows, points), jnp.bfloat16)],
+        compiler_params=pltpu.CompilerParams(vmem_limit_bytes=16 << 20),
+        cost_estimate=BRIEF,
+    )(extrap, sources, records, shots, *firsts)
 
 
 def correlate(finished, theirs, own_scale, unit, part):
@@ -300,8 +308,7 @@
 
     operator = extrap[0, 0]
     sources, records = source_field[0], record_field[0]
-    order = [head(operator, sources, records, shot_of_record, part)]
-    above, finished = surface(sources, records, shot_of_record, chunk_count, order[0])
+    firsts = head(operator, sources, records, shot_of_record, part)
 
     number = freq_index[0].astype(jnp.float32).reshape(1, 1) + 1.0
     span = freq_count // 2
@@ -311,25 +318,28 @@
     theirs = []
     round_count = first_round(depth_count - 1) + chunk_count
     for round_index in range(round_count):
+        if round_index == EARLY:
+            finished = rest(operator, sources, records, shot_of_record, firsts, chunk_count)
         for parity in (0, 1):
-            levels = [
-                z for z in range(parity, depth_count, 2) if handled(round_index, z, chunk_count)
+            if not any(
+                handled(round_index, level, chunk_count)
+                for level in range(parity, depth_count, 2)
+            ):
+                continue
+            pairs = [
+                (level, level + 1)
+                for level in senders(round_index, parity, depth_count, chunk_count)
             ]
-            if not levels:
-                continue
-            pairs = [(z, z + 1) for z in senders(round_index, parity, depth_count, chunk_count)]
-            if round_index or parity:
-                arrived = sent.get((1 - parity, round_index - LAGS[parity]))
-                entering = ()
-                if parity == 0 and round_index < chunk_count:
-                    entering = (above[round_index : round_index + 1],)
-                    if arrived is None:
-                        arrived, entering = above[round_index], ()
+            if round_index < EARLY:
+                order = firsts[round_index]
+            else:
+                arrived = sent.get((1 - parity, round_index - LAGS[parity]), firsts[0])
                 *order, finished = extend(
-                    arrived, operator, finished, round_index, parity, entering, bool(pairs)
+                    arrived, operator, finished, round_index, parity, bool(pairs)
                 )
+                order = order[0] if pairs else None
             if pairs:
-                sent[parity, round_index] = lax.ppermute(order[0], "depth", pairs)
+                sent[parity, round_index] = lax.ppermute(order, "depth", pairs)
         stop = sum(GROUPS[: len(theirs) + 1])
         if len(theirs) < len(GROUPS) and round_index - first_round(depth_count - 1) == stop - 1:
             start = stop - GROUPS[len(theirs)]

time: 117 us -> 109 us (0.932)
  starting transfers between devices: 48.8 us -> 44.7 us
  Pallas kernels: 17.6 us -> 13.7 us
  blocking collectives: 35.4 us -> 32.4 us
  waiting for transfers between devices: 11 us -> 13.3 us
    pallas_call x45 -> x44, Pallas kernels: 8.23 us -> 1.61 us  [extend(): pl.pallas_call(kernel, out_shape=[sent, kept] if sends else [kept], in_sp...]
    ppermute x8 -> x4, starting transfers between devices: 9.33 us -> 4.9 us  [shards(): theirs.append(lax.ppermute(payload, 'freq', partner))]
    all_to_all x1, blocking collectives: 35.4 us -> 32.4 us  [shards(): lax.all_to_all(image, 'depth', split_axis=0, concat_axis=0, tiled=True)]
    ppermute x8 -> x4, waiting for transfers between devices: 9 us -> 11.3 us  [shards(): theirs.append(lax.ppermute(payload, 'freq', partner))]
    pallas_call x2, Pallas kernels: 6.85 us -> 8.28 us  [the longest x1 4.38 us: head(): pl.pallas_call(kernel, out_shape=[jax.ShapeDtypeStruct((rows, points), jn...]
    pallas_call x8 -> x4, Pallas kernels: 0.16 us -> 1.43 us  [pack(): pl.pallas_call(kernel, out_shape=jax.ShapeDtypeStruct((count + 16 * noted...]
  transfers between devices with their start and end apart: 50 -> 46, of which waited for: 8 -> 3; matrix products, arithmetic and copies ran while one was open for 0% -> 0% of each run, Pallas kernels for 9% -> 6%
where the time goes in v4:
time: 109 us; the launch traced here: 108 us
  starting transfers between devices  44.7 us (41%)
  blocking collectives  32.4 us (30%)
  Pallas kernels  13.7 us (13%)
  waiting for transfers between devices  13.3 us (12%)
  local copies, waits for them, and re-layouts  1.82 us (2%)
  between operations  1.7 us (2%)
    ppermute x41, starting transfers between devices, shards(): sent[parity, round_index] = lax.ppermute(order, 'depth', pairs)  39.7 us
    all_to_all x1, blocking collectives, shards(): lax.all_to_all(image, 'depth', split_axis=0, concat_axis=0, tiled=True)  32.4 us
    ppermute x4, waiting for transfers between devices, shards(): theirs.append(lax.ppermute(payload, 'freq', partner))  11.3 us
    ppermute x4, starting transfers between devices, shards(): theirs.append(lax.ppermute(payload, 'freq', partner))  4.9 us
    pallas_call x1, Pallas kernels, head(): pl.pallas_call(kernel, out_shape=[jax.ShapeDtypeStruct((rows, points), jn...  4.38 us
    pallas_call x1, Pallas kernels, rest(): pl.pallas_call(kernel, out_shape=jax.ShapeDtypeStruct((chunk_count, rows,...  3.9 us
  transfers between devices with their start and end apart: 46, of which 3 were waited for; matrix products, arithmetic and copies ran while one was open for 0% of the time, Pallas kernels for 6%

profile of v4, /device:TPU:0, one launch (start us, length us, event | category | flops | bytes accessed | tf_op | source)
XLA Modules:
  0.0 108.0 jit_solution(16485911154304340048)
XLA Ops:
  0.0 4.4 %shard_map.64 = (bf16[64,1024]{1,0:T(8,128)(2,1)}, bf16[64,1024]{1,0:T(8,128)(2,1)}) custom-call(bf16[2,1024,1024]{2,1,0:T(8,128)(2,1)} %bitcast.6, bf16[128,2,1024]{2,1,0:T(2,128)(2,1)} %bitcast.53, bf16[128,2,1024]{2,1,0:T(2,128)(2,1)} %bitcast.55, s32[128]{0:T(128)} %shot_ref.1), custom_call_target="tpu_custom_call" | custom-call | tf_op jit(solution)/shard_map/pallas_call | solution.py:172
  4.4 1.5 %collective-permute-start.2 = (bf16[64,1024]{1,0:T(8,128)(2,1)}, bf16[64,1024]{1,0:T(8,128)(2,1)S(1)}, u32[]{:S(2)}, u32[]{:S(2)}) collective-permute-start(bf16[64,1024]{1,0:T(8,128)(2,1)} %get-tuple-element.93.refs_0_.arrived_ref), channel_id=1, source_target_pairs={{0,4},{1,5},{2,6},{3,7}} | collective-permute-start | bytes 393224 | tf_op jit(solution)/shard_map/ppermute | solution.py:342
  5.9 1.3 %collective-permute-start.1 = (bf16[64,1024]{1,0:T(8,128)(2,1)}, bf16[64,1024]{1,0:T(8,128)(2,1)S(1)}, u32[]{:S(2)}, u32[]{:S(2)}) collective-permute-start(bf16[64,1024]{1,0:T(8,128)(2,1)} %get-tuple-element.94.refs_1_), channel_id=1, source_target_pairs={{0,4},{1,5},{2,6},{3,7}} | collective-permute-start | bytes 393224 | tf_op jit(solution)/shard_map/ppermute | solution.py:342
  7.3 0.9 copy-done.3
  8.2 0.9 copy-done.5
  9.1 3.9 %shard_map.65.finished_in = bf16[8,64,1024]{2,1,0:T(8,128)(2,1)S(1)} custom-call(bf16[2,1024,1024]{2,1,0:T(8,128)(2,1)S(1)} %bitcast.7, bf16[128,2,1024]{2,1,0:T(2,128)(2,1)S(1)} %bitcast.54, bf16[128,2,1024]{2,1,0:T(2,128)(2,1)S(1)} %bitcast.56, s32[128]{0:T(128)S(1)} %copy-done.6, bf16[64,1024]{1,0:T(8,128)(2,1)S(1)} %copy-done.3, ...), custom_call_target="tpu_custom_call" | custom-call | tf_op jit(solution)/shard_map/pallas_call | solution.py:206
  13.0 1.3 %collective-permute-start = (bf16[64,1024]{1,0:T(8,128)(2,1)S(1)}, bf16[64,1024]{1,0:T(8,128)(2,1)S(1)}, u32[]{:S(2)}, u32[]{:S(2)}) collective-permute-start(bf16[64,1024]{1,0:T(8,128)(2,1)S(1)} %get-tuple-element.95), channel_id=1, source_target_pairs={{0,4},{1,5},{2,6},{3,7}} | collective-permute-start | bytes 393224 | tf_op jit(solution)/shard_map/ppermute | solution.py:342
  14.4 0.7 collective-permute-start.7
  15.1 1.4 %collective-permute-start.6 = (bf16[64,1024]{1,0:T(8,128)(2,1)S(1)}, bf16[64,1024]{1,0:T(8,128)(2,1)S(1)}, u32[]{:S(2)}, u32[]{:S(2)}) collective-permute-start(bf16[64,1024]{1,0:T(8,128)(2,1)S(1)} %get-tuple-element.104), channel_id=1, source_target_pairs={{0,4},{1,5},{2,6},{3,7}} | collective-permute-start | bytes 393224 | tf_op jit(solution)/shard_map/ppermute | solution.py:342
  16.5 0.7 collective-permute-start.5
  17.3 2.8 %collective-permute-start.4 = (bf16[64,1024]{1,0:T(8,128)(2,1)S(1)}, bf16[64,1024]{1,0:T(8,128)(2,1)S(1)}, u32[]{:S(2)}, u32[]{:S(2)}) collective-permute-start(bf16[64,1024]{1,0:T(8,128)(2,1)S(1)} %get-tuple-element.102), channel_id=1, source_target_pairs={{0,4},{1,5},{2,6},{3,7}} | collective-permute-start | bytes 393224 | tf_op jit(solution)/shard_map/ppermute | solution.py:342
  20.1 0.7 collective-permute-start.3
  20.8 3.9 %collective-permute-start.12 = (bf16[64,1024]{1,0:T(8,128)(2,1)S(1)}, bf16[64,1024]{1,0:T(8,128)(2,1)S(1)}, u32[]{:S(2)}, u32[]{:S(2)}) collective-permute-start(bf16[64,1024]{1,0:T(8,128)(2,1)S(1)} %get-tuple-element.115), channel_id=1, source_target_pairs={{0,4},{8,12},{1,5},{9,13},{2,6},{10,14},{3,7},{11,15}} | collective-permute-start | bytes 393224 | tf_op jit(solution)/shard_map/ppermute | solution.py:342
  24.8 0.7 collective-permute-start.11
  25.5 2.8 %collective-permute-start.10 = (bf16[64,1024]{1,0:T(8,128)(2,1)S(1)}, bf16[64,1024]{1,0:T(8,128)(2,1)S(1)}, u32[]{:S(2)}, u32[]{:S(2)}) collective-permute-start(bf16[64,1024]{1,0:T(8,128)(2,1)S(1)} %get-tuple-element.113), channel_id=1, source_target_pairs={{0,4},{8,12},{1,5},{9,13},{2,6},{10,14},{3,7},{11,15}} | collective-permute-start | bytes 393224 | tf_op jit(solution)/shard_map/ppermute | solution.py:342
  28.3 0.7 collective-permute-start.9
  29.2 2.8 %collective-permute-start.8 = (bf16[64,1024]{1,0:T(8,128)(2,1)S(1)}, bf16[64,1024]{1,0:T(8,128)(2,1)S(1)}, u32[]{:S(2)}, u32[]{:S(2)}) collective-permute-start(bf16[64,1024]{1,0:T(8,128)(2,1)S(1)} %get-tuple-element.111), channel_id=1, source_target_pairs={{0,4},{8,12},{1,5},{9,13},{2,6},{10,14},{3,7},{11,15}} | collective-permute-start | bytes 393224 | tf_op jit(solution)/shard_map/ppermute | solution.py:342
  32.0 0.7 collective-permute-start.17
  32.7 0.7 collective-permute-start.16
  33.5 0.7 collective-permute-start.15
  34.2 0.7 collective-permute-start.14
  34.9 0.7 collective-permute-start.13
  35.6 0.7 collective-permute-start.22
  36.4 0.7 collective-permute-start.21
  37.1 0.7 collective-permute-start.20
  37.8 0.7 collective-permute-start.19
  38.5 0.7 collective-permute-start.18
  39.3 0.7 collective-permute-start.27
  40.0 0.7 collective-permute-start.26
  40.7 0.7 collective-permute-start.25
  41.4 0.7 collective-permute-start.24
  42.1 0.7 collective-permute-start.23
  42.9 0.7 collective-permute-start.32
  43.6 0.7 collective-permute-start.31
  44.3 0.7 collective-permute-start.30
  45.0 0.7 collective-permute-start.29
  46.0 0.7 collective-permute-start.28
  46.7 0.7 collective-permute-start.37
  51.0 2.7 %collective-permute-start.41 = (bf16[112,1536]{1,0:T(8,128)(2,1)S(1)}, bf16[112,1536]{1,0:T(8,128)(2,1)S(1)}, u32[]{:S(2)}, u32[]{:S(2)}) collective-permute-start(bf16[112,1536]{1,0:T(8,128)(2,1)S(1)} %shard_map.102), channel_id=1, source_target_pairs={{0,2},{1,3},{2,0},{3,1},{4,6},{5,7},{6,4},{7,5},{8,10},{9,11},{10,... | collective-permute-start | bytes 1032200 | tf_op jit(solution)/shard_map/ppermute | solution.py:348
  55.3 0.7 collective-permute-start.38
  56.1 0.7 shard_map.111
  56.8 1.9 %collective-permute-start.43 = (bf16[64,1536]{1,0:T(8,128)(2,1)}, bf16[64,1536]{1,0:T(8,128)(2,1)S(1)}, u32[]{:S(2)}, u32[]{:S(2)}) collective-permute-start(bf16[64,1536]{1,0:T(8,128)(2,1)} %shard_map.111), channel_id=1, source_target_pairs={{0,2},{1,3},{2,0},{3,1},{4,6},{5,7},{6,4},{7,5},{8,10},{9,11},{10,... | collective-permute-start | bytes 589832 | tf_op jit(solution)/shard_map/ppermute | solution.py:348
  59.5 7.4 %collective-permute-done.42.refs_1_ = bf16[64,1536]{1,0:T(8,128)(2,1)S(1)} collective-permute-done((bf16[64,1536]{1,0:T(8,128)(2,1)S(1)}, bf16[64,1536]{1,0:T(8,128)(2,1)S(1)}, u32[]{:S(2)}, u32[]{:S(2)}) %collective-permute-start.42) | collective-permute-done | bytes 196640 | tf_op jit(solution)/shard_map/ppermute | solution.py:348
  66.9 3.9 %collective-permute-done.44.refs_3_ = bf16[32,1536]{1,0:T(8,128)(2,1)S(1)} collective-permute-done((bf16[32,1536]{1,0:T(8,128)(2,1)}, bf16[32,1536]{1,0:T(8,128)(2,1)S(1)}, u32[]{:S(2)}, u32[]{:S(2)}) %collective-permute-start.44) | collective-permute-done | bytes 98336 | tf_op jit(solution)/shard_map/ppermute | solution.py:348
  70.8 0.8 shard_map.114
  71.7 1.9 %collective-permute-done.45 = bf16[256,1024]{1,0:T(8,128)(2,1)S(1)} collective-permute-done((bf16[256,1024]{1,0:T(8,128)(2,1)S(1)}, bf16[256,1024]{1,0:T(8,128)(2,1)S(1)}, u32[]{:S(2)}, u32[]{:S(2)}) %collective-permute-start.45) | collective-permute-done | bytes 524320 | tf_op jit(solution)/shard_map/ppermute | solution.py:360
  73.9 32.4 %all_to_all.11 = bf16[8,32,1024]{2,1,0:T(8,128)(2,1)S(1)} all-to-all(bf16[8,32,1024]{2,1,0:T(8,128)(2,1)S(1)} %bitcast.57), channel_id=1, replica_groups=mesh['depth'=8,'freq'=4] {'depth'}, dimensions={0} | all-to-all | bytes 1048576 | tf_op jit(solution)/shard_map/all_to_all | solution.py:363
  106.3 1.6 %shard_map.115 = f32[32,8,256]{2,1,0:T(8,128)} custom-call(bf16[256,1024]{1,0:T(8,128)(2,1)S(1)} %bitcast.52, s32[1024,256]{1,0:T(8,128)S(1)} %copy-done.4), custom_call_target="tpu_custom_call" | custom-call | tf_op jit(solution)/shard_map/pallas_call | solution.py:291
  (113 shorter events, 7.1 us)
Async XLA Ops:
  0.0 7.2 %copy-start.6 = (s32[128]{0:T(128)S(1)}, s32[128]{0:T(128)}, u32[]{:S(2)}) copy-start(s32[128]{0:T(128)} %shot_ref.1) | copy-start | bytes 1540
  4.4 9.9 %collective-permute-start.2 = (bf16[64,1024]{1,0:T(8,128)(2,1)}, bf16[64,1024]{1,0:T(8,128)(2,1)S(1)}, u32[]{:S(2)}, u32[]{:S(2)}) collective-permute-start(bf16[64,1024]{1,0:T(8,128)(2,1)} %get-tuple-element.93.refs_0_.arrived_ref), channel_id=1, source_target_pairs={{0,4},{1,5},{2,6},{3,7}} | collective-permute-start | bytes 393224 | tf_op jit(solution)/shard_map/ppermute | solution.py:342
  5.9 10.6 %collective-permute-start.1 = (bf16[64,1024]{1,0:T(8,128)(2,1)}, bf16[64,1024]{1,0:T(8,128)(2,1)S(1)}, u32[]{:S(2)}, u32[]{:S(2)}) collective-permute-start(bf16[64,1024]{1,0:T(8,128)(2,1)} %get-tuple-element.94.refs_1_), channel_id=1, source_target_pairs={{0,4},{1,5},{2,6},{3,7}} | collective-permute-start | bytes 393224 | tf_op jit(solution)/shard_map/ppermute | solution.py:342
  13.0 7.0 %collective-permute-start = (bf16[64,1024]{1,0:T(8,128)(2,1)S(1)}, bf16[64,1024]{1,0:T(8,128)(2,1)S(1)}, u32[]{:S(2)}, u32[]{:S(2)}) collective-permute-start(bf16[64,1024]{1,0:T(8,128)(2,1)S(1)} %get-tuple-element.95), channel_id=1, source_target_pairs={{0,4},{1,5},{2,6},{3,7}} | collective-permute-start | bytes 393224 | tf_op jit(solution)/shard_map/ppermute | solution.py:342
  14.4 6.4 %collective-permute-start.7 = (bf16[64,1024]{1,0:T(8,128)(2,1)S(1)}, bf16[64,1024]{1,0:T(8,128)(2,1)S(1)}, u32[]{:S(2)}, u32[]{:S(2)}) collective-permute-start(bf16[64,1024]{1,0:T(8,128)(2,1)S(1)} %get-tuple-element.105), channel_id=1, source_target_pairs={{4,8},{5,9},{6,10},{7,11}} | collective-permute-start | bytes 393224 | tf_op jit(solution)/shard_map/ppermute | solution.py:342
  15.1 9.6 %collective-permute-start.6 = (bf16[64,1024]{1,0:T(8,128)(2,1)S(1)}, bf16[64,1024]{1,0:T(8,128)(2,1)S(1)}, u32[]{:S(2)}, u32[]{:S(2)}) collective-permute-start(bf16[64,1024]{1,0:T(8,128)(2,1)S(1)} %get-tuple-element.104), channel_id=1, source_target_pairs={{0,4},{1,5},{2,6},{3,7}} | collective-permute-start | bytes 393224 | tf_op jit(solution)/shard_map/ppermute | solution.py:342
  16.5 8.9 %collective-permute-start.5 = (bf16[64,1024]{1,0:T(8,128)(2,1)S(1)}, bf16[64,1024]{1,0:T(8,128)(2,1)S(1)}, u32[]{:S(2)}, u32[]{:S(2)}) collective-permute-start(bf16[64,1024]{1,0:T(8,128)(2,1)S(1)} %get-tuple-element.103), channel_id=1, source_target_pairs={{4,8},{5,9},{6,10},{7,11}} | collective-permute-start | bytes 393224 | tf_op jit(solution)/shard_map/ppermute | solution.py:342
  17.3 11.0 %collective-permute-start.4 = (bf16[64,1024]{1,0:T(8,128)(2,1)S(1)}, bf16[64,1024]{1,0:T(8,128)(2,1)S(1)}, u32[]{:S(2)}, u32[]{:S(2)}) collective-permute-start(bf16[64,1024]{1,0:T(8,128)(2,1)S(1)} %get-tuple-element.102), channel_id=1, source_target_pairs={{0,4},{1,5},{2,6},{3,7}} | collective-permute-start | bytes 393224 | tf_op jit(solution)/shard_map/ppermute | solution.py:342
  20.1 8.9 %collective-permute-start.3 = (bf16[64,1024]{1,0:T(8,128)(2,1)S(1)}, bf16[64,1024]{1,0:T(8,128)(2,1)S(1)}, u32[]{:S(2)}, u32[]{:S(2)}) collective-permute-start(bf16[64,1024]{1,0:T(8,128)(2,1)S(1)} %get-tuple-element.101), channel_id=1, source_target_pairs={{4,8},{5,9},{6,10},{7,11}} | collective-permute-start | bytes 393224 | tf_op jit(solution)/shard_map/ppermute | solution.py:342
  20.8 11.2 %collective-permute-start.12 = (bf16[64,1024]{1,0:T(8,128)(2,1)S(1)}, bf16[64,1024]{1,0:T(8,128)(2,1)S(1)}, u32[]{:S(2)}, u32[]{:S(2)}) collective-permute-start(bf16[64,1024]{1,0:T(8,128)(2,1)S(1)} %get-tuple-element.115), channel_id=1, source_target_pairs={{0,4},{8,12},{1,5},{9,13},{2,6},{10,14},{3,7},{11,15}} | collective-permute-start | bytes 393224 | tf_op jit(solution)/shard_map/ppermute | solution.py:342
  24.8 7.9 %collective-permute-start.11 = (bf16[64,1024]{1,0:T(8,128)(2,1)S(1)}, bf16[64,1024]{1,0:T(8,128)(2,1)S(1)}, u32[]{:S(2)}, u32[]{:S(2)}) collective-permute-start(bf16[64,1024]{1,0:T(8,128)(2,1)S(1)} %get-tuple-element.114), channel_id=1, source_target_pairs={{4,8},{5,9},{6,10},{7,11}} | collective-permute-start | bytes 393224 | tf_op jit(solution)/shard_map/ppermute | solution.py:342
  25.5 7.9 %collective-permute-start.10 = (bf16[64,1024]{1,0:T(8,128)(2,1)S(1)}, bf16[64,1024]{1,0:T(8,128)(2,1)S(1)}, u32[]{:S(2)}, u32[]{:S(2)}) collective-permute-start(bf16[64,1024]{1,0:T(8,128)(2,1)S(1)} %get-tuple-element.113), channel_id=1, source_target_pairs={{0,4},{8,12},{1,5},{9,13},{2,6},{10,14},{3,7},{11,15}} | collective-permute-start | bytes 393224 | tf_op jit(solution)/shard_map/ppermute | solution.py:342
  28.3 5.8 %collective-permute-start.9 = (bf16[64,1024]{1,0:T(8,128)(2,1)S(1)}, bf16[64,1024]{1,0:T(8,128)(2,1)S(1)}, u32[]{:S(2)}, u32[]{:S(2)}) collective-permute-start(bf16[64,1024]{1,0:T(8,128)(2,1)S(1)} %get-tuple-element.112), channel_id=1, source_target_pairs={{4,8},{5,9},{6,10},{7,11}} | collective-permute-start | bytes 393224 | tf_op jit(solution)/shard_map/ppermute | solution.py:342
  29.2 5.7 %collective-permute-start.8 = (bf16[64,1024]{1,0:T(8,128)(2,1)S(1)}, bf16[64,1024]{1,0:T(8,128)(2,1)S(1)}, u32[]{:S(2)}, u32[]{:S(2)}) collective-permute-start(bf16[64,1024]{1,0:T(8,128)(2,1)S(1)} %get-tuple-element.111), channel_id=1, source_target_pairs={{0,4},{8,12},{1,5},{9,13},{2,6},{10,14},{3,7},{11,15}} | collective-permute-start | bytes 393224 | tf_op jit(solution)/shard_map/ppermute | solution.py:342
  32.0 3.6 %collective-permute-start.17 = (bf16[64,1024]{1,0:T(8,128)(2,1)S(1)}, bf16[64,1024]{1,0:T(8,128)(2,1)S(1)}, u32[]{:S(2)}, u32[]{:S(2)}) collective-permute-start(bf16[64,1024]{1,0:T(8,128)(2,1)S(1)} %get-tuple-element.125), channel_id=1, source_target_pairs={{4,8},{12,16},{5,9},{13,17},{6,10},{14,18},{7,11},{15,19}} | collective-permute-start | bytes 393224 | tf_op jit(solution)/shard_map/ppermute | solution.py:342
  32.7 3.6 %collective-permute-start.16 = (bf16[64,1024]{1,0:T(8,128)(2,1)S(1)}, bf16[64,1024]{1,0:T(8,128)(2,1)S(1)}, u32[]{:S(2)}, u32[]{:S(2)}) collective-permute-start(bf16[64,1024]{1,0:T(8,128)(2,1)S(1)} %get-tuple-element.124), channel_id=1, source_target_pairs={{8,12},{16,20},{9,13},{17,21},{10,14},{18,22},{11,15},{19,23}} | collective-permute-start | bytes 393224 | tf_op jit(solution)/shard_map/ppermute | solution.py:342
  33.5 3.6 %collective-permute-start.15 = (bf16[64,1024]{1,0:T(8,128)(2,1)S(1)}, bf16[64,1024]{1,0:T(8,128)(2,1)S(1)}, u32[]{:S(2)}, u32[]{:S(2)}) collective-permute-start(bf16[64,1024]{1,0:T(8,128)(2,1)S(1)} %get-tuple-element.123), channel_id=1, source_target_pairs={{4,8},{12,16},{5,9},{13,17},{6,10},{14,18},{7,11},{15,19}} | collective-permute-start | bytes 393224 | tf_op jit(solution)/shard_map/ppermute | solution.py:342
  34.2 3.6 %collective-permute-start.14 = (bf16[64,1024]{1,0:T(8,128)(2,1)S(1)}, bf16[64,1024]{1,0:T(8,128)(2,1)S(1)}, u32[]{:S(2)}, u32[]{:S(2)}) collective-permute-start(bf16[64,1024]{1,0:T(8,128)(2,1)S(1)} %get-tuple-element.122), channel_id=1, source_target_pairs={{8,12},{16,20},{9,13},{17,21},{10,14},{18,22},{11,15},{19,23}} | collective-permute-start | bytes 393224 | tf_op jit(solution)/shard_map/ppermute | solution.py:342
  34.9 3.6 %collective-permute-start.13 = (bf16[64,1024]{1,0:T(8,128)(2,1)S(1)}, bf16[64,1024]{1,0:T(8,128)(2,1)S(1)}, u32[]{:S(2)}, u32[]{:S(2)}) collective-permute-start(bf16[64,1024]{1,0:T(8,128)(2,1)S(1)} %get-tuple-element.121), channel_id=1, source_target_pairs={{4,8},{12,16},{5,9},{13,17},{6,10},{14,18},{7,11},{15,19}} | collective-permute-start | bytes 393224 | tf_op jit(solution)/shard_map/ppermute | solution.py:342
  35.6 3.6 %collective-permute-start.22 = (bf16[64,1024]{1,0:T(8,128)(2,1)S(1)}, bf16[64,1024]{1,0:T(8,128)(2,1)S(1)}, u32[]{:S(2)}, u32[]{:S(2)}) collective-permute-start(bf16[64,1024]{1,0:T(8,128)(2,1)S(1)} %get-tuple-element.135), channel_id=1, source_target_pairs={{8,12},{16,20},{9,13},{17,21},{10,14},{18,22},{11,15},{19,23}} | collective-permute-start | bytes 393224 | tf_op jit(solution)/shard_map/ppermute | solution.py:342
  36.4 3.6 %collective-permute-start.21 = (bf16[64,1024]{1,0:T(8,128)(2,1)S(1)}, bf16[64,1024]{1,0:T(8,128)(2,1)S(1)}, u32[]{:S(2)}, u32[]{:S(2)}) collective-permute-start(bf16[64,1024]{1,0:T(8,128)(2,1)S(1)} %get-tuple-element.134), channel_id=1, source_target_pairs={{12,16},{20,24},{13,17},{21,25},{14,18},{22,26},{15,19},{23,27}} | collective-permute-start | bytes 393224 | tf_op jit(solution)/shard_map/ppermute | solution.py:342
  37.1 3.6 %collective-permute-start.20 = (bf16[64,1024]{1,0:T(8,128)(2,1)S(1)}, bf16[64,1024]{1,0:T(8,128)(2,1)S(1)}, u32[]{:S(2)}, u32[]{:S(2)}) collective-permute-start(bf16[64,1024]{1,0:T(8,128)(2,1)S(1)} %get-tuple-element.133), channel_id=1, source_target_pairs={{8,12},{16,20},{9,13},{17,21},{10,14},{18,22},{11,15},{19,23}} | collective-permute-start | bytes 393224 | tf_op jit(solution)/shard_map/ppermute | solution.py:342
  37.8 3.6 %collective-permute-start.19 = (bf16[64,1024]{1,0:T(8,128)(2,1)S(1)}, bf16[64,1024]{1,0:T(8,128)(2,1)S(1)}, u32[]{:S(2)}, u32[]{:S(2)}) collective-permute-start(bf16[64,1024]{1,0:T(8,128)(2,1)S(1)} %get-tuple-element.132), channel_id=1, source_target_pairs={{12,16},{20,24},{13,17},{21,25},{14,18},{22,26},{15,19},{23,27}} | collective-permute-start | bytes 393224 | tf_op jit(solution)/shard_map/ppermute | solution.py:342
  38.5 3.6 %collective-permute-start.18 = (bf16[64,1024]{1,0:T(8,128)(2,1)S(1)}, bf16[64,1024]{1,0:T(8,128)(2,1)S(1)}, u32[]{:S(2)}, u32[]{:S(2)}) collective-permute-start(bf16[64,1024]{1,0:T(8,128)(2,1)S(1)} %get-tuple-element.131), channel_id=1, source_target_pairs={{8,12},{16,20},{9,13},{17,21},{10,14},{18,22},{11,15},{19,23}} | collective-permute-start | bytes 393224 | tf_op jit(solution)/shard_map/ppermute | solution.py:342
  39.3 3.6 %collective-permute-start.27 = (bf16[64,1024]{1,0:T(8,128)(2,1)S(1)}, bf16[64,1024]{1,0:T(8,128)(2,1)S(1)}, u32[]{:S(2)}, u32[]{:S(2)}) collective-permute-start(bf16[64,1024]{1,0:T(8,128)(2,1)S(1)} %get-tuple-element.145), channel_id=1, source_target_pairs={{12,16},{20,24},{13,17},{21,25},{14,18},{22,26},{15,19},{23,27}} | collective-permute-start | bytes 393224 | tf_op jit(solution)/shard_map/ppermute | solution.py:342
  40.0 3.6 %collective-permute-start.26 = (bf16[64,1024]{1,0:T(8,128)(2,1)S(1)}, bf16[64,1024]{1,0:T(8,128)(2,1)S(1)}, u32[]{:S(2)}, u32[]{:S(2)}) collective-permute-start(bf16[64,1024]{1,0:T(8,128)(2,1)S(1)} %get-tuple-element.144), channel_id=1, source_target_pairs={{16,20},{24,28},{17,21},{25,29},{18,22},{26,30},{19,23},{27,31}} | collective-permute-start | bytes 393224 | tf_op jit(solution)/shard_map/ppermute | solution.py:342
  40.7 3.6 %collective-permute-start.25 = (bf16[64,1024]{1,0:T(8,128)(2,1)S(1)}, bf16[64,1024]{1,0:T(8,128)(2,1)S(1)}, u32[]{:S(2)}, u32[]{:S(2)}) collective-permute-start(bf16[64,1024]{1,0:T(8,128)(2,1)S(1)} %get-tuple-element.143), channel_id=1, source_target_pairs={{12,16},{20,24},{13,17},{21,25},{14,18},{22,26},{15,19},{23,27}} | collective-permute-start | bytes 393224 | tf_op jit(solution)/shard_map/ppermute | solution.py:342
  41.4 3.6 %collective-permute-start.24 = (bf16[64,1024]{1,0:T(8,128)(2,1)S(1)}, bf16[64,1024]{1,0:T(8,128)(2,1)S(1)}, u32[]{:S(2)}, u32[]{:S(2)}) collective-permute-start(bf16[64,1024]{1,0:T(8,128)(2,1)S(1)} %get-tuple-element.142), channel_id=1, source_target_pairs={{16,20},{24,28},{17,21},{25,29},{18,22},{26,30},{19,23},{27,31}} | collective-permute-start | bytes 393224 | tf_op jit(solution)/shard_map/ppermute | solution.py:342
  42.1 3.6 %collective-permute-start.23 = (bf16[64,1024]{1,0:T(8,128)(2,1)S(1)}, bf16[64,1024]{1,0:T(8,128)(2,1)S(1)}, u32[]{:S(2)}, u32[]{:S(2)}) collective-permute-start(bf16[64,1024]{1,0:T(8,128)(2,1)S(1)} %get-tuple-element.141), channel_id=1, source_target_pairs={{12,16},{20,24},{13,17},{21,25},{14,18},{22,26},{15,19},{23,27}} | collective-permute-start | bytes 393224 | tf_op jit(solution)/shard_map/ppermute | solution.py:342
  42.9 3.8 %collective-permute-start.32 = (bf16[64,1024]{1,0:T(8,128)(2,1)S(1)}, bf16[64,1024]{1,0:T(8,128)(2,1)S(1)}, u32[]{:S(2)}, u32[]{:S(2)}) collective-permute-start(bf16[64,1024]{1,0:T(8,128)(2,1)S(1)} %get-tuple-element.155), channel_id=1, source_target_pairs={{16,20},{24,28},{17,21},{25,29},{18,22},{26,30},{19,23},{27,31}} | collective-permute-start | bytes 393224 | tf_op jit(solution)/shard_map/ppermute | solution.py:342
  43.6 3.8 %collective-permute-start.31 = (bf16[64,1024]{1,0:T(8,128)(2,1)S(1)}, bf16[64,1024]{1,0:T(8,128)(2,1)S(1)}, u32[]{:S(2)}, u32[]{:S(2)}) collective-permute-start(bf16[64,1024]{1,0:T(8,128)(2,1)S(1)} %get-tuple-element.154), channel_id=1, source_target_pairs={{20,24},{21,25},{22,26},{23,27}} | collective-permute-start | bytes 393224 | tf_op jit(solution)/shard_map/ppermute | solution.py:342
  44.3 3.8 %collective-permute-start.30 = (bf16[64,1024]{1,0:T(8,128)(2,1)S(1)}, bf16[64,1024]{1,0:T(8,128)(2,1)S(1)}, u32[]{:S(2)}, u32[]{:S(2)}) collective-permute-start(bf16[64,1024]{1,0:T(8,128)(2,1)S(1)} %get-tuple-element.153), channel_id=1, source_target_pairs={{16,20},{24,28},{17,21},{25,29},{18,22},{26,30},{19,23},{27,31}} | collective-permute-start | bytes 393224 | tf_op jit(solution)/shard_map/ppermute | solution.py:342
  45.0 3.8 %collective-permute-start.29 = (bf16[64,1024]{1,0:T(8,128)(2,1)S(1)}, bf16[64,1024]{1,0:T(8,128)(2,1)S(1)}, u32[]{:S(2)}, u32[]{:S(2)}) collective-permute-start(bf16[64,1024]{1,0:T(8,128)(2,1)S(1)} %get-tuple-element.152), channel_id=1, source_target_pairs={{20,24},{21,25},{22,26},{23,27}} | collective-permute-start | bytes 393224 | tf_op jit(solution)/shard_map/ppermute | solution.py:342
  46.0 3.6 %collective-permute-start.28 = (bf16[64,1024]{1,0:T(8,128)(2,1)S(1)}, bf16[64,1024]{1,0:T(8,128)(2,1)S(1)}, u32[]{:S(2)}, u32[]{:S(2)}) collective-permute-start(bf16[64,1024]{1,0:T(8,128)(2,1)S(1)} %get-tuple-element.151), channel_id=1, source_target_pairs={{16,20},{24,28},{17,21},{25,29},{18,22},{26,30},{19,23},{27,31}} | collective-permute-start | bytes 393224 | tf_op jit(solution)/shard_map/ppermute | solution.py:342
  46.7 4.3 %collective-permute-start.37 = (bf16[64,1024]{1,0:T(8,128)(2,1)S(1)}, bf16[64,1024]{1,0:T(8,128)(2,1)S(1)}, u32[]{:S(2)}, u32[]{:S(2)}) collective-permute-start(bf16[64,1024]{1,0:T(8,128)(2,1)S(1)} %get-tuple-element.165), channel_id=1, source_target_pairs={{20,24},{21,25},{22,26},{23,27}} | collective-permute-start | bytes 393224 | tf_op jit(solution)/shard_map/ppermute | solution.py:342
  47.4 6.3 %collective-permute-start.36 = (bf16[64,1024]{1,0:T(8,128)(2,1)S(1)}, bf16[64,1024]{1,0:T(8,128)(2,1)S(1)}, u32[]{:S(2)}, u32[]{:S(2)}) collective-permute-start(bf16[64,1024]{1,0:T(8,128)(2,1)S(1)} %get-tuple-element.164), channel_id=1, source_target_pairs={{24,28},{25,29},{26,30},{27,31}} | collective-permute-start | bytes 393224 | tf_op jit(solution)/shard_map/ppermute | solution.py:342
  48.2 6.3 %collective-permute-start.35 = (bf16[64,1024]{1,0:T(8,128)(2,1)S(1)}, bf16[64,1024]{1,0:T(8,128)(2,1)S(1)}, u32[]{:S(2)}, u32[]{:S(2)}) collective-permute-start(bf16[64,1024]{1,0:T(8,128)(2,1)S(1)} %get-tuple-element.163), channel_id=1, source_target_pairs={{20,24},{21,25},{22,26},{23,27}} | collective-permute-start | bytes 393224 | tf_op jit(solution)/shard_map/ppermute | solution.py:342
  48.9 6.3 %collective-permute-start.34 = (bf16[64,1024]{1,0:T(8,128)(2,1)S(1)}, bf16[64,1024]{1,0:T(8,128)(2,1)S(1)}, u32[]{:S(2)}, u32[]{:S(2)}) collective-permute-start(bf16[64,1024]{1,0:T(8,128)(2,1)S(1)} %get-tuple-element.162), channel_id=1, source_target_pairs={{24,28},{25,29},{26,30},{27,31}} | collective-permute-start | bytes 393224 | tf_op jit(solution)/shard_map/ppermute | solution.py:342
  49.6 5.6 %collective-permute-start.33 = (bf16[64,1024]{1,0:T(8,128)(2,1)S(1)}, bf16[64,1024]{1,0:T(8,128)(2,1)S(1)}, u32[]{:S(2)}, u32[]{:S(2)}) collective-permute-start(bf16[64,1024]{1,0:T(8,128)(2,1)S(1)} %get-tuple-element.161), channel_id=1, source_target_pairs={{20,24},{21,25},{22,26},{23,27}} | collective-permute-start | bytes 393224 | tf_op jit(solution)/shard_map/ppermute | solution.py:342
  51.0 15.9 %collective-permute-start.41 = (bf16[112,1536]{1,0:T(8,128)(2,1)S(1)}, bf16[112,1536]{1,0:T(8,128)(2,1)S(1)}, u32[]{:S(2)}, u32[]{:S(2)}) collective-permute-start(bf16[112,1536]{1,0:T(8,128)(2,1)S(1)} %shard_map.102), channel_id=1, source_target_pairs={{0,2},{1,3},{2,0},{3,1},{4,6},{5,7},{6,4},{7,5},{8,10},{9,11},{10,... | collective-permute-start | bytes 1032200 | tf_op jit(solution)/shard_map/ppermute | solution.py:348
  53.7 2.4 %collective-permute-start.40 = (bf16[64,1024]{1,0:T(8,128)(2,1)S(1)}, bf16[64,1024]{1,0:T(8,128)(2,1)S(1)}, u32[]{:S(2)}, u32[]{:S(2)}) collective-permute-start(bf16[64,1024]{1,0:T(8,128)(2,1)S(1)} %get-tuple-element.173), channel_id=1, source_target_pairs={{24,28},{25,29},{26,30},{27,31}} | collective-permute-start | bytes 393224 | tf_op jit(solution)/shard_map/ppermute | solution.py:342
  54.5 1.6 %collective-permute-start.39 = (bf16[64,1024]{1,0:T(8,128)(2,1)S(1)}, bf16[64,1024]{1,0:T(8,128)(2,1)S(1)}, u32[]{:S(2)}, u32[]{:S(2)}) collective-permute-start(bf16[64,1024]{1,0:T(8,128)(2,1)S(1)} %get-tuple-element.172), channel_id=1, source_target_pairs={{24,28},{25,29},{26,30},{27,31}} | collective-permute-start | bytes 393224 | tf_op jit(solution)/shard_map/ppermute | solution.py:342
  55.3 3.5 %collective-permute-start.38 = (bf16[64,1024]{1,0:T(8,128)(2,1)S(1)}, bf16[64,1024]{1,0:T(8,128)(2,1)S(1)}, u32[]{:S(2)}, u32[]{:S(2)}) collective-permute-start(bf16[64,1024]{1,0:T(8,128)(2,1)S(1)} %get-tuple-element.171), channel_id=1, source_target_pairs={{24,28},{25,29},{26,30},{27,31}} | collective-permute-start | bytes 393224 | tf_op jit(solution)/shard_map/ppermute | solution.py:342
  56.0 11.0 %collective-permute-start.42 = (bf16[64,1536]{1,0:T(8,128)(2,1)S(1)}, bf16[64,1536]{1,0:T(8,128)(2,1)S(1)}, u32[]{:S(2)}, u32[]{:S(2)}) collective-permute-start(bf16[64,1536]{1,0:T(8,128)(2,1)S(1)} %shard_map.107), channel_id=1, source_target_pairs={{0,2},{1,3},{2,0},{3,1},{4,6},{5,7},{6,4},{7,5},{8,10},{9,11},{10,... | collective-permute-start | bytes 589832 | tf_op jit(solution)/shard_map/ppermute | solution.py:348
  56.8 14.0 %collective-permute-start.43 = (bf16[64,1536]{1,0:T(8,128)(2,1)}, bf16[64,1536]{1,0:T(8,128)(2,1)S(1)}, u32[]{:S(2)}, u32[]{:S(2)}) collective-permute-start(bf16[64,1536]{1,0:T(8,128)(2,1)} %shard_map.111), channel_id=1, source_target_pairs={{0,2},{1,3},{2,0},{3,1},{4,6},{5,7},{6,4},{7,5},{8,10},{9,11},{10,... | collective-permute-start | bytes 589832 | tf_op jit(solution)/shard_map/ppermute | solution.py:348
  58.8 47.5 %copy-start.4 = (s32[1024,256]{1,0:T(8,128)S(1)}, s32[1024,256]{1,0:T(8,128)}, u32[]{:S(2)}) copy-start(s32[1024,256]{1,0:T(8,128)} %lag_ref.1) | copy-start | bytes 3145732
  59.4 11.4 %collective-permute-start.44 = (bf16[32,1536]{1,0:T(8,128)(2,1)}, bf16[32,1536]{1,0:T(8,128)(2,1)S(1)}, u32[]{:S(2)}, u32[]{:S(2)}) collective-permute-start(bf16[32,1536]{1,0:T(8,128)(2,1)} %shard_map.113), channel_id=1, source_target_pairs={{0,2},{1,3},{2,0},{3,1},{4,6},{5,7},{6,4},{7,5},{8,10},{9,11},{10,... | collective-permute-start | bytes 294920 | tf_op jit(solution)/shard_map/ppermute | solution.py:348
  71.6 2.0 %collective-permute-start.45 = (bf16[256,1024]{1,0:T(8,128)(2,1)S(1)}, bf16[256,1024]{1,0:T(8,128)(2,1)S(1)}, u32[]{:S(2)}, u32[]{:S(2)}) collective-permute-start(bf16[256,1024]{1,0:T(8,128)(2,1)S(1)} %broadcast_select_fusion), channel_id=1, source_target_pairs={{0,1},{1,0},{2,3},{3,2},{4,5},{5,4},{6,7},{7,6},{8,9},{9,8},{10,11... | collective-permute-start | bytes 1572872 | tf_op jit(solution)/shard_map/ppermute | solution.py:360
  (5 other events, 23.5 us)

commit v5 on v4

--- a/solution.py
+++ b/solution.py
@@ -11,6 +11,7 @@
 GROUPS = (3, 2, 2, 1)
 LAGS = (3, 2)
 EARLY = LAGS[1]
+SLICES = 2
 
 WHOLE = pl.BlockSpec(memory_space=pltpu.VMEM)
 FAR = pl.BlockSpec(memory_space=pltpu.HBM)
@@ -36,10 +37,14 @@
 
 
 def march(values, extrap_ref, out_refs):
+    real = jnp.dot(values, extrap_ref[0], preferred_element_type=jnp.float32)
+    imag = jnp.dot(values, extrap_ref[1], preferred_element_type=jnp.float32)
+    combine(real, imag, out_refs)
+
+
+def combine(real, imag, out_refs):
     rows = out_refs[0].shape[0]
     half = rows // 2
-    real = jnp.dot(values, extrap_ref[0], preferred_element_type=jnp.float32)
-    imag = jnp.dot(values, extrap_ref[1], preferred_element_type=jnp.float32)
     for chunk, out_ref in enumerate(out_refs):
         upper = slice(chunk * rows, chunk * rows + half)
         lower = slice(chunk * rows + half, (chunk + 1) * rows)
@@ -47,7 +52,7 @@
         out_ref[half:] = (imag[upper] + real[lower]).astype(out_ref.dtype)
 
 
-def extend(arrived, extrap, finished, round_index, parity, sends):
+def extend(arrived, extrap, finished, round_index, parity, sends, first=()):
     rows, points = arrived.shape
     chunk_count = finished.shape[0]
 
@@ -74,18 +79,20 @@
                 @pl.when(level == 0)
                 def _():
                     out_ref[...] = finished_ref[round_index]
+                    if first:
+                        finished_ref[round_index - EARLY] = refs[0][...]
 
     kept = jax.ShapeDtypeStruct(finished.shape, finished.dtype)
     sent = jax.ShapeDtypeStruct((rows, points), jnp.bfloat16)
     return pl.pallas_call(
         kernel,
         out_shape=[sent, kept] if sends else [kept],
-        in_specs=[WHOLE, WHOLE, WHOLE],
+        in_specs=[WHOLE] * (3 + len(first)),
         out_specs=[WHOLE, WHOLE] if sends else [WHOLE],
         input_output_aliases={2: 1 if sends else 0},
         compiler_params=pltpu.CompilerParams(vmem_limit_bytes=8 << 20),
         cost_estimate=BRIEF,
-    )(arrived, extrap, finished)
+    )(arrived, extrap, finished, *first)
 
 
 def pack(finished, number, start, stop, noted):
@@ -159,15 +166,26 @@
                 pltpu.make_async_copy(shot_hbm, shot_ref, sems.at[0]),
                 pltpu.make_async_copy(source_hbm, source_ref, sems.at[1]),
                 pltpu.make_async_copy(record_hbm.at[pl.ds(0, EARLY * part)], record_ref, sems.at[2]),
-                pltpu.make_async_copy(extrap_hbm, extrap_ref, sems.at[3]),
+            ]
+            bands = [pl.ds(index * points // SLICES, points // SLICES) for index in range(SLICES)]
+            copies += [
+                pltpu.make_async_copy(
+                    extrap_hbm.at[:, band], extrap_ref.at[:, band], sems.at[3 + index]
+                )
+                for index, band in enumerate(bands)
             ]
             for copy in copies:
                 copy.start()
             for copy in copies[:3]:
                 copy.wait()
             fill(chunk_ref, shot_ref, source_ref, record_ref, 0, part)
-            copies[3].wait()
-            march(chunk_ref[...], extrap_ref, out_refs)
+            real = imag = 0.0
+            for copy, band in zip(copies[3:], bands):
+                copy.wait()
+                values = chunk_ref[:, band]
+                real += jnp.dot(values, extrap_ref[0, band], preferred_element_type=jnp.float32)
+                imag += jnp.dot(values, extrap_ref[1, band], preferred_element_type=jnp.float32)
+            combine(real, imag, out_refs)
 
     return pl.pallas_call(
         kernel,
@@ -180,67 +198,78 @@
             pltpu.VMEM((EARLY * part,) + records.shape[1:], records.dtype),
             pltpu.VMEM(shots.shape, shots.dtype),
             pltpu.VMEM((EARLY * rows, points), jnp.bfloat16),
-            pltpu.SemaphoreType.DMA((4,)),
+            pltpu.SemaphoreType.DMA((3 + SLICES,)),
         ],
         compiler_params=pltpu.CompilerParams(vmem_limit_bytes=56 << 20),
     )(extrap, sources, records, shots)
 
 
-def rest(extrap, sources, records, shots, firsts, chunk_count):
+def rest(extrap, sources, records, shots, chunk_count):
     shot_count, _, points = sources.shape
     part = shot_count // chunk_count
     rows = 4 * part
 
-    def kernel(extrap_ref, source_ref, record_ref, shot_ref, *refs):
-        first_refs = refs[: len(firsts)]
-        finished_ref, chunk_ref = refs[len(firsts) :]
-
+    def kernel(extrap_ref, source_ref, record_ref, shot_ref, finished_ref, chunk_ref):
         @pl.when(lax.axis_index("depth") == 0)
         def _():
-            fill(chunk_ref, shot_ref, source_ref, record_ref, len(firsts), part)
-            others = [finished_ref.at[chunk] for chunk in range(len(firsts), chunk_count)]
+            fill(chunk_ref, shot_ref, source_ref, record_ref, EARLY, part)
+            others = [finished_ref.at[chunk] for chunk in range(EARLY, chunk_count)]
             march(chunk_ref[...], extrap_ref, others)
-            for chunk, first_ref in enumerate(first_refs):
-                finished_ref[chunk] = first_ref[...]
 
     return pl.pallas_call(
         kernel,
         out_shape=jax.ShapeDtypeStruct((chunk_count, rows, points), jnp.bfloat16),
-        in_specs=[WHOLE] * (4 + len(firsts)),
+        in_specs=[WHOLE] * 4,
         out_specs=WHOLE,
-        scratch_shapes=[pltpu.VMEM(((chunk_count - len(firsts)) * rows, points), jnp.bfloat16)],
+        scratch_shapes=[pltpu.VMEM(((chunk_count - EARLY) * rows, points), jnp.bfloat16)],
         compiler_params=pltpu.CompilerParams(vmem_limit_bytes=16 << 20),
         cost_estimate=BRIEF,
-    )(extrap, sources, records, shots, *firsts)
-
-
-def correlate(finished, theirs, own_scale, unit, part):
-    points = finished.shape[2]
-    chunk_count = finished.shape[0]
+    )(extrap, sources, records, shots)
+
+
+def outer(source, record):
+    return lax.dot_general(
+        source, record, (((0,), (0,)), ((), ())), preferred_element_type=jnp.float32
+    )
+
+
+def correlate_own(finished, scale, part):
+    chunk_count, _, points = finished.shape
     width = points // 2
     depth = 2 * chunk_count * part
 
-    def kernel(finished_ref, *refs):
-        their_refs = refs[: len(theirs)]
-        scale_ref, out_ref, source_ref, record_ref = refs[len(theirs) :]
+    def kernel(finished_ref, scale_ref, out_ref, source_ref, record_ref):
         span = lax.axis_size("freq") // 2
         upper = (lax.axis_index("freq") // span) % 2
         column = pl.ds(pl.multiple_of(upper * width, width), width)
-
-        def product():
-            return lax.dot_general(
-                source_ref[...],
-                record_ref[...],
-                (((0,), (0,)), ((), ())),
-                preferred_element_type=jnp.float32,
-            )
-
         for chunk in range(chunk_count):
             for index, (first, second) in enumerate(((0, 3), (2, 1))):
                 row = pl.ds((2 * chunk + index) * part, part)
                 source_ref[row] = finished_ref[chunk, pl.ds(first * part, part), column]
                 record_ref[row] = finished_ref[chunk, pl.ds(second * part, part), :]
-        total = product() * scale_ref[...]
+        out_ref[...] = outer(source_ref[...], record_ref[...]) * scale_ref[...]
+
+    return pl.pallas_call(
+        kernel,
+        out_shape=jax.ShapeDtypeStruct((width, points), jnp.float32),
+        in_specs=[WHOLE] * 2,
+        out_specs=WHOLE,
+        scratch_shapes=[
+            pltpu.VMEM((depth, width), jnp.bfloat16),
+            pltpu.VMEM((depth, points), jnp.bfloat16),
+        ],
+        compiler_params=pltpu.CompilerParams(vmem_limit_bytes=12 << 20),
+        cost_estimate=BRIEF,
+    )(finished, scale)
+
+
+def correlate(own, theirs, unit, part):
+    width, points = own.shape
+    depth = 2 * sum(GROUPS) * part
+
+    def kernel(own_ref, *refs):
+        their_refs = refs[: len(theirs)]
+        out_ref, source_ref, record_ref = refs[len(theirs) :]
         start = 0
         for group, ref in zip(GROUPS, their_refs):
             count = 2 * group * part
@@ -249,20 +278,20 @@
             start += count
         count = 2 * GROUPS[0] * part
         number = their_refs[0][count : count + 16, :128].astype(jnp.float32)[:1, :1]
-        total += product() * (number * unit)
+        total = own_ref[...] + outer(source_ref[...], record_ref[...]) * (number * unit)
         out_ref[...] = total.astype(out_ref.dtype)
 
     return pl.pallas_call(
         kernel,
         out_shape=jax.ShapeDtypeStruct((width, points), jnp.bfloat16),
-        in_specs=[WHOLE] * (2 + len(theirs)),
+        in_specs=[WHOLE] * (1 + len(theirs)),
         out_specs=WHOLE,
         scratch_shapes=[
             pltpu.VMEM((depth, width), jnp.bfloat16),
             pltpu.VMEM((depth, points), jnp.bfloat16),
         ],
-        compiler_params=pltpu.CompilerParams(vmem_limit_bytes=24 << 20),
-    )(finished, *theirs, own_scale)
+        compiler_params=pltpu.CompilerParams(vmem_limit_bytes=12 << 20),
+    )(own, *theirs)
 
 
 def angles(panel, angle_lag, depth_count):
@@ -319,7 +348,8 @@
     round_count = first_round(depth_count - 1) + chunk_count
     for round_index in range(round_count):
         if round_index == EARLY:
-            finished = rest(operator, sources, records, shot_of_record, firsts, chunk_count)
+            shots, _ = lax.optimization_barrier((shot_of_record, firsts[0]))
+            finished = rest(operator, sources, records, shots, chunk_count)
         for parity in (0, 1):
             if not any(
                 handled(round_index, level, chunk_count)
@@ -334,8 +364,11 @@
                 order = firsts[round_index]
             else:
                 arrived = sent.get((1 - parity, round_index - LAGS[parity]), firsts[0])
+                first = ()
+                if parity == 0 and round_index < 2 * EARLY:
+                    first = (firsts[round_index - EARLY],)
                 *order, finished = extend(
-                    arrived, operator, finished, round_index, parity, bool(pairs)
+                    arrived, operator, finished, round_index, parity, bool(pairs), first
                 )
                 order = order[0] if pairs else None
             if pairs:
@@ -348,7 +381,8 @@
             theirs.append(lax.ppermute(payload, "freq", partner))
 
     scale = 1.0 / (8 * freq_count) / math.sqrt(shot_count * freq_count)
-    image = correlate(finished, theirs, number * scale, scale, part)
+    own = correlate_own(finished, number * scale, part)
+    image = correlate(own, theirs, scale, part)
     width = points // 2
     span //= 2
     while span:

time: 109 us -> 107 us (0.982)
  local copies, waits for them, and re-layouts: 1.82 us -> 0.03 us
    unnamed x14, local copies, waits for them, and re-layouts: 1.82 us -> 0.03 us
    pallas_call x4, Pallas kernels: 1.43 us -> 0.12 us  [pack(): pl.pallas_call(kernel, out_shape=jax.ShapeDtypeStruct((count + 16 * noted...]
where the time goes in v5:
time: 107 us; the launch traced here: 106 us
  starting transfers between devices  45.7 us (43%)
  blocking collectives  31.8 us (30%)
  waiting for transfers between devices  13.8 us (13%)
  Pallas kernels  12.8 us (12%)
  between operations  1.76 us (2%)
    ppermute x41, starting transfers between devices, shards(): sent[parity, round_index] = lax.ppermute(order, 'depth', pairs)  40.3 us
    all_to_all x1, blocking collectives, shards(): lax.all_to_all(image, 'depth', split_axis=0, concat_axis=0, tiled=True)  31.8 us
    ppermute x4, waiting for transfers between devices, shards(): theirs.append(lax.ppermute(payload, 'freq', partner))  11.8 us
    ppermute x4, starting transfers between devices, shards(): theirs.append(lax.ppermute(payload, 'freq', partner))  5.29 us
    pallas_call x1, Pallas kernels, head(): pl.pallas_call(kernel, out_shape=[jax.ShapeDtypeStruct((rows, points), jn...  4.52 us
    pallas_call x1, Pallas kernels, rest(): pl.pallas_call(kernel, out_shape=jax.ShapeDtypeStruct((chunk_count, rows,...  3.91 us
  transfers between devices with their start and end apart: 46, of which 3 were waited for; matrix products, arithmetic and copies ran while one was open for 0% of the time, Pallas kernels for 6%

profile of v5, /device:TPU:0, one launch (start us, length us, event | category | flops | bytes accessed | tf_op | source)
XLA Modules:
  0.0 106.2 jit_solution(7474984455050182098)
XLA Ops:
  0.0 4.5 %shard_map.64 = (bf16[64,1024]{1,0:T(8,128)(2,1)}, bf16[64,1024]{1,0:T(8,128)(2,1)}) custom-call(bf16[2,1024,1024]{2,1,0:T(8,128)(2,1)} %bitcast.6, bf16[128,2,1024]{2,1,0:T(2,128)(2,1)} %bitcast.53, bf16[128,2,1024]{2,1,0:T(2,128)(2,1)} %bitcast.55, s32[128]{0:T(128)} %shot_ref), custom_call_target="tpu_custom_call" | custom-call | tf_op jit(solution)/shard_map/pallas_call | solution.py:190
  4.6 1.4 %collective-permute-start.2 = (bf16[64,1024]{1,0:T(8,128)(2,1)}, bf16[64,1024]{1,0:T(8,128)(2,1)S(1)}, u32[]{:S(2)}, u32[]{:S(2)}) collective-permute-start(bf16[64,1024]{1,0:T(8,128)(2,1)} %get-tuple-element.94.arrived_ref.refs_0_), channel_id=1, source_target_pairs={{0,4},{1,5},{2,6},{3,7}} | collective-permute-start | bytes 393224 | tf_op jit(solution)/shard_map/ppermute | solution.py:375
  6.0 1.3 %collective-permute-start.1 = (bf16[64,1024]{1,0:T(8,128)(2,1)}, bf16[64,1024]{1,0:T(8,128)(2,1)S(1)}, u32[]{:S(2)}, u32[]{:S(2)}) collective-permute-start(bf16[64,1024]{1,0:T(8,128)(2,1)} %get-tuple-element.97.refs_0_), channel_id=1, source_target_pairs={{0,4},{1,5},{2,6},{3,7}} | collective-permute-start | bytes 393224 | tf_op jit(solution)/shard_map/ppermute | solution.py:375
  7.3 3.9 %shard_map.65.finished_in = bf16[8,64,1024]{2,1,0:T(8,128)(2,1)S(1)} custom-call(bf16[2,1024,1024]{2,1,0:T(8,128)(2,1)S(1)} %bitcast.7, bf16[128,2,1024]{2,1,0:T(2,128)(2,1)S(1)} %bitcast.54, bf16[128,2,1024]{2,1,0:T(2,128)(2,1)S(1)} %bitcast.56, s32[128]{0:T(128)S(1)} %copy-done.6), custom_call_target="tpu_custom_call" | custom-call | tf_op jit(solution)/shard_map/pallas_call | solution.py:219
  11.3 1.3 %collective-permute-start = (bf16[64,1024]{1,0:T(8,128)(2,1)S(1)}, bf16[64,1024]{1,0:T(8,128)(2,1)S(1)}, u32[]{:S(2)}, u32[]{:S(2)}) collective-permute-start(bf16[64,1024]{1,0:T(8,128)(2,1)S(1)} %get-tuple-element.96), channel_id=1, source_target_pairs={{0,4},{1,5},{2,6},{3,7}} | collective-permute-start | bytes 393224 | tf_op jit(solution)/shard_map/ppermute | solution.py:375
  12.7 0.7 collective-permute-start.7
  13.4 3.2 %collective-permute-start.6 = (bf16[64,1024]{1,0:T(8,128)(2,1)S(1)}, bf16[64,1024]{1,0:T(8,128)(2,1)S(1)}, u32[]{:S(2)}, u32[]{:S(2)}) collective-permute-start(bf16[64,1024]{1,0:T(8,128)(2,1)S(1)} %get-tuple-element.106), channel_id=1, source_target_pairs={{0,4},{1,5},{2,6},{3,7}} | collective-permute-start | bytes 393224 | tf_op jit(solution)/shard_map/ppermute | solution.py:375
  16.7 0.7 collective-permute-start.5
  17.4 2.8 %collective-permute-start.4 = (bf16[64,1024]{1,0:T(8,128)(2,1)S(1)}, bf16[64,1024]{1,0:T(8,128)(2,1)S(1)}, u32[]{:S(2)}, u32[]{:S(2)}) collective-permute-start(bf16[64,1024]{1,0:T(8,128)(2,1)S(1)} %get-tuple-element.104), channel_id=1, source_target_pairs={{0,4},{1,5},{2,6},{3,7}} | collective-permute-start | bytes 393224 | tf_op jit(solution)/shard_map/ppermute | solution.py:375
  20.2 0.7 collective-permute-start.3
  21.0 2.8 %collective-permute-start.12 = (bf16[64,1024]{1,0:T(8,128)(2,1)S(1)}, bf16[64,1024]{1,0:T(8,128)(2,1)S(1)}, u32[]{:S(2)}, u32[]{:S(2)}) collective-permute-start(bf16[64,1024]{1,0:T(8,128)(2,1)S(1)} %get-tuple-element.117), channel_id=1, source_target_pairs={{0,4},{8,12},{1,5},{9,13},{2,6},{10,14},{3,7},{11,15}} | collective-permute-start | bytes 393224 | tf_op jit(solution)/shard_map/ppermute | solution.py:375
  23.8 0.7 collective-permute-start.11
  24.5 2.8 %collective-permute-start.10 = (bf16[64,1024]{1,0:T(8,128)(2,1)S(1)}, bf16[64,1024]{1,0:T(8,128)(2,1)S(1)}, u32[]{:S(2)}, u32[]{:S(2)}) collective-permute-start(bf16[64,1024]{1,0:T(8,128)(2,1)S(1)} %get-tuple-element.115), channel_id=1, source_target_pairs={{0,4},{8,12},{1,5},{9,13},{2,6},{10,14},{3,7},{11,15}} | collective-permute-start | bytes 393224 | tf_op jit(solution)/shard_map/ppermute | solution.py:375
  27.3 0.7 collective-permute-start.9
  28.2 2.8 %collective-permute-start.8 = (bf16[64,1024]{1,0:T(8,128)(2,1)S(1)}, bf16[64,1024]{1,0:T(8,128)(2,1)S(1)}, u32[]{:S(2)}, u32[]{:S(2)}) collective-permute-start(bf16[64,1024]{1,0:T(8,128)(2,1)S(1)} %get-tuple-element.113), channel_id=1, source_target_pairs={{0,4},{8,12},{1,5},{9,13},{2,6},{10,14},{3,7},{11,15}} | collective-permute-start | bytes 393224 | tf_op jit(solution)/shard_map/ppermute | solution.py:375
  31.0 0.7 collective-permute-start.17
  31.8 0.7 collective-permute-start.16
  32.5 0.7 collective-permute-start.15
  33.2 0.7 collective-permute-start.14
  33.9 0.7 collective-permute-start.13
  34.7 0.7 collective-permute-start.22
  35.4 0.7 collective-permute-start.21
  36.1 0.7 collective-permute-start.20
  36.8 0.7 collective-permute-start.19
  37.6 0.7 collective-permute-start.18
  38.3 0.7 collective-permute-start.27
  39.0 0.7 collective-permute-start.26
  39.7 0.7 collective-permute-start.25
  40.4 0.7 collective-permute-start.24
  41.2 0.7 collective-permute-start.23
  41.9 0.7 collective-permute-start.32
  42.6 0.7 collective-permute-start.31
  43.3 0.7 collective-permute-start.30
  44.1 0.7 collective-permute-start.29
  45.0 0.7 collective-permute-start.28
  45.7 0.7 collective-permute-start.37
  46.5 0.7 collective-permute-start.36
  47.2 0.7 collective-permute-start.35
  47.9 0.7 collective-permute-start.34
  48.6 0.7 collective-permute-start.33
  50.0 3.0 %collective-permute-start.41 = (bf16[112,1536]{1,0:T(8,128)(2,1)S(1)}, bf16[112,1536]{1,0:T(8,128)(2,1)S(1)}, u32[]{:S(2)}, u32[]{:S(2)}) collective-permute-start(bf16[112,1536]{1,0:T(8,128)(2,1)S(1)} %shard_map.102), channel_id=1, source_target_pairs={{0,2},{1,3},{2,0},{3,1},{4,6},{5,7},{6,4},{7,5},{8,10},{9,11},{10,... | collective-permute-start | bytes 1032200 | tf_op jit(solution)/shard_map/ppermute | solution.py:381
  53.8 0.7 collective-permute-start.39
  55.5 2.0 %collective-permute-start.43 = (bf16[64,1536]{1,0:T(8,128)(2,1)S(1)}, bf16[64,1536]{1,0:T(8,128)(2,1)S(1)}, u32[]{:S(2)}, u32[]{:S(2)}) collective-permute-start(bf16[64,1536]{1,0:T(8,128)(2,1)S(1)} %shard_map.111), channel_id=1, source_target_pairs={{0,2},{1,3},{2,0},{3,1},{4,6},{5,7},{6,4},{7,5},{8,10},{9,11},{10,... | collective-permute-start | bytes 589832 | tf_op jit(solution)/shard_map/ppermute | solution.py:381
  58.1 8.1 %collective-permute-done.42.refs_1_ = bf16[64,1536]{1,0:T(8,128)(2,1)S(1)} collective-permute-done((bf16[64,1536]{1,0:T(8,128)(2,1)S(1)}, bf16[64,1536]{1,0:T(8,128)(2,1)S(1)}, u32[]{:S(2)}, u32[]{:S(2)}) %collective-permute-start.42) | collective-permute-done | bytes 196640 | tf_op jit(solution)/shard_map/ppermute | solution.py:381
  66.2 3.8 %collective-permute-done.44.refs_3_ = bf16[32,1536]{1,0:T(8,128)(2,1)S(1)} collective-permute-done((bf16[32,1536]{1,0:T(8,128)(2,1)S(1)}, bf16[32,1536]{1,0:T(8,128)(2,1)S(1)}, u32[]{:S(2)}, u32[]{:S(2)}) %collective-permute-start.44) | collective-permute-done | bytes 98336 | tf_op jit(solution)/shard_map/ppermute | solution.py:381
  70.6 1.9 %collective-permute-done.45 = bf16[256,1024]{1,0:T(8,128)(2,1)S(1)} collective-permute-done((bf16[256,1024]{1,0:T(8,128)(2,1)S(1)}, bf16[256,1024]{1,0:T(8,128)(2,1)S(1)}, u32[]{:S(2)}, u32[]{:S(2)}) %collective-permute-start.45) | collective-permute-done | bytes 524320 | tf_op jit(solution)/shard_map/ppermute | solution.py:394
  72.8 31.8 %all_to_all.11 = bf16[8,32,1024]{2,1,0:T(8,128)(2,1)S(1)} all-to-all(bf16[8,32,1024]{2,1,0:T(8,128)(2,1)S(1)} %bitcast.57), channel_id=1, replica_groups=mesh['depth'=8,'freq'=4] {'depth'}, dimensions={0} | all-to-all | bytes 1048576 | tf_op jit(solution)/shard_map/all_to_all | solution.py:397
  104.6 1.6 %shard_map.116 = f32[32,8,256]{2,1,0:T(8,128)} custom-call(bf16[256,1024]{1,0:T(8,128)(2,1)S(1)} %bitcast.52, s32[1024,256]{1,0:T(8,128)S(1)} %copy-done.4), custom_call_target="tpu_custom_call" | custom-call | tf_op jit(solution)/shard_map/pallas_call | solution.py:320
  (114 shorter events, 4.9 us)
Async XLA Ops:
  0.0 7.3 %copy-start.6 = (s32[128]{0:T(128)S(1)}, s32[128]{0:T(128)}, u32[]{:S(2)}) copy-start(s32[128]{0:T(128)} %shot_ref) | copy-start | bytes 1540
  4.6 8.1 %collective-permute-start.2 = (bf16[64,1024]{1,0:T(8,128)(2,1)}, bf16[64,1024]{1,0:T(8,128)(2,1)S(1)}, u32[]{:S(2)}, u32[]{:S(2)}) collective-permute-start(bf16[64,1024]{1,0:T(8,128)(2,1)} %get-tuple-element.94.arrived_ref.refs_0_), channel_id=1, source_target_pairs={{0,4},{1,5},{2,6},{3,7}} | collective-permute-start | bytes 393224 | tf_op jit(solution)/shard_map/ppermute | solution.py:375
  6.0 10.7 %collective-permute-start.1 = (bf16[64,1024]{1,0:T(8,128)(2,1)}, bf16[64,1024]{1,0:T(8,128)(2,1)S(1)}, u32[]{:S(2)}, u32[]{:S(2)}) collective-permute-start(bf16[64,1024]{1,0:T(8,128)(2,1)} %get-tuple-element.97.refs_0_), channel_id=1, source_target_pairs={{0,4},{1,5},{2,6},{3,7}} | collective-permute-start | bytes 393224 | tf_op jit(solution)/shard_map/ppermute | solution.py:375
  11.3 8.9 %collective-permute-start = (bf16[64,1024]{1,0:T(8,128)(2,1)S(1)}, bf16[64,1024]{1,0:T(8,128)(2,1)S(1)}, u32[]{:S(2)}, u32[]{:S(2)}) collective-permute-start(bf16[64,1024]{1,0:T(8,128)(2,1)S(1)} %get-tuple-element.96), channel_id=1, source_target_pairs={{0,4},{1,5},{2,6},{3,7}} | collective-permute-start | bytes 393224 | tf_op jit(solution)/shard_map/ppermute | solution.py:375
  12.7 8.2 %collective-permute-start.7 = (bf16[64,1024]{1,0:T(8,128)(2,1)S(1)}, bf16[64,1024]{1,0:T(8,128)(2,1)S(1)}, u32[]{:S(2)}, u32[]{:S(2)}) collective-permute-start(bf16[64,1024]{1,0:T(8,128)(2,1)S(1)} %get-tuple-element.107), channel_id=1, source_target_pairs={{4,8},{5,9},{6,10},{7,11}} | collective-permute-start | bytes 393224 | tf_op jit(solution)/shard_map/ppermute | solution.py:375
  13.4 10.3 %collective-permute-start.6 = (bf16[64,1024]{1,0:T(8,128)(2,1)S(1)}, bf16[64,1024]{1,0:T(8,128)(2,1)S(1)}, u32[]{:S(2)}, u32[]{:S(2)}) collective-permute-start(bf16[64,1024]{1,0:T(8,128)(2,1)S(1)} %get-tuple-element.106), channel_id=1, source_target_pairs={{0,4},{1,5},{2,6},{3,7}} | collective-permute-start | bytes 393224 | tf_op jit(solution)/shard_map/ppermute | solution.py:375
  16.7 7.8 %collective-permute-start.5 = (bf16[64,1024]{1,0:T(8,128)(2,1)S(1)}, bf16[64,1024]{1,0:T(8,128)(2,1)S(1)}, u32[]{:S(2)}, u32[]{:S(2)}) collective-permute-start(bf16[64,1024]{1,0:T(8,128)(2,1)S(1)} %get-tuple-element.105), channel_id=1, source_target_pairs={{4,8},{5,9},{6,10},{7,11}} | collective-permute-start | bytes 393224 | tf_op jit(solution)/shard_map/ppermute | solution.py:375
  17.4 9.8 %collective-permute-start.4 = (bf16[64,1024]{1,0:T(8,128)(2,1)S(1)}, bf16[64,1024]{1,0:T(8,128)(2,1)S(1)}, u32[]{:S(2)}, u32[]{:S(2)}) collective-permute-start(bf16[64,1024]{1,0:T(8,128)(2,1)S(1)} %get-tuple-element.104), channel_id=1, source_target_pairs={{0,4},{1,5},{2,6},{3,7}} | collective-permute-start | bytes 393224 | tf_op jit(solution)/shard_map/ppermute | solution.py:375
  20.2 7.8 %collective-permute-start.3 = (bf16[64,1024]{1,0:T(8,128)(2,1)S(1)}, bf16[64,1024]{1,0:T(8,128)(2,1)S(1)}, u32[]{:S(2)}, u32[]{:S(2)}) collective-permute-start(bf16[64,1024]{1,0:T(8,128)(2,1)S(1)} %get-tuple-element.103), channel_id=1, source_target_pairs={{4,8},{5,9},{6,10},{7,11}} | collective-permute-start | bytes 393224 | tf_op jit(solution)/shard_map/ppermute | solution.py:375
  21.0 10.0 %collective-permute-start.12 = (bf16[64,1024]{1,0:T(8,128)(2,1)S(1)}, bf16[64,1024]{1,0:T(8,128)(2,1)S(1)}, u32[]{:S(2)}, u32[]{:S(2)}) collective-permute-start(bf16[64,1024]{1,0:T(8,128)(2,1)S(1)} %get-tuple-element.117), channel_id=1, source_target_pairs={{0,4},{8,12},{1,5},{9,13},{2,6},{10,14},{3,7},{11,15}} | collective-permute-start | bytes 393224 | tf_op jit(solution)/shard_map/ppermute | solution.py:375
  23.8 7.9 %collective-permute-start.11 = (bf16[64,1024]{1,0:T(8,128)(2,1)S(1)}, bf16[64,1024]{1,0:T(8,128)(2,1)S(1)}, u32[]{:S(2)}, u32[]{:S(2)}) collective-permute-start(bf16[64,1024]{1,0:T(8,128)(2,1)S(1)} %get-tuple-element.116), channel_id=1, source_target_pairs={{4,8},{5,9},{6,10},{7,11}} | collective-permute-start | bytes 393224 | tf_op jit(solution)/shard_map/ppermute | solution.py:375
  24.5 7.9 %collective-permute-start.10 = (bf16[64,1024]{1,0:T(8,128)(2,1)S(1)}, bf16[64,1024]{1,0:T(8,128)(2,1)S(1)}, u32[]{:S(2)}, u32[]{:S(2)}) collective-permute-start(bf16[64,1024]{1,0:T(8,128)(2,1)S(1)} %get-tuple-element.115), channel_id=1, source_target_pairs={{0,4},{8,12},{1,5},{9,13},{2,6},{10,14},{3,7},{11,15}} | collective-permute-start | bytes 393224 | tf_op jit(solution)/shard_map/ppermute | solution.py:375
  27.3 5.8 %collective-permute-start.9 = (bf16[64,1024]{1,0:T(8,128)(2,1)S(1)}, bf16[64,1024]{1,0:T(8,128)(2,1)S(1)}, u32[]{:S(2)}, u32[]{:S(2)}) collective-permute-start(bf16[64,1024]{1,0:T(8,128)(2,1)S(1)} %get-tuple-element.114), channel_id=1, source_target_pairs={{4,8},{5,9},{6,10},{7,11}} | collective-permute-start | bytes 393224 | tf_op jit(solution)/shard_map/ppermute | solution.py:375
  28.2 5.7 %collective-permute-start.8 = (bf16[64,1024]{1,0:T(8,128)(2,1)S(1)}, bf16[64,1024]{1,0:T(8,128)(2,1)S(1)}, u32[]{:S(2)}, u32[]{:S(2)}) collective-permute-start(bf16[64,1024]{1,0:T(8,128)(2,1)S(1)} %get-tuple-element.113), channel_id=1, source_target_pairs={{0,4},{8,12},{1,5},{9,13},{2,6},{10,14},{3,7},{11,15}} | collective-permute-start | bytes 393224 | tf_op jit(solution)/shard_map/ppermute | solution.py:375
  31.0 3.6 %collective-permute-start.17 = (bf16[64,1024]{1,0:T(8,128)(2,1)S(1)}, bf16[64,1024]{1,0:T(8,128)(2,1)S(1)}, u32[]{:S(2)}, u32[]{:S(2)}) collective-permute-start(bf16[64,1024]{1,0:T(8,128)(2,1)S(1)} %get-tuple-element.127), channel_id=1, source_target_pairs={{4,8},{12,16},{5,9},{13,17},{6,10},{14,18},{7,11},{15,19}} | collective-permute-start | bytes 393224 | tf_op jit(solution)/shard_map/ppermute | solution.py:375
  31.8 3.6 %collective-permute-start.16 = (bf16[64,1024]{1,0:T(8,128)(2,1)S(1)}, bf16[64,1024]{1,0:T(8,128)(2,1)S(1)}, u32[]{:S(2)}, u32[]{:S(2)}) collective-permute-start(bf16[64,1024]{1,0:T(8,128)(2,1)S(1)} %get-tuple-element.126), channel_id=1, source_target_pairs={{8,12},{16,20},{9,13},{17,21},{10,14},{18,22},{11,15},{19,23}} | collective-permute-start | bytes 393224 | tf_op jit(solution)/shard_map/ppermute | solution.py:375
  32.5 3.6 %collective-permute-start.15 = (bf16[64,1024]{1,0:T(8,128)(2,1)S(1)}, bf16[64,1024]{1,0:T(8,128)(2,1)S(1)}, u32[]{:S(2)}, u32[]{:S(2)}) collective-permute-start(bf16[64,1024]{1,0:T(8,128)(2,1)S(1)} %get-tuple-element.125), channel_id=1, source_target_pairs={{4,8},{12,16},{5,9},{13,17},{6,10},{14,18},{7,11},{15,19}} | collective-permute-start | bytes 393224 | tf_op jit(solution)/shard_map/ppermute | solution.py:375
  33.2 3.6 %collective-permute-start.14 = (bf16[64,1024]{1,0:T(8,128)(2,1)S(1)}, bf16[64,1024]{1,0:T(8,128)(2,1)S(1)}, u32[]{:S(2)}, u32[]{:S(2)}) collective-permute-start(bf16[64,1024]{1,0:T(8,128)(2,1)S(1)} %get-tuple-element.124), channel_id=1, source_target_pairs={{8,12},{16,20},{9,13},{17,21},{10,14},{18,22},{11,15},{19,23}} | collective-permute-start | bytes 393224 | tf_op jit(solution)/shard_map/ppermute | solution.py:375
  33.9 3.6 %collective-permute-start.13 = (bf16[64,1024]{1,0:T(8,128)(2,1)S(1)}, bf16[64,1024]{1,0:T(8,128)(2,1)S(1)}, u32[]{:S(2)}, u32[]{:S(2)}) collective-permute-start(bf16[64,1024]{1,0:T(8,128)(2,1)S(1)} %get-tuple-element.123), channel_id=1, source_target_pairs={{4,8},{12,16},{5,9},{13,17},{6,10},{14,18},{7,11},{15,19}} | collective-permute-start | bytes 393224 | tf_op jit(solution)/shard_map/ppermute | solution.py:375
  34.7 3.6 %collective-permute-start.22 = (bf16[64,1024]{1,0:T(8,128)(2,1)S(1)}, bf16[64,1024]{1,0:T(8,128)(2,1)S(1)}, u32[]{:S(2)}, u32[]{:S(2)}) collective-permute-start(bf16[64,1024]{1,0:T(8,128)(2,1)S(1)} %get-tuple-element.137), channel_id=1, source_target_pairs={{8,12},{16,20},{9,13},{17,21},{10,14},{18,22},{11,15},{19,23}} | collective-permute-start | bytes 393224 | tf_op jit(solution)/shard_map/ppermute | solution.py:375
  35.4 3.6 %collective-permute-start.21 = (bf16[64,1024]{1,0:T(8,128)(2,1)S(1)}, bf16[64,1024]{1,0:T(8,128)(2,1)S(1)}, u32[]{:S(2)}, u32[]{:S(2)}) collective-permute-start(bf16[64,1024]{1,0:T(8,128)(2,1)S(1)} %get-tuple-element.136), channel_id=1, source_target_pairs={{12,16},{20,24},{13,17},{21,25},{14,18},{22,26},{15,19},{23,27}} | collective-permute-start | bytes 393224 | tf_op jit(solution)/shard_map/ppermute | solution.py:375
  36.1 3.6 %collective-permute-start.20 = (bf16[64,1024]{1,0:T(8,128)(2,1)S(1)}, bf16[64,1024]{1,0:T(8,128)(2,1)S(1)}, u32[]{:S(2)}, u32[]{:S(2)}) collective-permute-start(bf16[64,1024]{1,0:T(8,128)(2,1)S(1)} %get-tuple-element.135), channel_id=1, source_target_pairs={{8,12},{16,20},{9,13},{17,21},{10,14},{18,22},{11,15},{19,23}} | collective-permute-start | bytes 393224 | tf_op jit(solution)/shard_map/ppermute | solution.py:375
  36.8 3.6 %collective-permute-start.19 = (bf16[64,1024]{1,0:T(8,128)(2,1)S(1)}, bf16[64,1024]{1,0:T(8,128)(2,1)S(1)}, u32[]{:S(2)}, u32[]{:S(2)}) collective-permute-start(bf16[64,1024]{1,0:T(8,128)(2,1)S(1)} %get-tuple-element.134), channel_id=1, source_target_pairs={{12,16},{20,24},{13,17},{21,25},{14,18},{22,26},{15,19},{23,27}} | collective-permute-start | bytes 393224 | tf_op jit(solution)/shard_map/ppermute | solution.py:375
  37.6 3.6 %collective-permute-start.18 = (bf16[64,1024]{1,0:T(8,128)(2,1)S(1)}, bf16[64,1024]{1,0:T(8,128)(2,1)S(1)}, u32[]{:S(2)}, u32[]{:S(2)}) collective-permute-start(bf16[64,1024]{1,0:T(8,128)(2,1)S(1)} %get-tuple-element.133), channel_id=1, source_target_pairs={{8,12},{16,20},{9,13},{17,21},{10,14},{18,22},{11,15},{19,23}} | collective-permute-start | bytes 393224 | tf_op jit(solution)/shard_map/ppermute | solution.py:375
  38.3 3.6 %collective-permute-start.27 = (bf16[64,1024]{1,0:T(8,128)(2,1)S(1)}, bf16[64,1024]{1,0:T(8,128)(2,1)S(1)}, u32[]{:S(2)}, u32[]{:S(2)}) collective-permute-start(bf16[64,1024]{1,0:T(8,128)(2,1)S(1)} %get-tuple-element.147), channel_id=1, source_target_pairs={{12,16},{20,24},{13,17},{21,25},{14,18},{22,26},{15,19},{23,27}} | collective-permute-start | bytes 393224 | tf_op jit(solution)/shard_map/ppermute | solution.py:375
  39.0 3.6 %collective-permute-start.26 = (bf16[64,1024]{1,0:T(8,128)(2,1)S(1)}, bf16[64,1024]{1,0:T(8,128)(2,1)S(1)}, u32[]{:S(2)}, u32[]{:S(2)}) collective-permute-start(bf16[64,1024]{1,0:T(8,128)(2,1)S(1)} %get-tuple-element.146), channel_id=1, source_target_pairs={{16,20},{24,28},{17,21},{25,29},{18,22},{26,30},{19,23},{27,31}} | collective-permute-start | bytes 393224 | tf_op jit(solution)/shard_map/ppermute | solution.py:375
  39.7 3.6 %collective-permute-start.25 = (bf16[64,1024]{1,0:T(8,128)(2,1)S(1)}, bf16[64,1024]{1,0:T(8,128)(2,1)S(1)}, u32[]{:S(2)}, u32[]{:S(2)}) collective-permute-start(bf16[64,1024]{1,0:T(8,128)(2,1)S(1)} %get-tuple-element.145), channel_id=1, source_target_pairs={{12,16},{20,24},{13,17},{21,25},{14,18},{22,26},{15,19},{23,27}} | collective-permute-start | bytes 393224 | tf_op jit(solution)/shard_map/ppermute | solution.py:375
  40.4 3.6 %collective-permute-start.24 = (bf16[64,1024]{1,0:T(8,128)(2,1)S(1)}, bf16[64,1024]{1,0:T(8,128)(2,1)S(1)}, u32[]{:S(2)}, u32[]{:S(2)}) collective-permute-start(bf16[64,1024]{1,0:T(8,128)(2,1)S(1)} %get-tuple-element.144), channel_id=1, source_target_pairs={{16,20},{24,28},{17,21},{25,29},{18,22},{26,30},{19,23},{27,31}} | collective-permute-start | bytes 393224 | tf_op jit(solution)/shard_map/ppermute | solution.py:375
  41.2 3.6 %collective-permute-start.23 = (bf16[64,1024]{1,0:T(8,128)(2,1)S(1)}, bf16[64,1024]{1,0:T(8,128)(2,1)S(1)}, u32[]{:S(2)}, u32[]{:S(2)}) collective-permute-start(bf16[64,1024]{1,0:T(8,128)(2,1)S(1)} %get-tuple-element.143), channel_id=1, source_target_pairs={{12,16},{20,24},{13,17},{21,25},{14,18},{22,26},{15,19},{23,27}} | collective-permute-start | bytes 393224 | tf_op jit(solution)/shard_map/ppermute | solution.py:375
  41.9 3.8 %collective-permute-start.32 = (bf16[64,1024]{1,0:T(8,128)(2,1)S(1)}, bf16[64,1024]{1,0:T(8,128)(2,1)S(1)}, u32[]{:S(2)}, u32[]{:S(2)}) collective-permute-start(bf16[64,1024]{1,0:T(8,128)(2,1)S(1)} %get-tuple-element.157), channel_id=1, source_target_pairs={{16,20},{24,28},{17,21},{25,29},{18,22},{26,30},{19,23},{27,31}} | collective-permute-start | bytes 393224 | tf_op jit(solution)/shard_map/ppermute | solution.py:375
  42.6 3.8 %collective-permute-start.31 = (bf16[64,1024]{1,0:T(8,128)(2,1)S(1)}, bf16[64,1024]{1,0:T(8,128)(2,1)S(1)}, u32[]{:S(2)}, u32[]{:S(2)}) collective-permute-start(bf16[64,1024]{1,0:T(8,128)(2,1)S(1)} %get-tuple-element.156), channel_id=1, source_target_pairs={{20,24},{21,25},{22,26},{23,27}} | collective-permute-start | bytes 393224 | tf_op jit(solution)/shard_map/ppermute | solution.py:375
  43.3 3.8 %collective-permute-start.30 = (bf16[64,1024]{1,0:T(8,128)(2,1)S(1)}, bf16[64,1024]{1,0:T(8,128)(2,1)S(1)}, u32[]{:S(2)}, u32[]{:S(2)}) collective-permute-start(bf16[64,1024]{1,0:T(8,128)(2,1)S(1)} %get-tuple-element.155), channel_id=1, source_target_pairs={{16,20},{24,28},{17,21},{25,29},{18,22},{26,30},{19,23},{27,31}} | collective-permute-start | bytes 393224 | tf_op jit(solution)/shard_map/ppermute | solution.py:375
  44.1 3.8 %collective-permute-start.29 = (bf16[64,1024]{1,0:T(8,128)(2,1)S(1)}, bf16[64,1024]{1,0:T(8,128)(2,1)S(1)}, u32[]{:S(2)}, u32[]{:S(2)}) collective-permute-start(bf16[64,1024]{1,0:T(8,128)(2,1)S(1)} %get-tuple-element.154), channel_id=1, source_target_pairs={{20,24},{21,25},{22,26},{23,27}} | collective-permute-start | bytes 393224 | tf_op jit(solution)/shard_map/ppermute | solution.py:375
  45.0 3.6 %collective-permute-start.28 = (bf16[64,1024]{1,0:T(8,128)(2,1)S(1)}, bf16[64,1024]{1,0:T(8,128)(2,1)S(1)}, u32[]{:S(2)}, u32[]{:S(2)}) collective-permute-start(bf16[64,1024]{1,0:T(8,128)(2,1)S(1)} %get-tuple-element.153), channel_id=1, source_target_pairs={{16,20},{24,28},{17,21},{25,29},{18,22},{26,30},{19,23},{27,31}} | collective-permute-start | bytes 393224 | tf_op jit(solution)/shard_map/ppermute | solution.py:375
  45.7 4.3 %collective-permute-start.37 = (bf16[64,1024]{1,0:T(8,128)(2,1)S(1)}, bf16[64,1024]{1,0:T(8,128)(2,1)S(1)}, u32[]{:S(2)}, u32[]{:S(2)}) collective-permute-start(bf16[64,1024]{1,0:T(8,128)(2,1)S(1)} %get-tuple-element.167), channel_id=1, source_target_pairs={{20,24},{21,25},{22,26},{23,27}} | collective-permute-start | bytes 393224 | tf_op jit(solution)/shard_map/ppermute | solution.py:375
  46.5 6.6 %collective-permute-start.36 = (bf16[64,1024]{1,0:T(8,128)(2,1)S(1)}, bf16[64,1024]{1,0:T(8,128)(2,1)S(1)}, u32[]{:S(2)}, u32[]{:S(2)}) collective-permute-start(bf16[64,1024]{1,0:T(8,128)(2,1)S(1)} %get-tuple-element.166), channel_id=1, source_target_pairs={{24,28},{25,29},{26,30},{27,31}} | collective-permute-start | bytes 393224 | tf_op jit(solution)/shard_map/ppermute | solution.py:375
  47.2 6.6 %collective-permute-start.35 = (bf16[64,1024]{1,0:T(8,128)(2,1)S(1)}, bf16[64,1024]{1,0:T(8,128)(2,1)S(1)}, u32[]{:S(2)}, u32[]{:S(2)}) collective-permute-start(bf16[64,1024]{1,0:T(8,128)(2,1)S(1)} %get-tuple-element.165), channel_id=1, source_target_pairs={{20,24},{21,25},{22,26},{23,27}} | collective-permute-start | bytes 393224 | tf_op jit(solution)/shard_map/ppermute | solution.py:375
  47.9 6.6 %collective-permute-start.34 = (bf16[64,1024]{1,0:T(8,128)(2,1)S(1)}, bf16[64,1024]{1,0:T(8,128)(2,1)S(1)}, u32[]{:S(2)}, u32[]{:S(2)}) collective-permute-start(bf16[64,1024]{1,0:T(8,128)(2,1)S(1)} %get-tuple-element.164), channel_id=1, source_target_pairs={{24,28},{25,29},{26,30},{27,31}} | collective-permute-start | bytes 393224 | tf_op jit(solution)/shard_map/ppermute | solution.py:375
  48.6 5.9 %collective-permute-start.33 = (bf16[64,1024]{1,0:T(8,128)(2,1)S(1)}, bf16[64,1024]{1,0:T(8,128)(2,1)S(1)}, u32[]{:S(2)}, u32[]{:S(2)}) collective-permute-start(bf16[64,1024]{1,0:T(8,128)(2,1)S(1)} %get-tuple-element.163), channel_id=1, source_target_pairs={{20,24},{21,25},{22,26},{23,27}} | collective-permute-start | bytes 393224 | tf_op jit(solution)/shard_map/ppermute | solution.py:375
  50.0 16.2 %collective-permute-start.41 = (bf16[112,1536]{1,0:T(8,128)(2,1)S(1)}, bf16[112,1536]{1,0:T(8,128)(2,1)S(1)}, u32[]{:S(2)}, u32[]{:S(2)}) collective-permute-start(bf16[112,1536]{1,0:T(8,128)(2,1)S(1)} %shard_map.102), channel_id=1, source_target_pairs={{0,2},{1,3},{2,0},{3,1},{4,6},{5,7},{6,4},{7,5},{8,10},{9,11},{10,... | collective-permute-start | bytes 1032200 | tf_op jit(solution)/shard_map/ppermute | solution.py:381
  53.0 2.4 %collective-permute-start.40 = (bf16[64,1024]{1,0:T(8,128)(2,1)S(1)}, bf16[64,1024]{1,0:T(8,128)(2,1)S(1)}, u32[]{:S(2)}, u32[]{:S(2)}) collective-permute-start(bf16[64,1024]{1,0:T(8,128)(2,1)S(1)} %get-tuple-element.175), channel_id=1, source_target_pairs={{24,28},{25,29},{26,30},{27,31}} | collective-permute-start | bytes 393224 | tf_op jit(solution)/shard_map/ppermute | solution.py:375
  53.8 1.6 %collective-permute-start.39 = (bf16[64,1024]{1,0:T(8,128)(2,1)S(1)}, bf16[64,1024]{1,0:T(8,128)(2,1)S(1)}, u32[]{:S(2)}, u32[]{:S(2)}) collective-permute-start(bf16[64,1024]{1,0:T(8,128)(2,1)S(1)} %get-tuple-element.174), channel_id=1, source_target_pairs={{24,28},{25,29},{26,30},{27,31}} | collective-permute-start | bytes 393224 | tf_op jit(solution)/shard_map/ppermute | solution.py:375
  54.6 2.9 %collective-permute-start.38 = (bf16[64,1024]{1,0:T(8,128)(2,1)S(1)}, bf16[64,1024]{1,0:T(8,128)(2,1)S(1)}, u32[]{:S(2)}, u32[]{:S(2)}) collective-permute-start(bf16[64,1024]{1,0:T(8,128)(2,1)S(1)} %get-tuple-element.173), channel_id=1, source_target_pairs={{24,28},{25,29},{26,30},{27,31}} | collective-permute-start | bytes 393224 | tf_op jit(solution)/shard_map/ppermute | solution.py:375
  55.2 11.0 %collective-permute-start.42 = (bf16[64,1536]{1,0:T(8,128)(2,1)S(1)}, bf16[64,1536]{1,0:T(8,128)(2,1)S(1)}, u32[]{:S(2)}, u32[]{:S(2)}) collective-permute-start(bf16[64,1536]{1,0:T(8,128)(2,1)S(1)} %shard_map.107), channel_id=1, source_target_pairs={{0,2},{1,3},{2,0},{3,1},{4,6},{5,7},{6,4},{7,5},{8,10},{9,11},{10,... | collective-permute-start | bytes 589832 | tf_op jit(solution)/shard_map/ppermute | solution.py:381
  55.5 14.5 %collective-permute-start.43 = (bf16[64,1536]{1,0:T(8,128)(2,1)S(1)}, bf16[64,1536]{1,0:T(8,128)(2,1)S(1)}, u32[]{:S(2)}, u32[]{:S(2)}) collective-permute-start(bf16[64,1536]{1,0:T(8,128)(2,1)S(1)} %shard_map.111), channel_id=1, source_target_pairs={{0,2},{1,3},{2,0},{3,1},{4,6},{5,7},{6,4},{7,5},{8,10},{9,11},{10,... | collective-permute-start | bytes 589832 | tf_op jit(solution)/shard_map/ppermute | solution.py:381
  57.5 12.5 %collective-permute-start.44 = (bf16[32,1536]{1,0:T(8,128)(2,1)S(1)}, bf16[32,1536]{1,0:T(8,128)(2,1)S(1)}, u32[]{:S(2)}, u32[]{:S(2)}) collective-permute-start(bf16[32,1536]{1,0:T(8,128)(2,1)S(1)} %shard_map.113), channel_id=1, source_target_pairs={{0,2},{1,3},{2,0},{3,1},{4,6},{5,7},{6,4},{7,5},{8,10},{9,11},{10,... | collective-permute-start | bytes 294920 | tf_op jit(solution)/shard_map/ppermute | solution.py:381
  58.1 46.4 %copy-start.4 = (s32[1024,256]{1,0:T(8,128)S(1)}, s32[1024,256]{1,0:T(8,128)}, u32[]{:S(2)}) copy-start(s32[1024,256]{1,0:T(8,128)} %lag_ref.1) | copy-start | bytes 3145732
  70.5 2.0 %collective-permute-start.45 = (bf16[256,1024]{1,0:T(8,128)(2,1)S(1)}, bf16[256,1024]{1,0:T(8,128)(2,1)S(1)}, u32[]{:S(2)}, u32[]{:S(2)}) collective-permute-start(bf16[256,1024]{1,0:T(8,128)(2,1)S(1)} %broadcast_select_fusion), channel_id=1, source_target_pairs={{0,1},{1,0},{2,3},{3,2},{4,5},{5,4},{6,7},{7,6},{8,9},{9,8},{10,11... | collective-permute-start | bytes 1572872 | tf_op jit(solution)/shard_map/ppermute | solution.py:394
  (5 other events, 30.7 us)

commit v6 on v5

--- a/solution.py
+++ b/solution.py
@@ -128,8 +128,9 @@
 def fill(out_ref, shot_ref, source_ref, record_ref, first, part):
     shot_count = source_ref.shape[0]
     chunk_count = out_ref.shape[0] // (4 * part)
+    count = shot_count if first else chunk_count * part
     pick = (
-        shot_ref[...][None, :] == lax.broadcasted_iota(jnp.int32, (shot_count, shot_count), 0)
+        shot_ref[:count][None, :] == lax.broadcasted_iota(jnp.int32, (shot_count, count), 0)
     ).astype(jnp.bfloat16)
 
     def picked(component):
@@ -263,22 +264,26 @@
     )(finished, scale)
 
 
-def correlate(own, theirs, unit, part):
+def correlate(own, theirs, unit, part, away):
     width, points = own.shape
+    width //= 2
     depth = 2 * sum(GROUPS) * part
 
     def kernel(own_ref, *refs):
         their_refs = refs[: len(theirs)]
         out_ref, source_ref, record_ref = refs[len(theirs) :]
+        upper = (lax.axis_index("freq") // (lax.axis_size("freq") // 4)) % 2
+        place = pl.multiple_of((1 - upper if away else upper) * width, width)
+        column = pl.ds(pl.multiple_of(points + place, width), width)
         start = 0
         for group, ref in zip(GROUPS, their_refs):
             count = 2 * group * part
-            source_ref[start : start + count] = ref[:count, points:]
+            source_ref[start : start + count] = ref[pl.ds(0, count), column]
             record_ref[start : start + count] = ref[:count, :points]
             start += count
         count = 2 * GROUPS[0] * part
         number = their_refs[0][count : count + 16, :128].astype(jnp.float32)[:1, :1]
-        total = own_ref[...] + outer(source_ref[...], record_ref[...]) * (number * unit)
+        total = own_ref[pl.ds(place, width)] + outer(source_ref[...], record_ref[...]) * (number * unit)
         out_ref[...] = total.astype(out_ref.dtype)
 
     return pl.pallas_call(
@@ -382,8 +387,12 @@
 
     scale = 1.0 / (8 * freq_count) / math.sqrt(shot_count * freq_count)
     own = correlate_own(finished, number * scale, part)
-    image = correlate(own, theirs, scale, part)
-    width = points // 2
+    away, keep = (correlate(own, theirs, scale, part, side) for side in (True, False))
+    width = points // 4
+    span //= 2
+    partner = [(slot, slot ^ span) for slot in range(freq_count)]
+    received = lax.ppermute(away, "freq", partner)
+    image = (keep.astype(jnp.float32) + received.astype(jnp.float32)).astype(jnp.bfloat16)
     span //= 2
     while span:
         width //= 2

time: 107 us -> 106 us (level)
  no operation moved by 1% of the time
where the time goes in v6:
time: 106 us
  starting transfers between devices  45.7 us (43%)
  blocking collectives  31.8 us (30%)
  waiting for transfers between devices  13.5 us (13%)
  Pallas kernels  12.9 us (12%)
  between operations  1.75 us (2%)
    ppermute x41, starting transfers between devices, shards(): sent[parity, round_index] = lax.ppermute(order, 'depth', pairs)  40.3 us
    all_to_all x1, blocking collectives, shards(): lax.all_to_all(image, 'depth', split_axis=0, concat_axis=0, tiled=True)  31.8 us
    ppermute x4, waiting for transfers between devices, shards(): theirs.append(lax.ppermute(payload, 'freq', partner))  11.8 us
    ppermute x4, starting transfers between devices, shards(): theirs.append(lax.ppermute(payload, 'freq', partner))  5.27 us
    pallas_call x1, Pallas kernels, head(): pl.pallas_call(kernel, out_shape=[jax.ShapeDtypeStruct((rows, points), jn...  4.46 us
    pallas_call x1, Pallas kernels, rest(): pl.pallas_call(kernel, out_shape=jax.ShapeDtypeStruct((chunk_count, rows,...  3.91 us
  transfers between devices with their start and end apart: 46, of which 3 were waited for; matrix products, arithmetic and copies ran while one was open for 0% of the time, Pallas kernels for 6%

profile of v6, /device:TPU:0, one launch (start us, length us, event | category | flops | bytes accessed | tf_op | source)
XLA Modules:
  0.0 105.8 jit_solution(75069222342264099)
XLA Ops:
  0.0 4.5 %shard_map.64 = (bf16[64,1024]{1,0:T(8,128)(2,1)}, bf16[64,1024]{1,0:T(8,128)(2,1)}) custom-call(bf16[2,1024,1024]{2,1,0:T(8,128)(2,1)} %bitcast.6, bf16[128,2,1024]{2,1,0:T(2,128)(2,1)} %bitcast.53, bf16[128,2,1024]{2,1,0:T(2,128)(2,1)} %bitcast.55, s32[128]{0:T(128)} %shot_ref), custom_call_target="tpu_custom_call" | custom-call | tf_op jit(solution)/shard_map/pallas_call | solution.py:191
  4.5 1.4 %collective-permute-start.2 = (bf16[64,1024]{1,0:T(8,128)(2,1)}, bf16[64,1024]{1,0:T(8,128)(2,1)S(1)}, u32[]{:S(2)}, u32[]{:S(2)}) collective-permute-start(bf16[64,1024]{1,0:T(8,128)(2,1)} %get-tuple-element.94.arrived_ref.refs_0_), channel_id=1, source_target_pairs={{0,4},{1,5},{2,6},{3,7}} | collective-permute-start | bytes 393224 | tf_op jit(solution)/shard_map/ppermute | solution.py:380
  5.9 1.3 %collective-permute-start.1 = (bf16[64,1024]{1,0:T(8,128)(2,1)}, bf16[64,1024]{1,0:T(8,128)(2,1)S(1)}, u32[]{:S(2)}, u32[]{:S(2)}) collective-permute-start(bf16[64,1024]{1,0:T(8,128)(2,1)} %get-tuple-element.97.refs_0_), channel_id=1, source_target_pairs={{0,4},{1,5},{2,6},{3,7}} | collective-permute-start | bytes 393224 | tf_op jit(solution)/shard_map/ppermute | solution.py:380
  7.3 3.9 %shard_map.65.finished_in = bf16[8,64,1024]{2,1,0:T(8,128)(2,1)S(1)} custom-call(bf16[2,1024,1024]{2,1,0:T(8,128)(2,1)S(1)} %bitcast.7, bf16[128,2,1024]{2,1,0:T(2,128)(2,1)S(1)} %bitcast.54, bf16[128,2,1024]{2,1,0:T(2,128)(2,1)S(1)} %bitcast.56, s32[128]{0:T(128)S(1)} %copy-done.6), custom_call_target="tpu_custom_call" | custom-call | tf_op jit(solution)/shard_map/pallas_call | solution.py:220
  11.3 1.3 %collective-permute-start = (bf16[64,1024]{1,0:T(8,128)(2,1)S(1)}, bf16[64,1024]{1,0:T(8,128)(2,1)S(1)}, u32[]{:S(2)}, u32[]{:S(2)}) collective-permute-start(bf16[64,1024]{1,0:T(8,128)(2,1)S(1)} %get-tuple-element.96), channel_id=1, source_target_pairs={{0,4},{1,5},{2,6},{3,7}} | collective-permute-start | bytes 393224 | tf_op jit(solution)/shard_map/ppermute | solution.py:380
  12.6 0.7 collective-permute-start.7
  13.4 3.2 %collective-permute-start.6 = (bf16[64,1024]{1,0:T(8,128)(2,1)S(1)}, bf16[64,1024]{1,0:T(8,128)(2,1)S(1)}, u32[]{:S(2)}, u32[]{:S(2)}) collective-permute-start(bf16[64,1024]{1,0:T(8,128)(2,1)S(1)} %get-tuple-element.106), channel_id=1, source_target_pairs={{0,4},{1,5},{2,6},{3,7}} | collective-permute-start | bytes 393224 | tf_op jit(solution)/shard_map/ppermute | solution.py:380
  16.7 0.7 collective-permute-start.5
  17.4 2.8 %collective-permute-start.4 = (bf16[64,1024]{1,0:T(8,128)(2,1)S(1)}, bf16[64,1024]{1,0:T(8,128)(2,1)S(1)}, u32[]{:S(2)}, u32[]{:S(2)}) collective-permute-start(bf16[64,1024]{1,0:T(8,128)(2,1)S(1)} %get-tuple-element.104), channel_id=1, source_target_pairs={{0,4},{1,5},{2,6},{3,7}} | collective-permute-start | bytes 393224 | tf_op jit(solution)/shard_map/ppermute | solution.py:380
  20.2 0.7 collective-permute-start.3
  20.9 2.8 %collective-permute-start.12 = (bf16[64,1024]{1,0:T(8,128)(2,1)S(1)}, bf16[64,1024]{1,0:T(8,128)(2,1)S(1)}, u32[]{:S(2)}, u32[]{:S(2)}) collective-permute-start(bf16[64,1024]{1,0:T(8,128)(2,1)S(1)} %get-tuple-element.117), channel_id=1, source_target_pairs={{0,4},{8,12},{1,5},{9,13},{2,6},{10,14},{3,7},{11,15}} | collective-permute-start | bytes 393224 | tf_op jit(solution)/shard_map/ppermute | solution.py:380
  23.7 0.7 collective-permute-start.11
  24.5 2.8 %collective-permute-start.10 = (bf16[64,1024]{1,0:T(8,128)(2,1)S(1)}, bf16[64,1024]{1,0:T(8,128)(2,1)S(1)}, u32[]{:S(2)}, u32[]{:S(2)}) collective-permute-start(bf16[64,1024]{1,0:T(8,128)(2,1)S(1)} %get-tuple-element.115), channel_id=1, source_target_pairs={{0,4},{8,12},{1,5},{9,13},{2,6},{10,14},{3,7},{11,15}} | collective-permute-start | bytes 393224 | tf_op jit(solution)/shard_map/ppermute | solution.py:380
  27.3 0.7 collective-permute-start.9
  28.2 2.8 %collective-permute-start.8 = (bf16[64,1024]{1,0:T(8,128)(2,1)S(1)}, bf16[64,1024]{1,0:T(8,128)(2,1)S(1)}, u32[]{:S(2)}, u32[]{:S(2)}) collective-permute-start(bf16[64,1024]{1,0:T(8,128)(2,1)S(1)} %get-tuple-element.113), channel_id=1, source_target_pairs={{0,4},{8,12},{1,5},{9,13},{2,6},{10,14},{3,7},{11,15}} | collective-permute-start | bytes 393224 | tf_op jit(solution)/shard_map/ppermute | solution.py:380
  31.0 0.7 collective-permute-start.17
  31.7 0.7 collective-permute-start.16
  32.4 0.7 collective-permute-start.15
  33.2 0.7 collective-permute-start.14
  33.9 0.7 collective-permute-start.13
  34.6 0.7 collective-permute-start.22
  35.3 0.7 collective-permute-start.21
  36.1 0.7 collective-permute-start.20
  36.8 0.7 collective-permute-start.19
  37.5 0.7 collective-permute-start.18
  38.2 0.7 collective-permute-start.27
  38.9 0.7 collective-permute-start.26
  39.7 0.7 collective-permute-start.25
  40.4 0.7 collective-permute-start.24
  41.1 0.7 collective-permute-start.23
  41.8 0.7 collective-permute-start.32
  42.6 0.7 collective-permute-start.31
  43.3 0.7 collective-permute-start.30
  44.0 0.7 collective-permute-start.29
  45.0 0.7 collective-permute-start.28
  45.7 0.7 collective-permute-start.37
  46.4 0.7 collective-permute-start.36
  47.1 0.7 collective-permute-start.35
  47.8 0.7 collective-permute-start.34
  48.6 0.7 collective-permute-start.33
  50.0 3.0 %collective-permute-start.41 = (bf16[112,1536]{1,0:T(8,128)(2,1)S(1)}, bf16[112,1536]{1,0:T(8,128)(2,1)S(1)}, u32[]{:S(2)}, u32[]{:S(2)}) collective-permute-start(bf16[112,1536]{1,0:T(8,128)(2,1)S(1)} %shard_map.102), channel_id=1, source_target_pairs={{0,2},{1,3},{2,0},{3,1},{4,6},{5,7},{6,4},{7,5},{8,10},{9,11},{10,... | collective-permute-start | bytes 1032200 | tf_op jit(solution)/shard_map/ppermute | solution.py:386
  53.7 0.7 collective-permute-start.39
  55.4 2.0 %collective-permute-start.43 = (bf16[64,1536]{1,0:T(8,128)(2,1)S(1)}, bf16[64,1536]{1,0:T(8,128)(2,1)S(1)}, u32[]{:S(2)}, u32[]{:S(2)}) collective-permute-start(bf16[64,1536]{1,0:T(8,128)(2,1)S(1)} %shard_map.111), channel_id=1, source_target_pairs={{0,2},{1,3},{2,0},{3,1},{4,6},{5,7},{6,4},{7,5},{8,10},{9,11},{10,... | collective-permute-start | bytes 589832 | tf_op jit(solution)/shard_map/ppermute | solution.py:386
  58.1 8.1 %collective-permute-done.42.refs_1_ = bf16[64,1536]{1,0:T(8,128)(2,1)S(1)} collective-permute-done((bf16[64,1536]{1,0:T(8,128)(2,1)S(1)}, bf16[64,1536]{1,0:T(8,128)(2,1)S(1)}, u32[]{:S(2)}, u32[]{:S(2)}) %collective-permute-start.42) | collective-permute-done | bytes 196640 | tf_op jit(solution)/shard_map/ppermute | solution.py:386
  66.2 3.7 %collective-permute-done.44.refs_3_ = bf16[32,1536]{1,0:T(8,128)(2,1)S(1)} collective-permute-done((bf16[32,1536]{1,0:T(8,128)(2,1)S(1)}, bf16[32,1536]{1,0:T(8,128)(2,1)S(1)}, u32[]{:S(2)}, u32[]{:S(2)}) %collective-permute-start.44) | collective-permute-done | bytes 98336 | tf_op jit(solution)/shard_map/ppermute | solution.py:386
  70.7 1.6 %collective-permute-done.45 = bf16[256,1024]{1,0:T(8,128)(2,1)S(1)} collective-permute-done((bf16[256,1024]{1,0:T(8,128)(2,1)S(1)}, bf16[256,1024]{1,0:T(8,128)(2,1)S(1)}, u32[]{:S(2)}, u32[]{:S(2)}) %collective-permute-start.45) | collective-permute-done | bytes 524320 | tf_op jit(solution)/shard_map/ppermute | solution.py:394
  72.4 31.8 %all_to_all.11 = bf16[8,32,1024]{2,1,0:T(8,128)(2,1)S(1)} all-to-all(bf16[8,32,1024]{2,1,0:T(8,128)(2,1)S(1)} %bitcast.57), channel_id=1, replica_groups=mesh['depth'=8,'freq'=4] {'depth'}, dimensions={0} | all-to-all | bytes 1048576 | tf_op jit(solution)/shard_map/all_to_all | solution.py:406
  104.2 1.6 %shard_map.117 = f32[32,8,256]{2,1,0:T(8,128)} custom-call(bf16[256,1024]{1,0:T(8,128)(2,1)S(1)} %bitcast.52, s32[1024,256]{1,0:T(8,128)S(1)} %copy-done.4), custom_call_target="tpu_custom_call" | custom-call | tf_op jit(solution)/shard_map/pallas_call | solution.py:325
  (114 shorter events, 4.9 us)
Async XLA Ops:
  0.0 7.3 %copy-start = (bf16[1,1,2,1024,1024]{4,3,2,1,0:T(8,128)(2,1)S(1)}, bf16[1,1,2,1024,1024]{4,3,2,1,0:T(8,128)(2,1)}, u32[]{:S(2)}) copy-start(bf16[1,1,2,1024,1024]{4,3,2,1,0:T(8,128)(2,1)} %param.6) | copy-start | bytes 12582916
  4.5 8.1 %collective-permute-start.2 = (bf16[64,1024]{1,0:T(8,128)(2,1)}, bf16[64,1024]{1,0:T(8,128)(2,1)S(1)}, u32[]{:S(2)}, u32[]{:S(2)}) collective-permute-start(bf16[64,1024]{1,0:T(8,128)(2,1)} %get-tuple-element.94.arrived_ref.refs_0_), channel_id=1, source_target_pairs={{0,4},{1,5},{2,6},{3,7}} | collective-permute-start | bytes 393224 | tf_op jit(solution)/shard_map/ppermute | solution.py:380
  5.9 10.7 %collective-permute-start.1 = (bf16[64,1024]{1,0:T(8,128)(2,1)}, bf16[64,1024]{1,0:T(8,128)(2,1)S(1)}, u32[]{:S(2)}, u32[]{:S(2)}) collective-permute-start(bf16[64,1024]{1,0:T(8,128)(2,1)} %get-tuple-element.97.refs_0_), channel_id=1, source_target_pairs={{0,4},{1,5},{2,6},{3,7}} | collective-permute-start | bytes 393224 | tf_op jit(solution)/shard_map/ppermute | solution.py:380
  11.3 8.9 %collective-permute-start = (bf16[64,1024]{1,0:T(8,128)(2,1)S(1)}, bf16[64,1024]{1,0:T(8,128)(2,1)S(1)}, u32[]{:S(2)}, u32[]{:S(2)}) collective-permute-start(bf16[64,1024]{1,0:T(8,128)(2,1)S(1)} %get-tuple-element.96), channel_id=1, source_target_pairs={{0,4},{1,5},{2,6},{3,7}} | collective-permute-start | bytes 393224 | tf_op jit(solution)/shard_map/ppermute | solution.py:380
  12.6 8.2 %collective-permute-start.7 = (bf16[64,1024]{1,0:T(8,128)(2,1)S(1)}, bf16[64,1024]{1,0:T(8,128)(2,1)S(1)}, u32[]{:S(2)}, u32[]{:S(2)}) collective-permute-start(bf16[64,1024]{1,0:T(8,128)(2,1)S(1)} %get-tuple-element.107), channel_id=1, source_target_pairs={{4,8},{5,9},{6,10},{7,11}} | collective-permute-start | bytes 393224 | tf_op jit(solution)/shard_map/ppermute | solution.py:380
  13.4 10.3 %collective-permute-start.6 = (bf16[64,1024]{1,0:T(8,128)(2,1)S(1)}, bf16[64,1024]{1,0:T(8,128)(2,1)S(1)}, u32[]{:S(2)}, u32[]{:S(2)}) collective-permute-start(bf16[64,1024]{1,0:T(8,128)(2,1)S(1)} %get-tuple-element.106), channel_id=1, source_target_pairs={{0,4},{1,5},{2,6},{3,7}} | collective-permute-start | bytes 393224 | tf_op jit(solution)/shard_map/ppermute | solution.py:380
  16.7 7.7 %collective-permute-start.5 = (bf16[64,1024]{1,0:T(8,128)(2,1)S(1)}, bf16[64,1024]{1,0:T(8,128)(2,1)S(1)}, u32[]{:S(2)}, u32[]{:S(2)}) collective-permute-start(bf16[64,1024]{1,0:T(8,128)(2,1)S(1)} %get-tuple-element.105), channel_id=1, source_target_pairs={{4,8},{5,9},{6,10},{7,11}} | collective-permute-start | bytes 393224 | tf_op jit(solution)/shard_map/ppermute | solution.py:380
  17.4 9.8 %collective-permute-start.4 = (bf16[64,1024]{1,0:T(8,128)(2,1)S(1)}, bf16[64,1024]{1,0:T(8,128)(2,1)S(1)}, u32[]{:S(2)}, u32[]{:S(2)}) collective-permute-start(bf16[64,1024]{1,0:T(8,128)(2,1)S(1)} %get-tuple-element.104), channel_id=1, source_target_pairs={{0,4},{1,5},{2,6},{3,7}} | collective-permute-start | bytes 393224 | tf_op jit(solution)/shard_map/ppermute | solution.py:380
  20.2 7.8 %collective-permute-start.3 = (bf16[64,1024]{1,0:T(8,128)(2,1)S(1)}, bf16[64,1024]{1,0:T(8,128)(2,1)S(1)}, u32[]{:S(2)}, u32[]{:S(2)}) collective-permute-start(bf16[64,1024]{1,0:T(8,128)(2,1)S(1)} %get-tuple-element.103), channel_id=1, source_target_pairs={{4,8},{5,9},{6,10},{7,11}} | collective-permute-start | bytes 393224 | tf_op jit(solution)/shard_map/ppermute | solution.py:380
  20.9 10.0 %collective-permute-start.12 = (bf16[64,1024]{1,0:T(8,128)(2,1)S(1)}, bf16[64,1024]{1,0:T(8,128)(2,1)S(1)}, u32[]{:S(2)}, u32[]{:S(2)}) collective-permute-start(bf16[64,1024]{1,0:T(8,128)(2,1)S(1)} %get-tuple-element.117), channel_id=1, source_target_pairs={{0,4},{8,12},{1,5},{9,13},{2,6},{10,14},{3,7},{11,15}} | collective-permute-start | bytes 393224 | tf_op jit(solution)/shard_map/ppermute | solution.py:380
  23.7 7.9 %collective-permute-start.11 = (bf16[64,1024]{1,0:T(8,128)(2,1)S(1)}, bf16[64,1024]{1,0:T(8,128)(2,1)S(1)}, u32[]{:S(2)}, u32[]{:S(2)}) collective-permute-start(bf16[64,1024]{1,0:T(8,128)(2,1)S(1)} %get-tuple-element.116), channel_id=1, source_target_pairs={{4,8},{5,9},{6,10},{7,11}} | collective-permute-start | bytes 393224 | tf_op jit(solution)/shard_map/ppermute | solution.py:380
  24.5 7.9 %collective-permute-start.10 = (bf16[64,1024]{1,0:T(8,128)(2,1)S(1)}, bf16[64,1024]{1,0:T(8,128)(2,1)S(1)}, u32[]{:S(2)}, u32[]{:S(2)}) collective-permute-start(bf16[64,1024]{1,0:T(8,128)(2,1)S(1)} %get-tuple-element.115), channel_id=1, source_target_pairs={{0,4},{8,12},{1,5},{9,13},{2,6},{10,14},{3,7},{11,15}} | collective-permute-start | bytes 393224 | tf_op jit(solution)/shard_map/ppermute | solution.py:380
  27.3 5.8 %collective-permute-start.9 = (bf16[64,1024]{1,0:T(8,128)(2,1)S(1)}, bf16[64,1024]{1,0:T(8,128)(2,1)S(1)}, u32[]{:S(2)}, u32[]{:S(2)}) collective-permute-start(bf16[64,1024]{1,0:T(8,128)(2,1)S(1)} %get-tuple-element.114), channel_id=1, source_target_pairs={{4,8},{5,9},{6,10},{7,11}} | collective-permute-start | bytes 393224 | tf_op jit(solution)/shard_map/ppermute | solution.py:380
  28.2 5.7 %collective-permute-start.8 = (bf16[64,1024]{1,0:T(8,128)(2,1)S(1)}, bf16[64,1024]{1,0:T(8,128)(2,1)S(1)}, u32[]{:S(2)}, u32[]{:S(2)}) collective-permute-start(bf16[64,1024]{1,0:T(8,128)(2,1)S(1)} %get-tuple-element.113), channel_id=1, source_target_pairs={{0,4},{8,12},{1,5},{9,13},{2,6},{10,14},{3,7},{11,15}} | collective-permute-start | bytes 393224 | tf_op jit(solution)/shard_map/ppermute | solution.py:380
  31.0 3.6 %collective-permute-start.17 = (bf16[64,1024]{1,0:T(8,128)(2,1)S(1)}, bf16[64,1024]{1,0:T(8,128)(2,1)S(1)}, u32[]{:S(2)}, u32[]{:S(2)}) collective-permute-start(bf16[64,1024]{1,0:T(8,128)(2,1)S(1)} %get-tuple-element.127), channel_id=1, source_target_pairs={{4,8},{12,16},{5,9},{13,17},{6,10},{14,18},{7,11},{15,19}} | collective-permute-start | bytes 393224 | tf_op jit(solution)/shard_map/ppermute | solution.py:380
  31.7 3.6 %collective-permute-start.16 = (bf16[64,1024]{1,0:T(8,128)(2,1)S(1)}, bf16[64,1024]{1,0:T(8,128)(2,1)S(1)}, u32[]{:S(2)}, u32[]{:S(2)}) collective-permute-start(bf16[64,1024]{1,0:T(8,128)(2,1)S(1)} %get-tuple-element.126), channel_id=1, source_target_pairs={{8,12},{16,20},{9,13},{17,21},{10,14},{18,22},{11,15},{19,23}} | collective-permute-start | bytes 393224 | tf_op jit(solution)/shard_map/ppermute | solution.py:380
  32.4 3.6 %collective-permute-start.15 = (bf16[64,1024]{1,0:T(8,128)(2,1)S(1)}, bf16[64,1024]{1,0:T(8,128)(2,1)S(1)}, u32[]{:S(2)}, u32[]{:S(2)}) collective-permute-start(bf16[64,1024]{1,0:T(8,128)(2,1)S(1)} %get-tuple-element.125), channel_id=1, source_target_pairs={{4,8},{12,16},{5,9},{13,17},{6,10},{14,18},{7,11},{15,19}} | collective-permute-start | bytes 393224 | tf_op jit(solution)/shard_map/ppermute | solution.py:380
  33.2 3.6 %collective-permute-start.14 = (bf16[64,1024]{1,0:T(8,128)(2,1)S(1)}, bf16[64,1024]{1,0:T(8,128)(2,1)S(1)}, u32[]{:S(2)}, u32[]{:S(2)}) collective-permute-start(bf16[64,1024]{1,0:T(8,128)(2,1)S(1)} %get-tuple-element.124), channel_id=1, source_target_pairs={{8,12},{16,20},{9,13},{17,21},{10,14},{18,22},{11,15},{19,23}} | collective-permute-start | bytes 393224 | tf_op jit(solution)/shard_map/ppermute | solution.py:380
  33.9 3.6 %collective-permute-start.13 = (bf16[64,1024]{1,0:T(8,128)(2,1)S(1)}, bf16[64,1024]{1,0:T(8,128)(2,1)S(1)}, u32[]{:S(2)}, u32[]{:S(2)}) collective-permute-start(bf16[64,1024]{1,0:T(8,128)(2,1)S(1)} %get-tuple-element.123), channel_id=1, source_target_pairs={{4,8},{12,16},{5,9},{13,17},{6,10},{14,18},{7,11},{15,19}} | collective-permute-start | bytes 393224 | tf_op jit(solution)/shard_map/ppermute | solution.py:380
  34.6 3.6 %collective-permute-start.22 = (bf16[64,1024]{1,0:T(8,128)(2,1)S(1)}, bf16[64,1024]{1,0:T(8,128)(2,1)S(1)}, u32[]{:S(2)}, u32[]{:S(2)}) collective-permute-start(bf16[64,1024]{1,0:T(8,128)(2,1)S(1)} %get-tuple-element.137), channel_id=1, source_target_pairs={{8,12},{16,20},{9,13},{17,21},{10,14},{18,22},{11,15},{19,23}} | collective-permute-start | bytes 393224 | tf_op jit(solution)/shard_map/ppermute | solution.py:380
  35.3 3.6 %collective-permute-start.21 = (bf16[64,1024]{1,0:T(8,128)(2,1)S(1)}, bf16[64,1024]{1,0:T(8,128)(2,1)S(1)}, u32[]{:S(2)}, u32[]{:S(2)}) collective-permute-start(bf16[64,1024]{1,0:T(8,128)(2,1)S(1)} %get-tuple-element.136), channel_id=1, source_target_pairs={{12,16},{20,24},{13,17},{21,25},{14,18},{22,26},{15,19},{23,27}} | collective-permute-start | bytes 393224 | tf_op jit(solution)/shard_map/ppermute | solution.py:380
  36.1 3.6 %collective-permute-start.20 = (bf16[64,1024]{1,0:T(8,128)(2,1)S(1)}, bf16[64,1024]{1,0:T(8,128)(2,1)S(1)}, u32[]{:S(2)}, u32[]{:S(2)}) collective-permute-start(bf16[64,1024]{1,0:T(8,128)(2,1)S(1)} %get-tuple-element.135), channel_id=1, source_target_pairs={{8,12},{16,20},{9,13},{17,21},{10,14},{18,22},{11,15},{19,23}} | collective-permute-start | bytes 393224 | tf_op jit(solution)/shard_map/ppermute | solution.py:380
  36.8 3.6 %collective-permute-start.19 = (bf16[64,1024]{1,0:T(8,128)(2,1)S(1)}, bf16[64,1024]{1,0:T(8,128)(2,1)S(1)}, u32[]{:S(2)}, u32[]{:S(2)}) collective-permute-start(bf16[64,1024]{1,0:T(8,128)(2,1)S(1)} %get-tuple-element.134), channel_id=1, source_target_pairs={{12,16},{20,24},{13,17},{21,25},{14,18},{22,26},{15,19},{23,27}} | collective-permute-start | bytes 393224 | tf_op jit(solution)/shard_map/ppermute | solution.py:380
  37.5 3.6 %collective-permute-start.18 = (bf16[64,1024]{1,0:T(8,128)(2,1)S(1)}, bf16[64,1024]{1,0:T(8,128)(2,1)S(1)}, u32[]{:S(2)}, u32[]{:S(2)}) collective-permute-start(bf16[64,1024]{1,0:T(8,128)(2,1)S(1)} %get-tuple-element.133), channel_id=1, source_target_pairs={{8,12},{16,20},{9,13},{17,21},{10,14},{18,22},{11,15},{19,23}} | collective-permute-start | bytes 393224 | tf_op jit(solution)/shard_map/ppermute | solution.py:380
  38.2 3.6 %collective-permute-start.27 = (bf16[64,1024]{1,0:T(8,128)(2,1)S(1)}, bf16[64,1024]{1,0:T(8,128)(2,1)S(1)}, u32[]{:S(2)}, u32[]{:S(2)}) collective-permute-start(bf16[64,1024]{1,0:T(8,128)(2,1)S(1)} %get-tuple-element.147), channel_id=1, source_target_pairs={{12,16},{20,24},{13,17},{21,25},{14,18},{22,26},{15,19},{23,27}} | collective-permute-start | bytes 393224 | tf_op jit(solution)/shard_map/ppermute | solution.py:380
  38.9 3.6 %collective-permute-start.26 = (bf16[64,1024]{1,0:T(8,128)(2,1)S(1)}, bf16[64,1024]{1,0:T(8,128)(2,1)S(1)}, u32[]{:S(2)}, u32[]{:S(2)}) collective-permute-start(bf16[64,1024]{1,0:T(8,128)(2,1)S(1)} %get-tuple-element.146), channel_id=1, source_target_pairs={{16,20},{24,28},{17,21},{25,29},{18,22},{26,30},{19,23},{27,31}} | collective-permute-start | bytes 393224 | tf_op jit(solution)/shard_map/ppermute | solution.py:380
  39.7 3.6 %collective-permute-start.25 = (bf16[64,1024]{1,0:T(8,128)(2,1)S(1)}, bf16[64,1024]{1,0:T(8,128)(2,1)S(1)}, u32[]{:S(2)}, u32[]{:S(2)}) collective-permute-start(bf16[64,1024]{1,0:T(8,128)(2,1)S(1)} %get-tuple-element.145), channel_id=1, source_target_pairs={{12,16},{20,24},{13,17},{21,25},{14,18},{22,26},{15,19},{23,27}} | collective-permute-start | bytes 393224 | tf_op jit(solution)/shard_map/ppermute | solution.py:380
  40.4 3.6 %collective-permute-start.24 = (bf16[64,1024]{1,0:T(8,128)(2,1)S(1)}, bf16[64,1024]{1,0:T(8,128)(2,1)S(1)}, u32[]{:S(2)}, u32[]{:S(2)}) collective-permute-start(bf16[64,1024]{1,0:T(8,128)(2,1)S(1)} %get-tuple-element.144), channel_id=1, source_target_pairs={{16,20},{24,28},{17,21},{25,29},{18,22},{26,30},{19,23},{27,31}} | collective-permute-start | bytes 393224 | tf_op jit(solution)/shard_map/ppermute | solution.py:380
  41.1 3.6 %collective-permute-start.23 = (bf16[64,1024]{1,0:T(8,128)(2,1)S(1)}, bf16[64,1024]{1,0:T(8,128)(2,1)S(1)}, u32[]{:S(2)}, u32[]{:S(2)}) collective-permute-start(bf16[64,1024]{1,0:T(8,128)(2,1)S(1)} %get-tuple-element.143), channel_id=1, source_target_pairs={{12,16},{20,24},{13,17},{21,25},{14,18},{22,26},{15,19},{23,27}} | collective-permute-start | bytes 393224 | tf_op jit(solution)/shard_map/ppermute | solution.py:380
  41.8 3.8 %collective-permute-start.32 = (bf16[64,1024]{1,0:T(8,128)(2,1)S(1)}, bf16[64,1024]{1,0:T(8,128)(2,1)S(1)}, u32[]{:S(2)}, u32[]{:S(2)}) collective-permute-start(bf16[64,1024]{1,0:T(8,128)(2,1)S(1)} %get-tuple-element.157), channel_id=1, source_target_pairs={{16,20},{24,28},{17,21},{25,29},{18,22},{26,30},{19,23},{27,31}} | collective-permute-start | bytes 393224 | tf_op jit(solution)/shard_map/ppermute | solution.py:380
  42.6 3.8 %collective-permute-start.31 = (bf16[64,1024]{1,0:T(8,128)(2,1)S(1)}, bf16[64,1024]{1,0:T(8,128)(2,1)S(1)}, u32[]{:S(2)}, u32[]{:S(2)}) collective-permute-start(bf16[64,1024]{1,0:T(8,128)(2,1)S(1)} %get-tuple-element.156), channel_id=1, source_target_pairs={{20,24},{21,25},{22,26},{23,27}} | collective-permute-start | bytes 393224 | tf_op jit(solution)/shard_map/ppermute | solution.py:380
  43.3 3.8 %collective-permute-start.30 = (bf16[64,1024]{1,0:T(8,128)(2,1)S(1)}, bf16[64,1024]{1,0:T(8,128)(2,1)S(1)}, u32[]{:S(2)}, u32[]{:S(2)}) collective-permute-start(bf16[64,1024]{1,0:T(8,128)(2,1)S(1)} %get-tuple-element.155), channel_id=1, source_target_pairs={{16,20},{24,28},{17,21},{25,29},{18,22},{26,30},{19,23},{27,31}} | collective-permute-start | bytes 393224 | tf_op jit(solution)/shard_map/ppermute | solution.py:380
  44.0 3.8 %collective-permute-start.29 = (bf16[64,1024]{1,0:T(8,128)(2,1)S(1)}, bf16[64,1024]{1,0:T(8,128)(2,1)S(1)}, u32[]{:S(2)}, u32[]{:S(2)}) collective-permute-start(bf16[64,1024]{1,0:T(8,128)(2,1)S(1)} %get-tuple-element.154), channel_id=1, source_target_pairs={{20,24},{21,25},{22,26},{23,27}} | collective-permute-start | bytes 393224 | tf_op jit(solution)/shard_map/ppermute | solution.py:380
  45.0 3.6 %collective-permute-start.28 = (bf16[64,1024]{1,0:T(8,128)(2,1)S(1)}, bf16[64,1024]{1,0:T(8,128)(2,1)S(1)}, u32[]{:S(2)}, u32[]{:S(2)}) collective-permute-start(bf16[64,1024]{1,0:T(8,128)(2,1)S(1)} %get-tuple-element.153), channel_id=1, source_target_pairs={{16,20},{24,28},{17,21},{25,29},{18,22},{26,30},{19,23},{27,31}} | collective-permute-start | bytes 393224 | tf_op jit(solution)/shard_map/ppermute | solution.py:380
  45.7 4.3 %collective-permute-start.37 = (bf16[64,1024]{1,0:T(8,128)(2,1)S(1)}, bf16[64,1024]{1,0:T(8,128)(2,1)S(1)}, u32[]{:S(2)}, u32[]{:S(2)}) collective-permute-start(bf16[64,1024]{1,0:T(8,128)(2,1)S(1)} %get-tuple-element.167), channel_id=1, source_target_pairs={{20,24},{21,25},{22,26},{23,27}} | collective-permute-start | bytes 393224 | tf_op jit(solution)/shard_map/ppermute | solution.py:380
  46.4 6.6 %collective-permute-start.36 = (bf16[64,1024]{1,0:T(8,128)(2,1)S(1)}, bf16[64,1024]{1,0:T(8,128)(2,1)S(1)}, u32[]{:S(2)}, u32[]{:S(2)}) collective-permute-start(bf16[64,1024]{1,0:T(8,128)(2,1)S(1)} %get-tuple-element.166), channel_id=1, source_target_pairs={{24,28},{25,29},{26,30},{27,31}} | collective-permute-start | bytes 393224 | tf_op jit(solution)/shard_map/ppermute | solution.py:380
  47.1 6.5 %collective-permute-start.35 = (bf16[64,1024]{1,0:T(8,128)(2,1)S(1)}, bf16[64,1024]{1,0:T(8,128)(2,1)S(1)}, u32[]{:S(2)}, u32[]{:S(2)}) collective-permute-start(bf16[64,1024]{1,0:T(8,128)(2,1)S(1)} %get-tuple-element.165), channel_id=1, source_target_pairs={{20,24},{21,25},{22,26},{23,27}} | collective-permute-start | bytes 393224 | tf_op jit(solution)/shard_map/ppermute | solution.py:380
  47.8 6.5 %collective-permute-start.34 = (bf16[64,1024]{1,0:T(8,128)(2,1)S(1)}, bf16[64,1024]{1,0:T(8,128)(2,1)S(1)}, u32[]{:S(2)}, u32[]{:S(2)}) collective-permute-start(bf16[64,1024]{1,0:T(8,128)(2,1)S(1)} %get-tuple-element.164), channel_id=1, source_target_pairs={{24,28},{25,29},{26,30},{27,31}} | collective-permute-start | bytes 393224 | tf_op jit(solution)/shard_map/ppermute | solution.py:380
  48.6 5.9 %collective-permute-start.33 = (bf16[64,1024]{1,0:T(8,128)(2,1)S(1)}, bf16[64,1024]{1,0:T(8,128)(2,1)S(1)}, u32[]{:S(2)}, u32[]{:S(2)}) collective-permute-start(bf16[64,1024]{1,0:T(8,128)(2,1)S(1)} %get-tuple-element.163), channel_id=1, source_target_pairs={{20,24},{21,25},{22,26},{23,27}} | collective-permute-start | bytes 393224 | tf_op jit(solution)/shard_map/ppermute | solution.py:380
  50.0 16.2 %collective-permute-start.41 = (bf16[112,1536]{1,0:T(8,128)(2,1)S(1)}, bf16[112,1536]{1,0:T(8,128)(2,1)S(1)}, u32[]{:S(2)}, u32[]{:S(2)}) collective-permute-start(bf16[112,1536]{1,0:T(8,128)(2,1)S(1)} %shard_map.102), channel_id=1, source_target_pairs={{0,2},{1,3},{2,0},{3,1},{4,6},{5,7},{6,4},{7,5},{8,10},{9,11},{10,... | collective-permute-start | bytes 1032200 | tf_op jit(solution)/shard_map/ppermute | solution.py:386
  53.0 2.4 %collective-permute-start.40 = (bf16[64,1024]{1,0:T(8,128)(2,1)S(1)}, bf16[64,1024]{1,0:T(8,128)(2,1)S(1)}, u32[]{:S(2)}, u32[]{:S(2)}) collective-permute-start(bf16[64,1024]{1,0:T(8,128)(2,1)S(1)} %get-tuple-element.175), channel_id=1, source_target_pairs={{24,28},{25,29},{26,30},{27,31}} | collective-permute-start | bytes 393224 | tf_op jit(solution)/shard_map/ppermute | solution.py:380
  53.7 1.6 %collective-permute-start.39 = (bf16[64,1024]{1,0:T(8,128)(2,1)S(1)}, bf16[64,1024]{1,0:T(8,128)(2,1)S(1)}, u32[]{:S(2)}, u32[]{:S(2)}) collective-permute-start(bf16[64,1024]{1,0:T(8,128)(2,1)S(1)} %get-tuple-element.174), channel_id=1, source_target_pairs={{24,28},{25,29},{26,30},{27,31}} | collective-permute-start | bytes 393224 | tf_op jit(solution)/shard_map/ppermute | solution.py:380
  54.5 2.9 %collective-permute-start.38 = (bf16[64,1024]{1,0:T(8,128)(2,1)S(1)}, bf16[64,1024]{1,0:T(8,128)(2,1)S(1)}, u32[]{:S(2)}, u32[]{:S(2)}) collective-permute-start(bf16[64,1024]{1,0:T(8,128)(2,1)S(1)} %get-tuple-element.173), channel_id=1, source_target_pairs={{24,28},{25,29},{26,30},{27,31}} | collective-permute-start | bytes 393224 | tf_op jit(solution)/shard_map/ppermute | solution.py:380
  55.2 11.0 %collective-permute-start.42 = (bf16[64,1536]{1,0:T(8,128)(2,1)S(1)}, bf16[64,1536]{1,0:T(8,128)(2,1)S(1)}, u32[]{:S(2)}, u32[]{:S(2)}) collective-permute-start(bf16[64,1536]{1,0:T(8,128)(2,1)S(1)} %shard_map.107), channel_id=1, source_target_pairs={{0,2},{1,3},{2,0},{3,1},{4,6},{5,7},{6,4},{7,5},{8,10},{9,11},{10,... | collective-permute-start | bytes 589832 | tf_op jit(solution)/shard_map/ppermute | solution.py:386
  55.4 14.5 %collective-permute-start.43 = (bf16[64,1536]{1,0:T(8,128)(2,1)S(1)}, bf16[64,1536]{1,0:T(8,128)(2,1)S(1)}, u32[]{:S(2)}, u32[]{:S(2)}) collective-permute-start(bf16[64,1536]{1,0:T(8,128)(2,1)S(1)} %shard_map.111), channel_id=1, source_target_pairs={{0,2},{1,3},{2,0},{3,1},{4,6},{5,7},{6,4},{7,5},{8,10},{9,11},{10,... | collective-permute-start | bytes 589832 | tf_op jit(solution)/shard_map/ppermute | solution.py:386
  57.4 12.5 %collective-permute-start.44 = (bf16[32,1536]{1,0:T(8,128)(2,1)S(1)}, bf16[32,1536]{1,0:T(8,128)(2,1)S(1)}, u32[]{:S(2)}, u32[]{:S(2)}) collective-permute-start(bf16[32,1536]{1,0:T(8,128)(2,1)S(1)} %shard_map.113), channel_id=1, source_target_pairs={{0,2},{1,3},{2,0},{3,1},{4,6},{5,7},{6,4},{7,5},{8,10},{9,11},{10,... | collective-permute-start | bytes 294920 | tf_op jit(solution)/shard_map/ppermute | solution.py:386
  58.1 46.1 %copy-start.4 = (s32[1024,256]{1,0:T(8,128)S(1)}, s32[1024,256]{1,0:T(8,128)}, u32[]{:S(2)}) copy-start(s32[1024,256]{1,0:T(8,128)} %lag_ref.1) | copy-start | bytes 3145732
  70.3 2.0 %collective-permute-start.45 = (bf16[256,1024]{1,0:T(8,128)(2,1)S(1)}, bf16[256,1024]{1,0:T(8,128)(2,1)S(1)}, u32[]{:S(2)}, u32[]{:S(2)}) collective-permute-start(bf16[256,1024]{1,0:T(8,128)(2,1)S(1)} %shard_map.116), channel_id=1, source_target_pairs={{0,1},{1,0},{2,3},{3,2},{4,5},{5,4},{6,7},{7,6},{8,9},{9,8},{10,11... | collective-permute-start | bytes 1572872 | tf_op jit(solution)/shard_map/ppermute | solution.py:394
  (5 other events, 30.6 us)
